TPU v7x, 256 devices: a whole 4x4x8 slice. The times are simulated.
256 devices in a mesh: seq: 32 (over y, z), dp: 8 (over x, core).
Axes of the slice: x: 4, y: 4, z: 8, core: 2. Of those that a mesh axis runs over, the one named last changes fastest.
Arguments:
- prefix: bfloat16 [8, 4096, 1024], P('dp', 'seq'), may hold values from -6 to 6
- latents: bfloat16 [8, 1024, 1024], P('dp', 'seq'), may hold values from -96 to 96
- saved_out: bfloat16 [8, 1024, 1024], P('dp', 'seq'), may hold values from -6 to 6
- out_grad: bfloat16 [8, 1024, 1024], P('dp', 'seq'), may hold values from -24 to 24
- visible: int32 [8, 1024], P('dp'), may hold values from 1 to 4096, as said below
- w_query: bfloat16 [1024, 1024], replicated, may hold values from -0.5625 to 0.5625
- w_key: bfloat16 [1024, 1024], replicated, may hold values from -0.5625 to 0.5625
- w_value: bfloat16 [1024, 1024], replicated, may hold values from -0.1875 to 0.1875
Outputs:
- prefix_grad: bfloat16 [8, 4096, 1024], P('dp', 'seq')
- latent_grad: bfloat16 [8, 1024, 1024], P('dp', 'seq')
- key_wgrad: float32 [1024, 1024], P(('seq', 'dp'))
Inputs may be any that keep to these rules, and one draw needn't show every extreme that they name: Within a sample the visible lengths never fall from one latent to the next, and the last latent of every sample sees all 4096 prefix tokens.
All inputs are finite; a program needn't handle non-finite values.
Results may differ from a plain program's by a relative error of at most 0.022.
The roundings to bfloat16 on the way count: a program that leaves them out, or rounds other values in their place, can miss the bound.
Values may be sent and summed in bfloat16 or wider, within the bound.
No kernel may reach another device: no remote copies, remote signals or barrier semaphores. Data moves between devices by JAX's collectives and lax.ppermute only.
A program may use at most 64 MiB of HBM per device.

v0:
```python
import math

import jax
import jax.numpy as jnp
from jax import lax
from jax.sharding import PartitionSpec as P

H = 16
DH = 64


def head_block(tensor, group, width):
    piece = lax.dynamic_slice_in_dim(tensor, group * width, width, 2)
    return piece.reshape(piece.shape[0], piece.shape[1], 4, width // 4)


def on_device(prefix, latents, saved_out, out_grad, visible, w_query, w_key, w_value):
    scale = 1.0 / math.sqrt(DH)
    batch_dev, prefix_dev, width = prefix.shape
    latent_all = visible.shape[1]
    heads = H
    group_width = 4 * DH
    groups = heads // 4
    own_queries = jnp.einsum(
        "bld,de->ble", latents, w_query, preferred_element_type=jnp.float32
    ).astype(jnp.bfloat16)
    queries, grads, outputs = (
        lax.all_gather(own_queries, "seq", axis=1, tiled=True),
        lax.all_gather(out_grad, "seq", axis=1, tiled=True),
        lax.all_gather(saved_out, "seq", axis=1, tiled=True),
    )
    keys = jnp.einsum("bpd,de->bpe", prefix, w_key, preferred_element_type=jnp.float32).astype(
        jnp.bfloat16
    )
    values = jnp.einsum("bpd,de->bpe", prefix, w_value, preferred_element_type=jnp.float32).astype(
        jnp.bfloat16
    )
    positions = lax.axis_index("seq") * prefix_dev + jnp.arange(prefix_dev, dtype=jnp.int32)
    mask = (positions[None, None, :] < visible[:, :, None])[:, None]
    delta = (
        (grads.astype(jnp.float32) * outputs.astype(jnp.float32))
        .reshape(batch_dev, latent_all, heads, DH)
        .sum(-1)
    )
    delta = delta.transpose(0, 2, 1)

    def scores_of(group):
        q_group = head_block(queries, group, group_width)
        k_group = head_block(keys, group, group_width)
        scores = (
            jnp.einsum("bihd,bjhd->bhij", q_group, k_group, preferred_element_type=jnp.float32)
            * scale
        )
        return jnp.where(mask, scores, jnp.float32(-1e30))

    def stats_step(group, carry):
        local_max, local_total = carry
        scores = scores_of(group)
        rowmax = jnp.max(scores, axis=3)
        total = jnp.sum(
            jnp.where(mask, jnp.exp(scores - rowmax[..., None]), jnp.float32(0.0)), axis=3
        )
        local_max = lax.dynamic_update_slice_in_dim(local_max, rowmax, group * 4, 1)
        local_total = lax.dynamic_update_slice_in_dim(local_total, total, group * 4, 1)
        return (local_max, local_total)

    empty_stats = jnp.zeros((batch_dev, heads, latent_all), jnp.float32)
    local_max, local_total = lax.fori_loop(0, groups, stats_step, (empty_stats, empty_stats))
    global_max = lax.pmax(local_max.astype(jnp.bfloat16), "seq").astype(local_max.dtype)
    global_total = lax.psum(
        (local_total * jnp.exp(local_max - global_max)).astype(jnp.bfloat16), "seq"
    ).astype(jnp.float32)
    lse = global_max + jnp.log(global_total)

    def backward_step(group, carry):
        dq_acc, dk_acc, dv_acc = carry
        scores = scores_of(group)
        lse_group = lax.dynamic_slice_in_dim(lse, group * 4, 4, 1)
        delta_group = lax.dynamic_slice_in_dim(delta, group * 4, 4, 1)
        probs = jnp.where(mask, jnp.exp(scores - lse_group[..., None]), jnp.float32(0.0))
        probs_b = probs.astype(jnp.bfloat16)
        q_group = head_block(queries, group, group_width)
        k_group = head_block(keys, group, group_width)
        v_group = head_block(values, group, group_width)
        g_group = head_block(grads, group, group_width)
        dprobs = jnp.einsum("bihd,bjhd->bhij", g_group, v_group, preferred_element_type=jnp.float32)
        dscores = (probs * (dprobs - delta_group[..., None]) * scale).astype(jnp.bfloat16)
        dv_group = jnp.einsum(
            "bhij,bihd->bjhd", probs_b, g_group, preferred_element_type=jnp.float32
        )
        dk_group = jnp.einsum(
            "bhij,bihd->bjhd", dscores, q_group, preferred_element_type=jnp.float32
        )
        dq_group = jnp.einsum(
            "bhij,bjhd->bihd", dscores, k_group, preferred_element_type=jnp.float32
        )
        dv_acc = lax.dynamic_update_slice_in_dim(
            dv_acc,
            dv_group.reshape(batch_dev, prefix_dev, group_width).astype(jnp.bfloat16),
            group * group_width,
            2,
        )
        dk_acc = lax.dynamic_update_slice_in_dim(
            dk_acc,
            dk_group.reshape(batch_dev, prefix_dev, group_width).astype(jnp.bfloat16),
            group * group_width,
            2,
        )
        dq_acc = lax.dynamic_update_slice_in_dim(
            dq_acc, dq_group.reshape(batch_dev, latent_all, group_width), group * group_width, 2
        )
        return (dq_acc, dk_acc, dv_acc)

    start = (
        jnp.zeros((batch_dev, latent_all, width), jnp.float32),
        jnp.zeros((batch_dev, prefix_dev, width), jnp.bfloat16),
        jnp.zeros((batch_dev, prefix_dev, width), jnp.bfloat16),
    )
    dq_partial, dkeys, dvalues = lax.fori_loop(0, groups, backward_step, start)
    dqueries = lax.psum_scatter(
        dq_partial.astype(jnp.bfloat16), "seq", scatter_dimension=1, tiled=True
    )
    latent_grad = jnp.einsum(
        "bld,ed->ble", dqueries, w_query, preferred_element_type=jnp.float32
    ).astype(jnp.bfloat16)
    prefix_grad = (
        jnp.einsum("bpd,ed->bpe", dkeys, w_key, preferred_element_type=jnp.float32)
        + jnp.einsum("bpd,ed->bpe", dvalues, w_value, preferred_element_type=jnp.float32)
    ).astype(jnp.bfloat16)
    key_part = jnp.einsum("bpd,bpe->de", prefix, dkeys, preferred_element_type=jnp.float32)
    key_wgrad = lax.psum_scatter(key_part, ("seq", "dp"), scatter_dimension=0, tiled=True)
    return (prefix_grad, latent_grad, key_wgrad)


def solution(mesh):
    return jax.shard_map(
        on_device,
        mesh=mesh,
        in_specs=(
            P("dp", "seq", None),
            P("dp", "seq", None),
            P("dp", "seq", None),
            P("dp", "seq", None),
            P("dp", None),
            P(),
            P(),
            P(),
        ),
        out_specs=(P("dp", "seq", None), P("dp", "seq", None), P(("seq", "dp"), None)),
        check_vma=False,
    )
```

profile of v0, /device:TPU:2, one launch (start us, length us, event | category | flops | bytes accessed | tf_op | source)
XLA Modules:
  0.0 940.0 jit_solution(12605091551576224468)
XLA Ops:
  7.2 2.9 convolution_convert_fusion.5
  12.3 2.0 fusion.9
  14.4 77.7 %all-gather.9.cloned.1.call-done = bf16[1024,1024]{1,0:T(8,128)(2,1)} async-done(((bf16[32,1024]{1,0:T(8,128)(2,1)}), bf16[1024,1024]{1,0:T(8,128)(2,1)}) %all-gather.9.cloned.1.call-update) | async-done | bytes 2097168 | tf_op jit(solution)/shard_map/all_gather | solution.py:28
  92.1 3.9 copy.32
  96.0 12.6 %while.34 = (s32[]{:T(128)}, f32[1,16,1024]{2,1,0:T(8,128)S(1)}, f32[1,16,1024]{2,1,0:T(8,128)S(1)}, bf16[1,1024,1024]{1,2,0:T(8,128)(2,1)}, bf16[1,128,1024]{1,...) while((s32[]{:T(128)}, f32[1,16,1024]{2,1,0:T(8,128)S(1)}, ...), condition=%wide.region_3.0_spmd.clone, body=%wide.region_0.3_spmd.clone.sunk | while | flops 71426056 | bytes 6476525 | solution.py:68
  96.9 1.1 constant_dynamic-slice_fusion.13
  99.2 0.8 compare_bitcast_fusion.4
  100.1 1.1 constant_dynamic-slice_fusion.13
  102.4 0.8 compare_bitcast_fusion.4
  103.2 1.1 constant_dynamic-slice_fusion.13
  106.3 1.1 constant_dynamic-slice_fusion.13
  108.6 61.2 %all-gather.7.cloned.1.call-done = bf16[1,1024,1024]{2,1,0:T(8,128)(2,1)} async-done(((bf16[1,32,1024]{2,1,0:T(8,128)(2,1)}), bf16[1,1024,1024]{2,1,0:T(8,128)(2,1)}) %all-gather.7.cloned.1.call-update) | async-done | bytes 2097168 | tf_op jit(solution)/shard_map/all_gather | solution.py:30
  169.9 3.9 copy.30
  173.8 140.3 %pmax.7 = bf16[1,16,1024]{2,1,0:T(8,128)(2,1)S(1)} all-reduce(bf16[1,16,1024]{2,1,0:T(8,128)(2,1)S(1)} %convert_element_type.119), channel_id=1, replica_groups=mesh['seq'=32,'dp'=8] {'seq'}, use_global_device_ids=true, to_apply=%region_4.5 | all-reduce | flops 16384 | bytes 65536 | tf_op jit(solution)/shard_map/pmax | solution.py:69
  314.2 137.7 %psum.7 = bf16[1,16,1024]{2,1,0:T(8,128)(2,1)S(1)} all-reduce(bf16[1,16,1024]{2,1,0:T(8,128)(2,1)S(1)} %fusion.20), channel_id=1, replica_groups=mesh['seq'=32,'dp'=8] {'seq'}, use_global_device_ids=true, to_apply=%region_5.6 | all-reduce | flops 16384 | bytes 65536 | tf_op jit(solution)/shard_map/psum | solution.py:70
  451.9 4.0 copy.33
  455.9 5.1 convert_multiply_fusion
  461.0 2.7 reduce_sum.24
  463.8 1.6 broadcast_in_dim.74
  465.4 32.0 %while.35 = (s32[]{:T(128)}, bf16[1,1024,1024]{1,2,0:T(8,128)(2,1)}, bf16[1,128,1024]{1,2,0:T(8,128)(2,1)S(1)}, bf16[1,128,1024]{1,2,0:T(8,128)(2,1)S(1)}, bf16[...) while((s32[]{:T(128)}, ...), condition=%wide.region_8.9_spmd.clone, body=%wide.region_7.8_spmd.clone.sunk | while | flops 340459520 | bytes 17671144 | solution.py:119
  466.8 0.9 compare_bitcast_fusion.5
  467.7 1.3 constant_dynamic-slice_fusion.16
  468.9 1.4 exponential_select_fusion.2
  470.6 1.0 multiply_convert_fusion.2
  472.6 0.9 constant_dynamic-update-slice_fusion.6
  474.8 0.9 compare_bitcast_fusion.5
  475.7 1.3 constant_dynamic-slice_fusion.16
  477.0 1.4 exponential_select_fusion.2
  478.7 1.0 multiply_convert_fusion.2
  480.6 0.9 constant_dynamic-update-slice_fusion.6
  482.8 0.9 compare_bitcast_fusion.5
  483.7 1.3 constant_dynamic-slice_fusion.16
  485.0 1.4 exponential_select_fusion.2
  486.7 1.0 multiply_convert_fusion.2
  488.6 0.8 constant_dynamic-update-slice_fusion.6
  490.8 0.9 compare_bitcast_fusion.5
  491.7 1.3 constant_dynamic-slice_fusion.16
  493.0 1.4 exponential_select_fusion.2
  494.7 1.0 multiply_convert_fusion.2
  496.6 0.8 constant_dynamic-update-slice_fusion.6
  497.5 2.7 convolution_bitcast_fusion
  500.2 10.9 %copy.35 = bf16[1,1024,1024]{2,0,1:T(2,128)(2,1)} copy(bf16[1,1024,1024]{1,2,0:T(8,128)(2,1)} %get-tuple-element.303) | data formatting | bytes 4194304 | tf_op jit(solution)/shard_map/convert_element_type | solution.py:121
  514.6 1.6 fusion.7
  516.1 246.6 %all-reduce.7.cloned.1.call-done = f32[1024,1024]{0,1:T(8,128)} async-done(((f32[1024,1024]{0,1:T(8,128)}), f32[1024,1024]{0,1:T(8,128)}) %all-reduce.7.cloned.1.call-update) | async-done | bytes 4194320
  762.7 1.2 constant_dynamic-slice_fusion.6
  764.8 164.7 %all-reduce.5.cloned.1.call-done = bf16[1,1024,1024]{2,0,1:T(2,128)(2,1)} async-done(((bf16[1,1024,1024]{2,0,1:T(2,128)(2,1)}), bf16[1,1024,1024]{2,0,1:T(2,128)(2,1)}) %all-reduce.5.cloned.1.call-update) | async-done | bytes 2097168
  929.4 1.0 constant_dynamic-slice_fusion.7
  930.5 3.0 fusion.10
  (142 shorter events, 22.0 us)
Async XLA Ops:
  7.2 4.5 copy-start
  7.2 4.5 copy-start.2
  7.2 84.9 %all-gather.9.cloned.1.call-start = ((), (), s32[]{:S(2)}) async-start(), calls=%async_computation.2 | async-start | bytes 2162688 | tf_op jit(solution)/shard_map/all_gather | solution.py:28
  10.1 159.7 %all-gather.7.cloned.1.call-start = ((), (), s32[]{:S(2)}) async-start(), calls=%async_computation.1 | async-start | bytes 2162688 | tf_op jit(solution)/shard_map/all_gather | solution.py:30
  10.9 441.0 %all-gather.5.cloned.1.call-start = ((), (), s32[]{:S(2)}) async-start(), calls=%async_computation | async-start | bytes 2162688 | tf_op jit(solution)/shard_map/all_gather | solution.py:29
  11.6 751.1 %all-reduce.7.cloned.1.call-start = ((), (), s32[]{:S(2)}) async-start(), calls=%async_computation.4 | async-start | bytes 8388608
  465.4 0.5 copy-start.8
  465.4 1.2 copy-start.6
  465.4 1.2 copy-start.4
  466.7 2.2 copy-start.3
  471.7 1.7 copy-start.5
  471.7 1.7 copy-start.7
  471.7 1.7 copy-start.9
  473.4 0.5 copy-start.8
  473.4 1.1 copy-start.6
  473.5 1.1 copy-start.4
  474.7 2.2 copy-start.3
  479.7 1.7 copy-start.5
  479.7 1.7 copy-start.7
  479.7 1.7 copy-start.9
  481.5 0.5 copy-start.8
  481.5 1.1 copy-start.6
  481.5 1.1 copy-start.4
  482.7 2.2 copy-start.3
  487.7 1.7 copy-start.5
  487.7 1.7 copy-start.7
  487.7 1.7 copy-start.9
  489.5 0.5 copy-start.8
  489.5 1.1 copy-start.6
  489.5 1.1 copy-start.4
  490.8 2.2 copy-start.3
  495.7 1.7 copy-start.5
  495.7 1.7 copy-start.7
  495.8 1.7 copy-start.9
  500.1 429.3 %all-reduce.5.cloned.1.call-start = ((), (), s32[]{:S(2)}) async-start(), calls=%async_computation.3 | async-start | bytes 8388608
  511.0 0.7 copy-start.10
  513.0 1.6 copy-start.1
Sparse Core Ops, SparseCore 0:
  11.2 80.8 all-gather.8
  94.7 75.1 all-gather.6
  172.5 75.1 all-gather.4
  500.3 262.4 all-reduce.6
  766.6 162.7 all-reduce.4
where the time goes:
time: 941 us; the launch traced here: 940 us
  waiting for transfers between devices  552 us (59%)
  blocking collectives  278 us (30%)
  local copies, waits for them, and re-layouts  47.9 us (5%)
  matrix products  29.8 us (3%)
  other arithmetic  16.9 us (2%)
  between operations  14.6 us (2%)
    unnamed x7, waiting for transfers between devices  413 us
    pmax x1, blocking collectives, on_device(): lax.pmax(local_max.astype(jnp.bfloat16), 'seq').astype(local_max.dtype)  140 us
    psum x1, blocking collectives, on_device(): lax.psum((local_total * jnp.exp(local_max - global_max)).astype(jnp.bfloa...  138 us
    all_gather x1, waiting for transfers between devices, on_device(): lax.all_gather(own_queries, 'seq', axis=1, tiled=True)  77.7 us
    all_gather x1, waiting for transfers between devices, on_device(): lax.all_gather(saved_out, 'seq', axis=1, tiled=True)  61.2 us
  transfers between devices with their start and end apart: 5, of which 4 were waited for; matrix products, arithmetic and copies ran while one was open for 4% of the time, Pallas kernels for 0%

commit v1 on v0

v1 whole, which is shorter than its diff:
```python
import functools
import math

import jax
import jax.numpy as jnp
from jax import lax
from jax.experimental import pallas as pl
from jax.experimental.pallas import tpu as pltpu
from jax.sharding import Mesh, PartitionSpec as P

BF = jnp.bfloat16
F32 = jnp.float32
DH = 64
NEG = -1e30
FLOOR = -1e29
SCALE = 1.0 / math.sqrt(DH)
C = SCALE * math.log2(math.e)
NT_DIMS = (((1,), (1,)), ((), ()))
VMEM_LIMIT = 48 * 1024 * 1024
LAT_TILE = 256
SRC_CHUNK = 8


def dot(a, b):
    return jnp.dot(a, b, preferred_element_type=F32)


def dot_nt(a, b):
    return lax.dot_general(a, b, NT_DIMS, preferred_element_type=F32)


def swap(x):
    return jnp.concatenate([x[..., 64:], x[..., :64]], axis=-1)


def fold(x, rows):
    return jnp.concatenate([x[:rows], x[rows:]], axis=1)


def pre_kernel(prefix, latents, grad, saved, w_query, w_key, w_value, kq, vg):
    keys = dot(prefix[...], w_key[...]).astype(BF)
    values = dot(prefix[...], w_value[...]).astype(BF)
    queries = dot(latents[...], w_query[...]).astype(BF)
    g = grad[...]
    product = g.astype(F32) * saved[...].astype(F32)
    lat = product.shape[0]
    product = jnp.concatenate([product, jnp.zeros((128 - lat, product.shape[1]), F32)], axis=0)
    product = product.T
    half_tok = prefix.shape[0] // 2
    for head in range(4):
        cols = slice(head * DH, (head + 1) * DH)
        delta = jnp.sum(product[cols], axis=0, keepdims=True)
        high = delta.astype(BF)
        rest = delta - high.astype(F32)
        mid = rest.astype(BF)
        low = (rest - mid.astype(F32)).astype(BF)
        row = lax.broadcasted_iota(jnp.int32, (16, 128), 0)
        parts = jnp.where(
            row == 0,
            high.astype(F32),
            jnp.where(row == 1, mid.astype(F32), jnp.where(row == 2, low.astype(F32), 0.0)),
        ).astype(BF)
        q_fold = fold(queries[:, cols], lat // 2)
        g_fold = fold(g[:, cols], lat // 2)
        for half in range(2):
            toks = slice(half * half_tok, (half + 1) * half_tok)
            dest = 2 * head + half
            kq[dest, 0:32, :] = fold(keys[toks, cols], half_tok // 2)
            kq[dest, 32:48, :] = q_fold
            vg[dest, 0:32, :] = fold(values[toks, cols], half_tok // 2)
            vg[dest, 32:48, :] = g_fold
            vg[dest, 48:64, :] = parts


def unfold(folded, low_ref, high_ref):
    lane = lax.broadcasted_iota(jnp.int32, folded.shape, 2)
    other = swap(folded)
    zero = jnp.zeros_like(folded)
    left = lane < 64
    low = jnp.concatenate([jnp.where(left, folded, zero), jnp.where(left, other, zero)], axis=1)
    high = jnp.concatenate([jnp.where(left, zero, other), jnp.where(left, zero, folded)], axis=1)
    low_ref[...] = low.reshape(low_ref.shape)
    high_ref[...] = high.reshape(high_ref.shape)


def chunk_tokens(chunk, half, rows, cols):
    row = lax.broadcasted_iota(jnp.int32, (rows, cols), 0)
    return (chunk * SRC_CHUNK + (row >> 5)) * 128 + half * 64 + (row & 31)


def chunk_count(vis_s, half, tile):
    span = SRC_CHUNK * 128
    seen = vis_s[(tile + 1) * LAT_TILE - 1] - half * 64
    seen = jnp.maximum(seen, 0)
    return jnp.minimum((seen + span - 1) // span, 32 // SRC_CHUNK)


def stats_kernel(vis_s, half_s, vis, kq, out, q_low, q_high):
    half = half_s[0]
    unfold(kq[:, 32:48, :], q_low, q_high)
    rows = SRC_CHUNK * 32
    for tile in range(1024 // LAT_TILE):
        lanes = slice(tile * LAT_TILE, (tile + 1) * LAT_TILE)
        seen = vis[:, lanes]
        ql = q_low[lanes, :]
        qh = q_high[lanes, :]

        def step(chunk, carry):
            top, total = carry
            k = kq[pl.ds(chunk * SRC_CHUNK, SRC_CHUNK), 0:32, :].reshape(rows, 128)
            tok = chunk_tokens(chunk, half, rows, LAT_TILE)
            s_low = jnp.where(tok < seen, dot_nt(k, ql), NEG)
            s_high = jnp.where(tok < seen - 32, dot_nt(k, qh), NEG)
            new = jnp.maximum(jnp.max(s_low, axis=0, keepdims=True), jnp.max(s_high, axis=0, keepdims=True))
            new = jnp.maximum(new, top)
            part = jnp.sum(jnp.exp2((s_low - new) * C), axis=0, keepdims=True) + jnp.sum(
                jnp.exp2((s_high - new) * C), axis=0, keepdims=True
            )
            return new, total * jnp.exp2((top - new) * C) + part

        start = (jnp.full((1, LAT_TILE), FLOOR, F32), jnp.zeros((1, LAT_TILE), F32))
        top, total = lax.fori_loop(0, chunk_count(vis_s, half, tile), step, start)
        out[0:1, lanes] = top
        out[1:2, lanes] = total
    out[2:8, :] = jnp.zeros((6, 1024), F32)


def grad_kernel(vis_s, half_s, vis, kq, vg, own, other, dk_out, dvq_out,
                q_low, q_high, g_low, g_high, k_t, dk_acc, dv_acc, delta_ref):
    half = half_s[0]
    rows = SRC_CHUNK * 32
    unfold(kq[:, 32:48, :], q_low, q_high)
    unfold(vg[:, 32:48, :], g_low, g_high)
    for chunk in range(32 // SRC_CHUNK):
        k = kq[chunk * SRC_CHUNK : (chunk + 1) * SRC_CHUNK, 0:32, :].reshape(rows, 128)
        turned = k.T
        k_t[chunk] = jnp.concatenate([turned[0:64], turned[64:128]], axis=1)
    dk_acc[...] = jnp.zeros_like(dk_acc)
    dv_acc[...] = jnp.zeros_like(dv_acc)
    lane = lax.broadcasted_iota(jnp.int32, (1, 128), 1)
    for block in range(8):
        joined = jnp.zeros((1, 128), F32)
        for place in range(4):
            parts = vg[4 * block + place, 48:64, :].astype(F32)
            parts = jnp.sum(parts, axis=0, keepdims=True)
            if place:
                parts = pltpu.roll(parts, 32 * place, 1)
            joined = jnp.where((lane >> 5) == place, parts, joined)
        delta_ref[:, block * 128 : (block + 1) * 128] = joined
    top = jnp.maximum(own[0:1, :], other[0:1, :])
    total = own[1:2, :] * jnp.exp2((own[0:1, :] - top) * C) + other[1:2, :] * jnp.exp2((other[0:1, :] - top) * C)
    lse = top + jnp.log2(total) * (1.0 / C)
    for tile in range(1024 // LAT_TILE):
        lanes = slice(tile * LAT_TILE, (tile + 1) * LAT_TILE)
        seen = vis[:, lanes]
        lse_t = lse[:, lanes]
        delta = delta_ref[:, lanes]
        ql, qh, gl, gh = q_low[lanes, :], q_high[lanes, :], g_low[lanes, :], g_high[lanes, :]

        def step(chunk, dq):
            srcs = pl.ds(chunk * SRC_CHUNK, SRC_CHUNK)
            k = kq[srcs, 0:32, :].reshape(rows, 128)
            v = vg[srcs, 0:32, :].reshape(rows, 128)
            tok = chunk_tokens(chunk, half, rows, LAT_TILE)
            p_low = jnp.exp2((jnp.where(tok < seen, dot_nt(k, ql), NEG) - lse_t) * C)
            p_high = jnp.exp2((jnp.where(tok < seen - 32, dot_nt(k, qh), NEG) - lse_t) * C)
            ds_low = (p_low * (dot_nt(v, gl) - delta)).astype(BF)
            ds_high = (p_high * (dot_nt(v, gh) - delta)).astype(BF)
            place = pl.ds(pl.multiple_of(chunk * rows, rows), rows)
            dv_acc[place, :] += dot(p_low.astype(BF), gl) + dot(p_high.astype(BF), gh)
            dk_acc[place, :] += dot(ds_low, ql) + dot(ds_high, qh)
            return dq + dot(k_t[chunk], jnp.concatenate([ds_low, ds_high], axis=0))

        dq = lax.fori_loop(0, chunk_count(vis_s, half, tile), step, jnp.zeros((DH, LAT_TILE), F32))
        dq = (dq * SCALE).T
        for block in range(LAT_TILE // 32):
            part = dq[block * 32 : (block + 1) * 32]
            dvq_out[tile * (LAT_TILE // 32) + block, 32:48, :] = fold(part, 16).astype(BF)
    dk_out[...] = (dk_acc[...] * SCALE).astype(BF).reshape(dk_out.shape)
    dvq_out[:, 0:32, :] = dv_acc[...].astype(BF).reshape(32, 32, 128)


def tokens_of(ref, half, side):
    pieces = []
    for head in range(16):
        pieces.append(ref[2 * head + half, 0:32, side * 64 : (side + 1) * 64])
    return jnp.concatenate(pieces, axis=1)


def join_kernel(folded, out):
    for half in range(2):
        for side in range(2):
            at = half * 64 + side * 32
            out[at : at + 32, :] = tokens_of(folded, half, side)


def key_kernel(own_t, other_t, own_dk, other_dk, out):
    part = dot(own_t[...], own_dk[...]) + dot(other_t[...], other_dk[...])
    out[...] = part.astype(BF).reshape(out.shape)


def post_kernel(dk, folded, w_query, w_key, w_value, prefix_grad, latent_grad, dv, dq):
    @pl.when(pl.program_id(0) == 0)
    def _():
        for half in range(2):
            for side in range(2):
                at = half * 64 + side * 32
                dv[at : at + 32, :] = tokens_of(folded, half, side)
        for side in range(2):
            pieces = []
            for head in range(16):
                part = [folded[2 * head + half, 32:48, side * 64 : (side + 1) * 64].astype(F32) for half in range(2)]
                pieces.append(part[0] + part[1])
            dq[side * 16 : (side + 1) * 16, :] = jnp.concatenate(pieces, axis=1).astype(BF)

    prefix_grad[...] = (dot_nt(dk[...], w_key[...]) + dot_nt(dv[...], w_value[...])).astype(BF)
    latent_grad[...] = dot_nt(dq[...], w_query[...]).astype(BF)


def call(kernel, out_shape, flops=0, nbytes=0, **kwargs):
    return pl.pallas_call(
        kernel,
        out_shape=out_shape,
        compiler_params=pltpu.CompilerParams(vmem_limit_bytes=VMEM_LIMIT),
        cost_estimate=pl.CostEstimate(flops=flops, bytes_accessed=nbytes, transcendentals=0),
        **kwargs,
    )


def on_device(prefix, latents, saved, grad, visible, w_query, w_key, w_value):
    prefix, latents, saved, grad = prefix[0], latents[0], saved[0], grad[0]
    vis_row = visible
    vis_flat = visible[0]
    half = jnp.reshape(lax.axis_index("z") % 2, (1,)).astype(jnp.int32)
    core = lax.axis_index("core")
    vmem = pl.BlockSpec(memory_space=pltpu.VMEM)
    smem = pl.BlockSpec(memory_space=pltpu.SMEM)
    shape = jax.ShapeDtypeStruct

    whole = lambda rows: pl.BlockSpec((rows, 1024), lambda i: (0, 0))
    cols = lambda rows: pl.BlockSpec((rows, 256), lambda i: (0, i))
    kq, vg = call(
        pre_kernel,
        (shape((32, 48, 128), BF), shape((32, 64, 128), BF)),
        flops=2 * 288 * 1024 * 1024,
        nbytes=8 << 20,
        grid=(4,),
        in_specs=[whole(128), whole(32), cols(32), cols(32), cols(1024), cols(1024), cols(1024)],
        out_specs=(
            pl.BlockSpec((8, 48, 128), lambda i: (i, 0, 0)),
            pl.BlockSpec((8, 64, 128), lambda i: (i, 0, 0)),
        ),
    )(prefix, latents, grad, saved, w_query, w_key, w_value)
    kq = lax.all_to_all(kq, ("y", "z"), 0, 0, tiled=True)
    vg = lax.all_to_all(vg, ("y", "z"), 0, 0, tiled=True)

    at = lax.broadcasted_iota(jnp.int32, (1024, 1024), 0)
    c_at, y_at, x_at, z_at, k_at = at >> 9, (at >> 7) & 3, (at >> 5) & 3, (at >> 2) & 7, at & 3
    c_at = jnp.where(core == 0, c_at, 1 - c_at)
    wanted = (y_at * 8 + z_at) * 32 + x_at * 8 + c_at * 4 + k_at
    pick = (wanted == lax.broadcasted_iota(jnp.int32, (1024, 1024), 1)).astype(BF)
    prefix_t = dot_nt(pick, prefix).astype(BF)
    own_t = prefix_t[:512]
    other_t = lax.ppermute(prefix_t[512:], "core", [(0, 1), (1, 0)])

    stats = call(
        stats_kernel,
        shape((8, 1024), F32),
        flops=2 * 1024 * 2048 * 64,
        nbytes=1 << 19,
        in_specs=[smem, smem, vmem, vmem],
        out_specs=vmem,
        scratch_shapes=[pltpu.VMEM((1024, 128), BF)] * 2,
    )(vis_flat, half, vis_row, kq)
    other = lax.ppermute(stats, "z", [(i, i ^ 1) for i in range(8)])
    dk_fold, dvq = call(
        grad_kernel,
        (shape((32, 32, 128), BF), shape((32, 48, 128), BF)),
        flops=10 * 1024 * 2048 * 64,
        nbytes=1 << 20,
        in_specs=[smem, smem] + [vmem] * 5,
        out_specs=(vmem, vmem),
        scratch_shapes=[pltpu.VMEM((1024, 128), BF)] * 4
        + [
            pltpu.VMEM((32 // SRC_CHUNK, DH, SRC_CHUNK * 64), BF),
            pltpu.VMEM((1024, 128), F32),
            pltpu.VMEM((1024, 128), F32),
            pltpu.VMEM((1, 1024), F32),
        ],
    )(vis_flat, half, vis_row, kq, vg, stats, other)
    dk_fold = lax.all_to_all(dk_fold, ("y", "z"), 0, 0, tiled=True)
    dvq = lax.all_to_all(dvq, ("y", "z"), 0, 0, tiled=True)

    dk = call(
        join_kernel,
        shape((128, 1024), BF),
        nbytes=1 << 19,
        in_specs=[vmem],
        out_specs=vmem,
    )(dk_fold)
    dk_other = lax.ppermute(dk, "core", [(0, 1), (1, 0)])
    part = call(
        key_kernel,
        shape((16, 32, 1024), BF),
        flops=2 * 512 * 256 * 1024,
        nbytes=2 << 20,
        in_specs=[vmem] * 4,
        out_specs=vmem,
    )(own_t, other_t, dk, dk_other)
    part = lax.all_to_all(part, ("y", "x"), 0, 0, tiled=True)
    part = jnp.sum(part.astype(F32), axis=0)
    part = lax.all_to_all(part.reshape(8, 4, 1024), "z", 0, 0, tiled=True)
    key_wgrad = jnp.sum(part, axis=0)

    rows = lambda n: pl.BlockSpec((256, 1024), lambda i: (i, 0))
    prefix_grad, latent_grad = call(
        post_kernel,
        (shape((128, 1024), BF), shape((32, 1024), BF)),
        flops=2 * 288 * 1024 * 1024,
        nbytes=8 << 20,
        grid=(4,),
        in_specs=[whole(128), pl.BlockSpec((32, 48, 128), lambda i: (0, 0, 0))] + [rows(256)] * 3,
        out_specs=(cols(128), cols(32)),
        scratch_shapes=[pltpu.VMEM((128, 1024), BF), pltpu.VMEM((32, 1024), BF)],
    )(dk, dvq, w_query, w_key, w_value)
    return prefix_grad[None], latent_grad[None], key_wgrad


def solution(mesh):
    grid = Mesh(mesh.devices.reshape(4, 8, 4, 2), ("y", "z", "x", "core"))
    seq, dp = ("y", "z"), ("x", "core")
    return jax.shard_map(
        on_device,
        mesh=grid,
        in_specs=(
            P(dp, seq, None),
            P(dp, seq, None),
            P(dp, seq, None),
            P(dp, seq, None),
            P(dp, None),
            P(),
            P(),
            P(),
        ),
        out_specs=(P(dp, seq, None), P(dp, seq, None), P(seq + dp, None)),
        check_vma=False,
    )
```

time: 941 us -> 142 us (0.15)
  waiting for transfers between devices: 552 us -> 36.4 us
  blocking collectives: 278 us -> 48.9 us
  local copies, waits for them, and re-layouts: 47.9 us -> 8.96 us
  matrix products: 29.8 us -> 0.83 us
  Pallas kernels: 0 us -> 21.8 us
  starting transfers between devices: 0.2 us -> 21.3 us
  other arithmetic: 16.9 us -> 2.07 us
  between operations: 14.6 us -> 0.78 us
    unnamed x7 -> x0, waiting for transfers between devices: 413 us -> none
    pmax x1 -> x0, blocking collectives: 140 us -> none  [on_device(): lax.pmax(local_max.astype(jnp.bfloat16), 'seq').astype(local_max.dtype)]
    all_gather x3 -> x0, waiting for transfers between devices: 139 us -> none  [the longest x1 77.7 us: on_device(): lax.all_gather(own_queries, 'seq', axis=1, tiled=True)]
    psum x1 -> x0, blocking collectives: 138 us -> none  [on_device(): lax.psum((local_total * jnp.exp(local_max - global_max)).astype(jnp.bfloa...]
    all_to_all x0 -> x2, blocking collectives: none -> 48.9 us  [the longest x1 25.8 us: on_device(): kq = lax.all_to_all(kq, ('y', 'z'), 0, 0, tiled=True)]
    dot_general x31 -> x1, matrix products: 29.8 us -> 0.83 us  [dot_nt(): return lax.dot_general(a, b, NT_DIMS, preferred_element_type=F32)]
    all_to_all x0 -> x4, waiting for transfers between devices: none -> 27.9 us  [the longest x1 11.7 us: on_device(): dvq = lax.all_to_all(dvq, ('y', 'z'), 0, 0, tiled=True)]
    pallas_call x0 -> x6, Pallas kernels: none -> 21.8 us  [the longest x1 7.43 us: on_device(): call(grad_kernel, (shape((32, 32, 128), BF), shape((32, 48, 128), BF)), f...]
  transfers between devices with their start and end apart: 5 -> 7, of which waited for: 4 -> 6; matrix products, arithmetic and copies ran while one was open for 4% -> 2% of each run, Pallas kernels for 0% -> 6%
where the time goes in v1:
time: 142 us; the launch traced here: 141 us
  blocking collectives  48.9 us (34%)
  waiting for transfers between devices  36.4 us (26%)
  Pallas kernels  21.8 us (15%)
  starting transfers between devices  21.3 us (15%)
  local copies, waits for them, and re-layouts  8.96 us (6%)
  other arithmetic  2.07 us (1%)
    all_to_all x1, blocking collectives, on_device(): kq = lax.all_to_all(kq, ('y', 'z'), 0, 0, tiled=True)  25.8 us
    all_to_all x1, blocking collectives, on_device(): part = lax.all_to_all(part, ('y', 'x'), 0, 0, tiled=True)  23.1 us
    all_to_all x1, waiting for transfers between devices, on_device(): dvq = lax.all_to_all(dvq, ('y', 'z'), 0, 0, tiled=True)  11.7 us
    all_to_all x1, waiting for transfers between devices, on_device(): dk_fold = lax.all_to_all(dk_fold, ('y', 'z'), 0, 0, tiled=True)  10.5 us
    unnamed x20, local copies, waits for them, and re-layouts  8.25 us
    pallas_call x1, Pallas kernels, on_device(): call(grad_kernel, (shape((32, 32, 128), BF), shape((32, 48, 128), BF)), f...  7.43 us
    ppermute x1, waiting for transfers between devices, on_device(): other = lax.ppermute(stats, 'z', [(i, i ^ 1) for i in range(8)])  7.34 us
    all_to_all x1, starting transfers between devices, on_device(): dk_fold = lax.all_to_all(dk_fold, ('y', 'z'), 0, 0, tiled=True)  5.73 us
  transfers between devices with their start and end apart: 7, of which 6 were waited for; matrix products, arithmetic and copies ran while one was open for 2% of the time, Pallas kernels for 6%

profile of v1, /device:TPU:2, one launch (start us, length us, event | category | flops | bytes accessed | tf_op | source)
XLA Modules:
  0.0 140.9 jit_solution(4068444625077506219)
XLA Ops:
  0.6 0.0 copy-start
  0.6 1.6 %copy-done = bf16[1024,1024]{1,0:T(8,128)(2,1)S(1)} copy-done((bf16[1024,1024]{1,0:T(8,128)(2,1)S(1)}, bf16[1024,1024]{1,0:T(8,128)(2,1)}, u32[]{:S(2)}) %copy-start) | copy-done | bytes 2097176
  2.2 0.0 copy-start.2
  2.2 1.6 %copy-done.2 = bf16[1024,1024]{1,0:T(8,128)(2,1)S(1)} copy-done((bf16[1024,1024]{1,0:T(8,128)(2,1)S(1)}, bf16[1024,1024]{1,0:T(8,128)(2,1)}, u32[]{:S(2)}) %copy-start.2) | copy-done | bytes 2097176
  3.8 0.0 copy-start.4
  3.8 0.9 copy-done.4
  4.8 0.0 copy-start.6
  4.8 0.8 copy-done.6
  5.6 0.0 copy-start.7
  5.6 0.8 copy-done.7
  6.4 0.0 copy-start.8
  6.5 0.8 copy-done.8
  7.3 0.0 copy-start.9
  7.3 4.5 %shard_map.103 = (bf16[32,48,128]{2,1,0:T(8,128)(2,1)S(1)}, bf16[32,64,128]{2,1,0:T(8,128)(2,1)}) custom-call(bf16[128,1024]{1,0:T(8,128)(2,1)S(1)} %bitcast.10, bf16[32,1024]{1,0:T(8,128)(2,1)S(1)} %bitcast.11, bf16[32,1024]{1,0:T(8,128)(2,1)S(1)} %bitcast.12, bf16[32,1024]{1,0:T(8,128)(2,1)S(1)} %bitcast.13, bf16[1024,1024]{1,0:T(8,128)(2,1)S(1)} %copy-done, ...), custom_call_target="tpu_custom_call" | custom-call | flops 603979776 | bytes 8388608 | tf_op jit(solution)/shard_map/pallas_call | solution.py:242
  11.8 25.8 %all_to_all.30.kq = bf16[32,48,128]{2,1,0:T(8,128)(2,1)S(1)} all-to-all(bf16[32,48,128]{2,1,0:T(8,128)(2,1)S(1)} %get-tuple-element.9), channel_id=1, replica_groups=mesh['y'=4,'z'=8,'x'=4,'core'=2] {'y','z'}, dimensions={0} | all-to-all | bytes 786432 | tf_op jit(solution)/shard_map/all_to_all | solution.py:254
  37.6 5.1 %all-to-all-start.1 = ((bf16[32,64,128]{2,1,0:T(8,128)(2,1)}), bf16[32,64,128]{2,1,0:T(8,128)(2,1)S(1)}, u32[]{:S(2)}, u32[]{:S(2)}) async-start(bf16[32,64,128]{2,1,0:T(8,128)(2,1)} %get-tuple-element.10), calls=%async_computation.1 | async-start | bytes 1048576 | tf_op jit(solution)/shard_map/all_to_all | solution.py:255
  42.8 0.0 copy-done.9
  42.8 4.1 %shard_map.104.own = f32[8,1024]{1,0:T(8,128)S(1)} custom-call(s32[1024]{0:T(1024)S(1)} %bitcast.14, s32[1]{0:T(128)} %bitcast.1.half_s, s32[1,1024]{1,0:T(1,128)S(1)} %copy-done.9, bf16[32,48,128]{2,1,0:T(8,128)(2,1)S(1)} %all_to_all.30.kq), custom_call_target="tpu_custom_call" | custom-call | flops 268435456 | bytes 524288 | tf_op jit(solution)/shard_map/pallas_call | solution.py:266
  46.9 0.0 copy-start.5
  46.9 1.9 %collective-permute-start = (f32[8,1024]{1,0:T(8,128)S(1)}, f32[8,1024]{1,0:T(8,128)S(1)}, u32[]{:S(2)}, u32[]{:S(2)}) collective-permute-start(f32[8,1024]{1,0:T(8,128)S(1)} %shard_map.104.own), channel_id=1, source_target_pairs={{0,8},{8,0},{16,24},{24,16},{32,40},{40,32},{48,56},{56,48},{1,9},... | collective-permute-start | bytes 98312 | tf_op jit(solution)/shard_map/ppermute | solution.py:275
  48.9 7.3 %collective-permute-done.other = f32[8,1024]{1,0:T(8,128)S(1)} collective-permute-done((f32[8,1024]{1,0:T(8,128)S(1)}, f32[8,1024]{1,0:T(8,128)S(1)}, u32[]{:S(2)}, u32[]{:S(2)}) %collective-permute-start) | collective-permute-done | bytes 32800 | tf_op jit(solution)/shard_map/ppermute | solution.py:275
  56.2 3.1 %all-to-all-done.1.vg = bf16[32,64,128]{2,1,0:T(8,128)(2,1)S(1)} async-done(((bf16[32,64,128]{2,1,0:T(8,128)(2,1)}), bf16[32,64,128]{2,1,0:T(8,128)(2,1)S(1)}, u32[]{:S(2)}, u32[]{:S(2)}) %all-to-all-start.1) | async-done | bytes 524320 | tf_op jit(solution)/shard_map/all_to_all | solution.py:255
  59.3 7.4 %shard_map.105 = (bf16[32,32,128]{2,1,0:T(8,128)(2,1)}, bf16[32,48,128]{2,1,0:T(8,128)(2,1)}) custom-call(s32[1024]{0:T(1024)S(1)} %bitcast.15, s32[1]{0:T(128)} %bitcast.1.half_s, s32[1,1024]{1,0:T(1,128)S(1)} %copy-done.9, bf16[32,48,128]{2,1,0:T(8,128)(2,1)S(1)} %all_to_all.30.kq, bf16[32,64,128]{2,1,0:T(8,128)(2,1)S(1)} %all-to-all-done.1.vg, ...), custom_call_target="tpu_custom_call" | custom-call | flops 1342177280 | bytes 1048576 | tf_op jit(solution)/shard_map/pallas_call | solution.py:276
  66.7 5.7 %all-to-all-start.2 = ((bf16[32,32,128]{2,1,0:T(8,128)(2,1)}), bf16[32,32,128]{2,1,0:T(8,128)(2,1)S(1)}, u32[]{:S(2)}, u32[]{:S(2)}) async-start(bf16[32,32,128]{2,1,0:T(8,128)(2,1)} %get-tuple-element.11), calls=%async_computation.2 | async-start | bytes 524288 | tf_op jit(solution)/shard_map/all_to_all | solution.py:291
  72.5 0.0 copy-done.5
  72.5 0.8 fusion.2
  73.3 10.5 %all-to-all-done.2.folded = bf16[32,32,128]{2,1,0:T(8,128)(2,1)S(1)} async-done(((bf16[32,32,128]{2,1,0:T(8,128)(2,1)}), bf16[32,32,128]{2,1,0:T(8,128)(2,1)S(1)}, u32[]{:S(2)}, u32[]{:S(2)}) %all-to-all-start.2) | async-done | bytes 262176 | tf_op jit(solution)/shard_map/all_to_all | solution.py:291
  83.8 0.1 shard_map.106.dk.own_dk
  83.9 0.1 collective-permute-start.2
  84.1 0.6 collective-permute-start.1
  84.7 1.1 collective-permute-done.1.other_t
  85.8 0.0 collective-permute-done.2.other_dk
  85.8 0.7 shard_map.108
  86.4 0.0 copy-start.1
  86.5 23.1 %all_to_all.31 = bf16[16,32,1024]{2,1,0:T(8,128)(2,1)} all-to-all(bf16[16,32,1024]{2,1,0:T(8,128)(2,1)S(1)} %shard_map.108), channel_id=1, replica_groups=mesh['y'=4,'z'=8,'x'=4,'core'=2] {'y','x'}, dimensions={0} | all-to-all | bytes 2097152 | tf_op jit(solution)/shard_map/all_to_all | solution.py:310
  109.6 3.9 %all-to-all-start.3 = ((bf16[32,48,128]{2,1,0:T(8,128)(2,1)}), bf16[32,48,128]{2,1,0:T(8,128)(2,1)S(1)}, u32[]{:S(2)}, u32[]{:S(2)}) async-start(bf16[32,48,128]{2,1,0:T(8,128)(2,1)} %get-tuple-element.12), calls=%async_computation.3 | async-start | bytes 786432 | tf_op jit(solution)/shard_map/all_to_all | solution.py:292
  113.5 1.4 %convert_reduce_fusion = f32[32,1024]{1,0:T(8,128)S(1)} fusion(bf16[16,32,1024]{2,1,0:T(8,128)(2,1)} %all_to_all.31), kind=kLoop, calls=%fused_computation.2 | loop fusion | flops 1015808 | bytes 1179648 | tf_op jit(solution)/shard_map/reduce_sum | solution.py:311
  114.9 0.7 reshape.13
  115.6 11.7 %all-to-all-done.3.folded = bf16[32,48,128]{2,1,0:T(8,128)(2,1)S(1)} async-done(((bf16[32,48,128]{2,1,0:T(8,128)(2,1)}), bf16[32,48,128]{2,1,0:T(8,128)(2,1)S(1)}, u32[]{:S(2)}, u32[]{:S(2)}) %all-to-all-start.3) | async-done | bytes 393248 | tf_op jit(solution)/shard_map/all_to_all | solution.py:292
  127.3 3.9 %all-to-all-start.5 = ((f32[8,4,1024]{2,1,0:T(4,128)}), f32[8,4,1024]{2,1,0:T(4,128)S(1)}, u32[]{:S(2)}, u32[]{:S(2)}) async-start(f32[8,4,1024]{2,1,0:T(4,128)} %reshape.13), calls=%async_computation.5 | async-start | bytes 262144 | tf_op jit(solution)/shard_map/all_to_all | solution.py:312
  131.2 0.0 copy-done.1
  131.2 0.0 copy-start.3
  131.2 1.6 %copy-done.3 = bf16[1024,1024]{1,0:T(8,128)(2,1)S(1)} copy-done((bf16[1024,1024]{1,0:T(8,128)(2,1)S(1)}, bf16[1024,1024]{1,0:T(8,128)(2,1)}, u32[]{:S(2)}) %copy-start.3) | copy-done | bytes 2097176
  132.8 4.8 %shard_map.107 = (bf16[128,1024]{1,0:T(8,128)(2,1)}, bf16[32,1024]{1,0:T(8,128)(2,1)}) custom-call(bf16[128,1024]{1,0:T(8,128)(2,1)S(1)} %shard_map.106.dk.own_dk, bf16[32,48,128]{2,1,0:T(8,128)(2,1)S(1)} %all-to-all-done.3.folded, bf16[1024,1024]{1,0:T(8,128)(2,1)S(1)} %copy-done.1, bf16[1024,1024]{1,0:T(8,128)(2,1)S(1)} %copy-done.3, ...), custom_call_target="tpu_custom_call" | custom-call | flops 603979776 | bytes 8388608 | tf_op jit(solution)/shard_map/pallas_call | solution.py:316
  137.6 2.6 %all-to-all-done.5 = f32[8,4,1024]{2,1,0:T(4,128)S(1)} async-done(((f32[8,4,1024]{2,1,0:T(4,128)}), f32[8,4,1024]{2,1,0:T(4,128)S(1)}, u32[]{:S(2)}, u32[]{:S(2)}) %all-to-all-start.5) | async-done | bytes 131104 | tf_op jit(solution)/shard_map/all_to_all | solution.py:312
  140.3 0.6 reduce_sum.19
  (2 shorter events, 0.0 us)
Async XLA Ops:
  0.6 1.6 %copy-start = (bf16[1024,1024]{1,0:T(8,128)(2,1)S(1)}, bf16[1024,1024]{1,0:T(8,128)(2,1)}, u32[]{:S(2)}) copy-start(bf16[1024,1024]{1,0:T(8,128)(2,1)} %w_query.3) | copy-start | bytes 6291460
  2.2 1.6 %copy-start.2 = (bf16[1024,1024]{1,0:T(8,128)(2,1)S(1)}, bf16[1024,1024]{1,0:T(8,128)(2,1)}, u32[]{:S(2)}) copy-start(bf16[1024,1024]{1,0:T(8,128)(2,1)} %w_key.3) | copy-start | bytes 6291460
  3.8 0.9 copy-start.4
  4.8 0.8 copy-start.6
  5.6 0.8 copy-start.7
  6.4 0.8 copy-start.8
  7.3 35.5 %copy-start.9 = (s32[1,1024]{1,0:T(1,128)S(1)}, s32[1,1024]{1,0:T(1,128)}, u32[]{:S(2)}) copy-start(s32[1,1024]{1,0:T(1,128)} %vis.3) | copy-start | bytes 12292
  37.6 21.7 %all-to-all-start.1 = ((bf16[32,64,128]{2,1,0:T(8,128)(2,1)}), bf16[32,64,128]{2,1,0:T(8,128)(2,1)S(1)}, u32[]{:S(2)}, u32[]{:S(2)}) async-start(bf16[32,64,128]{2,1,0:T(8,128)(2,1)} %get-tuple-element.10), calls=%async_computation.1 | async-start | bytes 1048576 | tf_op jit(solution)/shard_map/all_to_all | solution.py:255
  46.9 25.6 %copy-start.5 = (bf16[1,128,1024]{2,1,0:T(8,128)(2,1)S(1)}, bf16[1,128,1024]{2,1,0:T(8,128)(2,1)}, u32[]{:S(2)}) copy-start(bf16[1,128,1024]{2,1,0:T(8,128)(2,1)} %param.8) | copy-start | bytes 786436
  46.9 9.3 %collective-permute-start = (f32[8,1024]{1,0:T(8,128)S(1)}, f32[8,1024]{1,0:T(8,128)S(1)}, u32[]{:S(2)}, u32[]{:S(2)}) collective-permute-start(f32[8,1024]{1,0:T(8,128)S(1)} %shard_map.104.own), channel_id=1, source_target_pairs={{0,8},{8,0},{16,24},{24,16},{32,40},{40,32},{48,56},{56,48},{1,9},... | collective-permute-start | bytes 98312 | tf_op jit(solution)/shard_map/ppermute | solution.py:275
  66.7 17.1 %all-to-all-start.2 = ((bf16[32,32,128]{2,1,0:T(8,128)(2,1)}), bf16[32,32,128]{2,1,0:T(8,128)(2,1)S(1)}, u32[]{:S(2)}, u32[]{:S(2)}) async-start(bf16[32,32,128]{2,1,0:T(8,128)(2,1)} %get-tuple-element.11), calls=%async_computation.2 | async-start | bytes 524288 | tf_op jit(solution)/shard_map/all_to_all | solution.py:291
  83.9 1.8 %collective-permute-start.2 = (bf16[128,1024]{1,0:T(8,128)(2,1)S(1)}, bf16[128,1024]{1,0:T(8,128)(2,1)S(1)}, u32[]{:S(2)}, u32[]{:S(2)}) collective-permute-start(bf16[128,1024]{1,0:T(8,128)(2,1)S(1)} %shard_map.106.dk.own_dk), channel_id=1, source_target_pairs={{0,1},{1,0},{2,3},{3,2},{4,5},{5,4},{6,7},{7,6},{8,9},{9,8},{10,11... | collective-permute-start | bytes 786440 | tf_op jit(solution)/shard_map/ppermute | solution.py:301
  84.1 1.7 %collective-permute-start.1 = (bf16[512,128]{1,0:T(8,128)(2,1)S(1)}, bf16[512,128]{1,0:T(8,128)(2,1)S(1)}, u32[]{:S(2)}, u32[]{:S(2)}) collective-permute-start(bf16[512,128]{1,0:T(8,128)(2,1)S(1)} %get-tuple-element.15), channel_id=1, source_target_pairs={{0,1},{1,0},{2,3},{3,2},{4,5},{5,4},{6,7},{7,6},{8,9},{9,8},{10,11... | collective-permute-start | bytes 393224 | tf_op jit(solution)/shard_map/ppermute | solution.py:264
  86.4 44.8 %copy-start.1 = (bf16[1024,1024]{1,0:T(8,128)(2,1)S(1)}, bf16[1024,1024]{1,0:T(8,128)(2,1)}, u32[]{:S(2)}) copy-start(bf16[1024,1024]{1,0:T(8,128)(2,1)} %w_query.3) | copy-start | bytes 6291460
  109.6 17.7 %all-to-all-start.3 = ((bf16[32,48,128]{2,1,0:T(8,128)(2,1)}), bf16[32,48,128]{2,1,0:T(8,128)(2,1)S(1)}, u32[]{:S(2)}, u32[]{:S(2)}) async-start(bf16[32,48,128]{2,1,0:T(8,128)(2,1)} %get-tuple-element.12), calls=%async_computation.3 | async-start | bytes 786432 | tf_op jit(solution)/shard_map/all_to_all | solution.py:292
  127.3 13.0 %all-to-all-start.5 = ((f32[8,4,1024]{2,1,0:T(4,128)}), f32[8,4,1024]{2,1,0:T(4,128)S(1)}, u32[]{:S(2)}, u32[]{:S(2)}) async-start(f32[8,4,1024]{2,1,0:T(4,128)} %reshape.13), calls=%async_computation.5 | async-start | bytes 262144 | tf_op jit(solution)/shard_map/all_to_all | solution.py:312
  131.2 1.6 %copy-start.3 = (bf16[1024,1024]{1,0:T(8,128)(2,1)S(1)}, bf16[1024,1024]{1,0:T(8,128)(2,1)}, u32[]{:S(2)}) copy-start(bf16[1024,1024]{1,0:T(8,128)(2,1)} %w_key.3) | copy-start | bytes 6291460

commit v2 on v1

--- a/solution.py
+++ b/solution.py
@@ -16,7 +16,6 @@
 SCALE = 1.0 / math.sqrt(DH)
 C = SCALE * math.log2(math.e)
 NT_DIMS = (((1,), (1,)), ((), ()))
-VMEM_LIMIT = 48 * 1024 * 1024
 LAT_TILE = 256
 SRC_CHUNK = 8
 
@@ -37,39 +36,31 @@
     return jnp.concatenate([x[:rows], x[rows:]], axis=1)
 
 
-def pre_kernel(prefix, latents, grad, saved, w_query, w_key, w_value, kq, vg):
+def pre_kernel(prefix, latents, grad, saved, w_query, w_key, w_value, out):
     keys = dot(prefix[...], w_key[...]).astype(BF)
     values = dot(prefix[...], w_value[...]).astype(BF)
     queries = dot(latents[...], w_query[...]).astype(BF)
     g = grad[...]
     product = g.astype(F32) * saved[...].astype(F32)
-    lat = product.shape[0]
-    product = jnp.concatenate([product, jnp.zeros((128 - lat, product.shape[1]), F32)], axis=0)
-    product = product.T
-    half_tok = prefix.shape[0] // 2
+    product = jnp.concatenate([product, jnp.zeros((96, product.shape[1]), F32)], axis=0).T
+    row = lax.broadcasted_iota(jnp.int32, (8, 128), 0)
     for head in range(4):
         cols = slice(head * DH, (head + 1) * DH)
         delta = jnp.sum(product[cols], axis=0, keepdims=True)
-        high = delta.astype(BF)
-        rest = delta - high.astype(F32)
-        mid = rest.astype(BF)
-        low = (rest - mid.astype(F32)).astype(BF)
-        row = lax.broadcasted_iota(jnp.int32, (16, 128), 0)
-        parts = jnp.where(
-            row == 0,
-            high.astype(F32),
-            jnp.where(row == 1, mid.astype(F32), jnp.where(row == 2, low.astype(F32), 0.0)),
-        ).astype(BF)
-        q_fold = fold(queries[:, cols], lat // 2)
-        g_fold = fold(g[:, cols], lat // 2)
+        high = delta.astype(BF).astype(F32)
+        mid = (delta - high).astype(BF).astype(F32)
+        low = delta - high - mid
+        parts = jnp.where(row == 0, high, jnp.where(row == 1, mid, jnp.where(row == 2, low, 0.0)))
+        q_fold = fold(queries[:, cols], 16)
+        g_fold = fold(g[:, cols], 16)
         for half in range(2):
-            toks = slice(half * half_tok, (half + 1) * half_tok)
+            toks = slice(half * 64, (half + 1) * 64)
             dest = 2 * head + half
-            kq[dest, 0:32, :] = fold(keys[toks, cols], half_tok // 2)
-            kq[dest, 32:48, :] = q_fold
-            vg[dest, 0:32, :] = fold(values[toks, cols], half_tok // 2)
-            vg[dest, 32:48, :] = g_fold
-            vg[dest, 48:64, :] = parts
+            out[dest, 0:32, :] = fold(keys[toks, cols], 32)
+            out[dest, 32:64, :] = fold(values[toks, cols], 32)
+            out[dest, 64:80, :] = q_fold
+            out[dest, 80:96, :] = g_fold
+            out[dest, 96:104, :] = parts.astype(BF)
 
 
 def unfold(folded, low_ref, high_ref):
@@ -95,9 +86,9 @@
     return jnp.minimum((seen + span - 1) // span, 32 // SRC_CHUNK)
 
 
-def stats_kernel(vis_s, half_s, vis, kq, out, q_low, q_high):
+def stats_kernel(vis_s, half_s, vis, data, out, q_low, q_high):
     half = half_s[0]
-    unfold(kq[:, 32:48, :], q_low, q_high)
+    unfold(data[:, 64:80, :], q_low, q_high)
     rows = SRC_CHUNK * 32
     for tile in range(1024 // LAT_TILE):
         lanes = slice(tile * LAT_TILE, (tile + 1) * LAT_TILE)
@@ -107,7 +98,7 @@
 
         def step(chunk, carry):
             top, total = carry
-            k = kq[pl.ds(chunk * SRC_CHUNK, SRC_CHUNK), 0:32, :].reshape(rows, 128)
+            k = data[pl.ds(chunk * SRC_CHUNK, SRC_CHUNK), 0:32, :].reshape(rows, 128)
             tok = chunk_tokens(chunk, half, rows, LAT_TILE)
             s_low = jnp.where(tok < seen, dot_nt(k, ql), NEG)
             s_high = jnp.where(tok < seen - 32, dot_nt(k, qh), NEG)
@@ -125,14 +116,14 @@
     out[2:8, :] = jnp.zeros((6, 1024), F32)
 
 
-def grad_kernel(vis_s, half_s, vis, kq, vg, own, other, dk_out, dvq_out,
+def grad_kernel(vis_s, half_s, vis, data, own, other, out,
                 q_low, q_high, g_low, g_high, k_t, dk_acc, dv_acc, delta_ref):
     half = half_s[0]
     rows = SRC_CHUNK * 32
-    unfold(kq[:, 32:48, :], q_low, q_high)
-    unfold(vg[:, 32:48, :], g_low, g_high)
+    unfold(data[:, 64:80, :], q_low, q_high)
+    unfold(data[:, 80:96, :], g_low, g_high)
     for chunk in range(32 // SRC_CHUNK):
-        k = kq[chunk * SRC_CHUNK : (chunk + 1) * SRC_CHUNK, 0:32, :].reshape(rows, 128)
+        k = data[chunk * SRC_CHUNK : (chunk + 1) * SRC_CHUNK, 0:32, :].reshape(rows, 128)
         turned = k.T
         k_t[chunk] = jnp.concatenate([turned[0:64], turned[64:128]], axis=1)
     dk_acc[...] = jnp.zeros_like(dk_acc)
@@ -141,7 +132,7 @@
     for block in range(8):
         joined = jnp.zeros((1, 128), F32)
         for place in range(4):
-            parts = vg[4 * block + place, 48:64, :].astype(F32)
+            parts = data[4 * block + place, 96:104, :].astype(F32)
             parts = jnp.sum(parts, axis=0, keepdims=True)
             if place:
                 parts = pltpu.roll(parts, 32 * place, 1)
@@ -159,8 +150,8 @@
 
         def step(chunk, dq):
             srcs = pl.ds(chunk * SRC_CHUNK, SRC_CHUNK)
-            k = kq[srcs, 0:32, :].reshape(rows, 128)
-            v = vg[srcs, 0:32, :].reshape(rows, 128)
+            k = data[srcs, 0:32, :].reshape(rows, 128)
+            v = data[srcs, 32:64, :].reshape(rows, 128)
             tok = chunk_tokens(chunk, half, rows, LAT_TILE)
             p_low = jnp.exp2((jnp.where(tok < seen, dot_nt(k, ql), NEG) - lse_t) * C)
             p_high = jnp.exp2((jnp.where(tok < seen - 32, dot_nt(k, qh), NEG) - lse_t) * C)
@@ -175,15 +166,15 @@
         dq = (dq * SCALE).T
         for block in range(LAT_TILE // 32):
             part = dq[block * 32 : (block + 1) * 32]
-            dvq_out[tile * (LAT_TILE // 32) + block, 32:48, :] = fold(part, 16).astype(BF)
-    dk_out[...] = (dk_acc[...] * SCALE).astype(BF).reshape(dk_out.shape)
-    dvq_out[:, 0:32, :] = dv_acc[...].astype(BF).reshape(32, 32, 128)
-
-
-def tokens_of(ref, half, side):
+            out[tile * (LAT_TILE // 32) + block, 64:80, :] = fold(part, 16).astype(BF)
+    out[:, 0:32, :] = (dk_acc[...] * SCALE).astype(BF).reshape(32, 32, 128)
+    out[:, 32:64, :] = dv_acc[...].astype(BF).reshape(32, 32, 128)
+
+
+def tokens_of(ref, half, side, start):
     pieces = []
     for head in range(16):
-        pieces.append(ref[2 * head + half, 0:32, side * 64 : (side + 1) * 64])
+        pieces.append(ref[2 * head + half, start : start + 32, side * 64 : (side + 1) * 64])
     return jnp.concatenate(pieces, axis=1)
 
 
@@ -191,7 +182,7 @@
     for half in range(2):
         for side in range(2):
             at = half * 64 + side * 32
-            out[at : at + 32, :] = tokens_of(folded, half, side)
+            out[at : at + 32, :] = tokens_of(folded, half, side, 0)
 
 
 def key_kernel(own_t, other_t, own_dk, other_dk, out):
@@ -205,11 +196,11 @@
         for half in range(2):
             for side in range(2):
                 at = half * 64 + side * 32
-                dv[at : at + 32, :] = tokens_of(folded, half, side)
+                dv[at : at + 32, :] = tokens_of(folded, half, side, 32)
         for side in range(2):
             pieces = []
             for head in range(16):
-                part = [folded[2 * head + half, 32:48, side * 64 : (side + 1) * 64].astype(F32) for half in range(2)]
+                part = [folded[2 * head + half, 64:80, side * 64 : (side + 1) * 64].astype(F32) for half in range(2)]
                 pieces.append(part[0] + part[1])
             dq[side * 16 : (side + 1) * 16, :] = jnp.concatenate(pieces, axis=1).astype(BF)
 
@@ -217,11 +208,11 @@
     latent_grad[...] = dot_nt(dq[...], w_query[...]).astype(BF)
 
 
-def call(kernel, out_shape, flops=0, nbytes=0, **kwargs):
+def call(kernel, out_shape, flops=0, nbytes=0, limit=48, **kwargs):
     return pl.pallas_call(
         kernel,
         out_shape=out_shape,
-        compiler_params=pltpu.CompilerParams(vmem_limit_bytes=VMEM_LIMIT),
+        compiler_params=pltpu.CompilerParams(vmem_limit_bytes=limit << 20),
         cost_estimate=pl.CostEstimate(flops=flops, bytes_accessed=nbytes, transcendentals=0),
         **kwargs,
     )
@@ -239,21 +230,6 @@
 
     whole = lambda rows: pl.BlockSpec((rows, 1024), lambda i: (0, 0))
     cols = lambda rows: pl.BlockSpec((rows, 256), lambda i: (0, i))
-    kq, vg = call(
-        pre_kernel,
-        (shape((32, 48, 128), BF), shape((32, 64, 128), BF)),
-        flops=2 * 288 * 1024 * 1024,
-        nbytes=8 << 20,
-        grid=(4,),
-        in_specs=[whole(128), whole(32), cols(32), cols(32), cols(1024), cols(1024), cols(1024)],
-        out_specs=(
-            pl.BlockSpec((8, 48, 128), lambda i: (i, 0, 0)),
-            pl.BlockSpec((8, 64, 128), lambda i: (i, 0, 0)),
-        ),
-    )(prefix, latents, grad, saved, w_query, w_key, w_value)
-    kq = lax.all_to_all(kq, ("y", "z"), 0, 0, tiled=True)
-    vg = lax.all_to_all(vg, ("y", "z"), 0, 0, tiled=True)
-
     at = lax.broadcasted_iota(jnp.int32, (1024, 1024), 0)
     c_at, y_at, x_at, z_at, k_at = at >> 9, (at >> 7) & 3, (at >> 5) & 3, (at >> 2) & 7, at & 3
     c_at = jnp.where(core == 0, c_at, 1 - c_at)
@@ -263,6 +239,18 @@
     own_t = prefix_t[:512]
     other_t = lax.ppermute(prefix_t[512:], "core", [(0, 1), (1, 0)])
 
+    data = call(
+        pre_kernel,
+        shape((32, 104, 128), BF),
+        limit=60,
+        flops=2 * 288 * 1024 * 1024,
+        nbytes=8 << 20,
+        grid=(4,),
+        in_specs=[whole(128), whole(32), cols(32), cols(32), cols(1024), cols(1024), cols(1024)],
+        out_specs=pl.BlockSpec((8, 104, 128), lambda i: (i, 0, 0)),
+    )(prefix, latents, grad, saved, w_query, w_key, w_value)
+    data = lax.all_to_all(data, ("y", "z"), 0, 0, tiled=True)
+
     stats = call(
         stats_kernel,
         shape((8, 1024), F32),
@@ -271,15 +259,15 @@
         in_specs=[smem, smem, vmem, vmem],
         out_specs=vmem,
         scratch_shapes=[pltpu.VMEM((1024, 128), BF)] * 2,
-    )(vis_flat, half, vis_row, kq)
+    )(vis_flat, half, vis_row, data)
     other = lax.ppermute(stats, "z", [(i, i ^ 1) for i in range(8)])
-    dk_fold, dvq = call(
+    back = call(
         grad_kernel,
-        (shape((32, 32, 128), BF), shape((32, 48, 128), BF)),
+        shape((32, 80, 128), BF),
         flops=10 * 1024 * 2048 * 64,
         nbytes=1 << 20,
-        in_specs=[smem, smem] + [vmem] * 5,
-        out_specs=(vmem, vmem),
+        in_specs=[smem, smem] + [vmem] * 4,
+        out_specs=vmem,
         scratch_shapes=[pltpu.VMEM((1024, 128), BF)] * 4
         + [
             pltpu.VMEM((32 // SRC_CHUNK, DH, SRC_CHUNK * 64), BF),
@@ -287,9 +275,8 @@
             pltpu.VMEM((1024, 128), F32),
             pltpu.VMEM((1, 1024), F32),
         ],
-    )(vis_flat, half, vis_row, kq, vg, stats, other)
-    dk_fold = lax.all_to_all(dk_fold, ("y", "z"), 0, 0, tiled=True)
-    dvq = lax.all_to_all(dvq, ("y", "z"), 0, 0, tiled=True)
+    )(vis_flat, half, vis_row, data, stats, other)
+    back = lax.all_to_all(back, ("y", "z"), 0, 0, tiled=True)
 
     dk = call(
         join_kernel,
@@ -297,7 +284,7 @@
         nbytes=1 << 19,
         in_specs=[vmem],
         out_specs=vmem,
-    )(dk_fold)
+    )(back)
     dk_other = lax.ppermute(dk, "core", [(0, 1), (1, 0)])
     part = call(
         key_kernel,
@@ -316,13 +303,14 @@
     prefix_grad, latent_grad = call(
         post_kernel,
         (shape((128, 1024), BF), shape((32, 1024), BF)),
+        limit=60,
         flops=2 * 288 * 1024 * 1024,
         nbytes=8 << 20,
         grid=(4,),
-        in_specs=[whole(128), pl.BlockSpec((32, 48, 128), lambda i: (0, 0, 0))] + [rows(256)] * 3,
+        in_specs=[whole(128), pl.BlockSpec((32, 80, 128), lambda i: (0, 0, 0))] + [rows(256)] * 3,
         out_specs=(cols(128), cols(32)),
         scratch_shapes=[pltpu.VMEM((128, 1024), BF), pltpu.VMEM((32, 1024), BF)],
-    )(dk, dvq, w_query, w_key, w_value)
+    )(dk, back, w_query, w_key, w_value)
     return prefix_grad[None], latent_grad[None], key_wgrad
 
 

time: 142 us -> 123 us (0.87)
  blocking collectives: 48.9 us -> 22.8 us
  waiting for transfers between devices: 36.4 us -> 48.8 us
  local copies, waits for them, and re-layouts: 8.96 us -> 0.72 us
  Pallas kernels: 21.8 us -> 23.9 us
  starting transfers between devices: 21.3 us -> 23.2 us
    all_to_all x1 -> x0, blocking collectives: 25.8 us -> none  [on_device(): kq = lax.all_to_all(kq, ('y', 'z'), 0, 0, tiled=True)]
    all_to_all x3 -> x2, waiting for transfers between devices: 25.3 us -> 42.2 us  [the longest x1 24.8 us: on_device(): data = lax.all_to_all(data, ('y', 'z'), 0, 0, tiled=True)]
    unnamed x20 -> x8, local copies, waits for them, and re-layouts: 8.25 us -> 0.02 us
    ppermute x1, waiting for transfers between devices: 7.34 us -> 2.4 us  [on_device(): other = lax.ppermute(stats, 'z', [(i, i ^ 1) for i in range(8)])]
    pallas_call x3, Pallas kernels: 16.8 us -> 18.9 us  [the longest x1 7.47 us: on_device(): call(grad_kernel, shape((32, 80, 128), BF), flops=10 * 1024 * 2048 * 64,...]
    all_to_all x3 -> x2, starting transfers between devices: 14.7 us -> 16.2 us  [the longest x1 11.5 us: on_device(): data = lax.all_to_all(data, ('y', 'z'), 0, 0, tiled=True)]
  transfers between devices with their start and end apart: 7 -> 6, of which waited for: 6 -> 5; matrix products, arithmetic and copies ran while one was open for 2% -> 1% of each run, Pallas kernels for 6% -> 5%
where the time goes in v2:
time: 123 us; the launch traced here: 122 us
  waiting for transfers between devices  48.8 us (40%)
  Pallas kernels  23.9 us (19%)
  starting transfers between devices  23.2 us (19%)
  blocking collectives  22.8 us (19%)
    all_to_all x1, waiting for transfers between devices, on_device(): data = lax.all_to_all(data, ('y', 'z'), 0, 0, tiled=True)  24.8 us
    all_to_all x1, blocking collectives, on_device(): part = lax.all_to_all(part, ('y', 'x'), 0, 0, tiled=True)  22.8 us
    all_to_all x1, waiting for transfers between devices, on_device(): back = lax.all_to_all(back, ('y', 'z'), 0, 0, tiled=True)  17.4 us
    all_to_all x1, starting transfers between devices, on_device(): data = lax.all_to_all(data, ('y', 'z'), 0, 0, tiled=True)  11.5 us
    pallas_call x1, Pallas kernels, on_device(): call(grad_kernel, shape((32, 80, 128), BF), flops=10 * 1024 * 2048 * 64,...  7.47 us
    pallas_call x1, Pallas kernels, on_device(): call(post_kernel, (shape((128, 1024), BF), shape((32, 1024), BF)), limit=...  6.02 us
    pallas_call x1, Pallas kernels, on_device(): call(pre_kernel, shape((32, 104, 128), BF), limit=60, flops=2 * 288 * 102...  5.45 us
    all_to_all x1, starting transfers between devices, on_device(): part = lax.all_to_all(part.reshape(8, 4, 1024), 'z', 0, 0, tiled=True)  4.72 us
  transfers between devices with their start and end apart: 6, of which 5 were waited for; matrix products, arithmetic and copies ran while one was open for 1% of the time, Pallas kernels for 5%

profile of v2, /device:TPU:2, one launch (start us, length us, event | category | flops | bytes accessed | tf_op | source)
XLA Modules:
  0.0 121.8 jit_solution(12704950223355999234)
XLA Ops:
  0.6 0.0 copy-start.2
  0.6 5.5 %shard_map.103 = bf16[32,104,128]{2,1,0:T(8,128)(2,1)} custom-call(bf16[128,1024]{1,0:T(8,128)(2,1)} %bitcast.12, bf16[32,1024]{1,0:T(8,128)(2,1)} %bitcast.13, bf16[32,1024]{1,0:T(8,128)(2,1)} %bitcast.14, bf16[32,1024]{1,0:T(8,128)(2,1)} %bitcast.15, bf16[1024,1024]{1,0:T(8,128)(2,1)} %w_query.3, bf16[1024,1024]{1,0:T(8,128)(2,1)} %w_key.3, ...), custom_call_target="tpu_custom_call" | custom-call | flops 603979776 | bytes 8388608 | tf_op jit(solution)/shard_map/pallas_call | solution.py:242
  6.1 11.5 %all-to-all-start = ((bf16[32,104,128]{2,1,0:T(8,128)(2,1)}), bf16[32,104,128]{2,1,0:T(8,128)(2,1)S(1)}, u32[]{:S(2)}, u32[]{:S(2)}) async-start(bf16[32,104,128]{2,1,0:T(8,128)(2,1)} %shard_map.103), calls=%async_computation | async-start | bytes 1703936 | tf_op jit(solution)/shard_map/all_to_all | solution.py:252
  17.6 24.8 %all-to-all-done.data = bf16[32,104,128]{2,1,0:T(8,128)(2,1)S(1)} async-done(((bf16[32,104,128]{2,1,0:T(8,128)(2,1)}), bf16[32,104,128]{2,1,0:T(8,128)(2,1)S(1)}, u32[]{:S(2)}, u32[]{:S(2)}) %all-to-all-start) | async-done | bytes 852000 | tf_op jit(solution)/shard_map/all_to_all | solution.py:252
  42.4 0.0 copy-done.2
  42.4 4.2 %shard_map.104.own = f32[8,1024]{1,0:T(8,128)S(1)} custom-call(s32[1024]{0:T(1024)S(1)} %bitcast.10, s32[1]{0:T(128)} %bitcast.1.half_s, s32[1,1024]{1,0:T(1,128)S(1)} %copy-done.2, bf16[32,104,128]{2,1,0:T(8,128)(2,1)S(1)} %all-to-all-done.data), custom_call_target="tpu_custom_call" | custom-call | flops 268435456 | bytes 524288 | tf_op jit(solution)/shard_map/pallas_call | solution.py:254
  46.6 0.0 copy-start.3
  46.6 1.6 %collective-permute-start = (f32[8,1024]{1,0:T(8,128)S(1)}, f32[8,1024]{1,0:T(8,128)S(1)}, u32[]{:S(2)}, u32[]{:S(2)}) collective-permute-start(f32[8,1024]{1,0:T(8,128)S(1)} %shard_map.104.own), channel_id=1, source_target_pairs={{0,8},{8,0},{16,24},{24,16},{32,40},{40,32},{48,56},{56,48},{1,9},... | collective-permute-start | bytes 98312 | tf_op jit(solution)/shard_map/ppermute | solution.py:263
  48.2 2.4 %collective-permute-done.other = f32[8,1024]{1,0:T(8,128)S(1)} collective-permute-done((f32[8,1024]{1,0:T(8,128)S(1)}, f32[8,1024]{1,0:T(8,128)S(1)}, u32[]{:S(2)}, u32[]{:S(2)}) %collective-permute-start) | collective-permute-done | bytes 32800 | tf_op jit(solution)/shard_map/ppermute | solution.py:263
  50.6 7.5 %shard_map.105 = bf16[32,80,128]{2,1,0:T(8,128)(2,1)} custom-call(s32[1024]{0:T(1024)S(1)} %bitcast.11, s32[1]{0:T(128)} %bitcast.1.half_s, s32[1,1024]{1,0:T(1,128)S(1)} %copy-done.2, bf16[32,104,128]{2,1,0:T(8,128)(2,1)S(1)} %all-to-all-done.data, f32[8,1024]{1,0:T(8,128)S(1)} %shard_map.104.own, f32[8,1024]{1,0:T(8,128)S(1)} %collective-permute-done.other), custom_call_target="tpu_custom_call" | custom-call | flops 1342177280 | bytes 1048576 | tf_op jit(solution)/shard_map/pallas_call | solution.py:264
  58.0 4.7 %all-to-all-start.1 = ((bf16[32,80,128]{2,1,0:T(8,128)(2,1)}), bf16[32,80,128]{2,1,0:T(8,128)(2,1)S(1)}, u32[]{:S(2)}, u32[]{:S(2)}) async-start(bf16[32,80,128]{2,1,0:T(8,128)(2,1)} %shard_map.105), calls=%async_computation.1 | async-start | bytes 1310720 | tf_op jit(solution)/shard_map/all_to_all | solution.py:279
  62.8 0.0 copy-done.3
  62.8 0.8 fusion.2
  63.6 17.4 %all-to-all-done.1.folded = bf16[32,80,128]{2,1,0:T(8,128)(2,1)S(1)} async-done(((bf16[32,80,128]{2,1,0:T(8,128)(2,1)}), bf16[32,80,128]{2,1,0:T(8,128)(2,1)S(1)}, u32[]{:S(2)}, u32[]{:S(2)}) %all-to-all-start.1) | async-done | bytes 655392 | tf_op jit(solution)/shard_map/all_to_all | solution.py:279
  81.1 0.0 copy-start
  81.1 0.1 shard_map.106.dk.own_dk
  81.2 0.0 copy-start.1
  81.2 0.1 collective-permute-start.2
  81.3 0.6 collective-permute-start.1
  81.9 1.1 collective-permute-done.1.other_t
  83.0 0.0 collective-permute-done.2.other_dk
  83.0 0.7 shard_map.108
  83.7 22.8 %all_to_all.20 = bf16[16,32,1024]{2,1,0:T(8,128)(2,1)S(1)} all-to-all(bf16[16,32,1024]{2,1,0:T(8,128)(2,1)S(1)} %shard_map.108), channel_id=1, replica_groups=mesh['y'=4,'z'=8,'x'=4,'core'=2] {'y','x'}, dimensions={0} | all-to-all | bytes 2097152 | tf_op jit(solution)/shard_map/all_to_all | solution.py:297
  106.5 0.0 copy-done
  106.5 0.0 copy-done.1
  106.5 0.2 convert_reduce_fusion
  106.7 0.7 reshape.13
  107.4 4.7 %all-to-all-start.3 = ((f32[8,4,1024]{2,1,0:T(4,128)}), f32[8,4,1024]{2,1,0:T(4,128)S(1)}, u32[]{:S(2)}, u32[]{:S(2)}) async-start(f32[8,4,1024]{2,1,0:T(4,128)} %reshape.13), calls=%async_computation.3 | async-start | bytes 262144 | tf_op jit(solution)/shard_map/all_to_all | solution.py:299
  112.1 6.0 %shard_map.107 = (bf16[128,1024]{1,0:T(8,128)(2,1)}, bf16[32,1024]{1,0:T(8,128)(2,1)}) custom-call(bf16[128,1024]{1,0:T(8,128)(2,1)} %copy-done.1, bf16[32,80,128]{2,1,0:T(8,128)(2,1)} %copy-done, bf16[1024,1024]{1,0:T(8,128)(2,1)} %w_query.3, bf16[1024,1024]{1,0:T(8,128)(2,1)} %w_key.3, bf16[1024,1024]{1,0:T(8,128)(2,1)} %w_value.3), custom_call_target="tpu_custom_call" | custom-call | flops 603979776 | bytes 8388608 | tf_op jit(solution)/shard_map/pallas_call | solution.py:303
  118.1 3.1 %all-to-all-done.3 = f32[8,4,1024]{2,1,0:T(4,128)S(1)} async-done(((f32[8,4,1024]{2,1,0:T(4,128)}), f32[8,4,1024]{2,1,0:T(4,128)S(1)}, u32[]{:S(2)}, u32[]{:S(2)}) %all-to-all-start.3) | async-done | bytes 131104 | tf_op jit(solution)/shard_map/all_to_all | solution.py:299
  121.2 0.6 reduce_sum.19
  (2 shorter events, 0.0 us)
Async XLA Ops:
  0.6 41.7 %copy-start.2 = (s32[1,1024]{1,0:T(1,128)S(1)}, s32[1,1024]{1,0:T(1,128)}, u32[]{:S(2)}) copy-start(s32[1,1024]{1,0:T(1,128)} %vis.3) | copy-start | bytes 12292
  6.1 36.3 %all-to-all-start = ((bf16[32,104,128]{2,1,0:T(8,128)(2,1)}), bf16[32,104,128]{2,1,0:T(8,128)(2,1)S(1)}, u32[]{:S(2)}, u32[]{:S(2)}) async-start(bf16[32,104,128]{2,1,0:T(8,128)(2,1)} %shard_map.103), calls=%async_computation | async-start | bytes 1703936 | tf_op jit(solution)/shard_map/all_to_all | solution.py:252
  46.6 16.2 %copy-start.3 = (bf16[1,128,1024]{2,1,0:T(8,128)(2,1)S(1)}, bf16[1,128,1024]{2,1,0:T(8,128)(2,1)}, u32[]{:S(2)}) copy-start(bf16[1,128,1024]{2,1,0:T(8,128)(2,1)} %param.8) | copy-start | bytes 786436
  46.6 4.0 %collective-permute-start = (f32[8,1024]{1,0:T(8,128)S(1)}, f32[8,1024]{1,0:T(8,128)S(1)}, u32[]{:S(2)}, u32[]{:S(2)}) collective-permute-start(f32[8,1024]{1,0:T(8,128)S(1)} %shard_map.104.own), channel_id=1, source_target_pairs={{0,8},{8,0},{16,24},{24,16},{32,40},{40,32},{48,56},{56,48},{1,9},... | collective-permute-start | bytes 98312 | tf_op jit(solution)/shard_map/ppermute | solution.py:263
  58.0 23.0 %all-to-all-start.1 = ((bf16[32,80,128]{2,1,0:T(8,128)(2,1)}), bf16[32,80,128]{2,1,0:T(8,128)(2,1)S(1)}, u32[]{:S(2)}, u32[]{:S(2)}) async-start(bf16[32,80,128]{2,1,0:T(8,128)(2,1)} %shard_map.105), calls=%async_computation.1 | async-start | bytes 1310720 | tf_op jit(solution)/shard_map/all_to_all | solution.py:279
  81.1 25.4 %copy-start = (bf16[32,80,128]{2,1,0:T(8,128)(2,1)}, bf16[32,80,128]{2,1,0:T(8,128)(2,1)S(1)}, u32[]{:S(2)}) copy-start(bf16[32,80,128]{2,1,0:T(8,128)(2,1)S(1)} %all-to-all-done.1.folded) | copy-start | bytes 1966084
  81.2 25.3 %copy-start.1 = (bf16[128,1024]{1,0:T(8,128)(2,1)}, bf16[128,1024]{1,0:T(8,128)(2,1)S(1)}, u32[]{:S(2)}) copy-start(bf16[128,1024]{1,0:T(8,128)(2,1)S(1)} %shard_map.106.dk.own_dk) | copy-start | bytes 786436
  81.2 1.8 %collective-permute-start.2 = (bf16[128,1024]{1,0:T(8,128)(2,1)S(1)}, bf16[128,1024]{1,0:T(8,128)(2,1)S(1)}, u32[]{:S(2)}, u32[]{:S(2)}) collective-permute-start(bf16[128,1024]{1,0:T(8,128)(2,1)S(1)} %shard_map.106.dk.own_dk), channel_id=1, source_target_pairs={{0,1},{1,0},{2,3},{3,2},{4,5},{5,4},{6,7},{7,6},{8,9},{9,8},{10,11... | collective-permute-start | bytes 786440 | tf_op jit(solution)/shard_map/ppermute | solution.py:288
  81.3 1.7 %collective-permute-start.1 = (bf16[512,128]{1,0:T(8,128)(2,1)S(1)}, bf16[512,128]{1,0:T(8,128)(2,1)S(1)}, u32[]{:S(2)}, u32[]{:S(2)}) collective-permute-start(bf16[512,128]{1,0:T(8,128)(2,1)S(1)} %get-tuple-element.7), channel_id=1, source_target_pairs={{0,1},{1,0},{2,3},{3,2},{4,5},{5,4},{6,7},{7,6},{8,9},{9,8},{10,11... | collective-permute-start | bytes 393224 | tf_op jit(solution)/shard_map/ppermute | solution.py:240
  107.4 13.8 %all-to-all-start.3 = ((f32[8,4,1024]{2,1,0:T(4,128)}), f32[8,4,1024]{2,1,0:T(4,128)S(1)}, u32[]{:S(2)}, u32[]{:S(2)}) async-start(f32[8,4,1024]{2,1,0:T(4,128)} %reshape.13), calls=%async_computation.3 | async-start | bytes 262144 | tf_op jit(solution)/shard_map/all_to_all | solution.py:299

commit v3 on v2

v3 whole, which is shorter than its diff:
```python
import functools
import math

import jax
import jax.numpy as jnp
from jax import lax
from jax.experimental import pallas as pl
from jax.experimental.pallas import tpu as pltpu
from jax.sharding import Mesh, PartitionSpec as P

BF = jnp.bfloat16
F32 = jnp.float32
DH = 64
NEG = -1e30
FLOOR = -1e29
SCALE = 1.0 / math.sqrt(DH)
C = SCALE * math.log2(math.e)
NT_DIMS = (((1,), (1,)), ((), ()))
LAT_TILE = 512
SRC_CHUNK = 16


def dot(a, b):
    return jnp.dot(a, b, preferred_element_type=F32)


def dot_nt(a, b):
    return lax.dot_general(a, b, NT_DIMS, preferred_element_type=F32)


def swap(x):
    return jnp.concatenate([x[..., 64:], x[..., :64]], axis=-1)


def fold(x, rows):
    return jnp.concatenate([x[:rows], x[rows:]], axis=1)


def pre_kernel(prefix, latents, grad, saved, w_query, w_key, w_value, out):
    keys = dot(prefix[...], w_key[...]).astype(BF)
    values = dot(prefix[...], w_value[...]).astype(BF)
    queries = dot(latents[...], w_query[...]).astype(BF)
    g = grad[...]
    product = g.astype(F32) * saved[...].astype(F32)
    product = jnp.concatenate([product, jnp.zeros((96, product.shape[1]), F32)], axis=0).T
    row = lax.broadcasted_iota(jnp.int32, (8, 128), 0)
    for head in range(8):
        cols = slice(head * DH, (head + 1) * DH)
        delta = jnp.sum(product[cols], axis=0, keepdims=True)
        high = delta.astype(BF).astype(F32)
        mid = (delta - high).astype(BF).astype(F32)
        low = delta - high - mid
        parts = jnp.where(row == 0, high, jnp.where(row == 1, mid, jnp.where(row == 2, low, 0.0)))
        q_fold = fold(queries[:, cols], 16)
        g_fold = fold(g[:, cols], 16)
        for half in range(2):
            toks = slice(half * 64, (half + 1) * 64)
            dest = 2 * head + half
            out[dest, 0:32, :] = fold(keys[toks, cols], 32)
            out[dest, 32:64, :] = fold(values[toks, cols], 32)
            out[dest, 64:80, :] = q_fold
            out[dest, 80:96, :] = g_fold
            out[dest, 96:104, :] = parts.astype(BF)


def unfold(folded, low_ref, high_ref):
    lane = lax.broadcasted_iota(jnp.int32, folded.shape, 2)
    other = swap(folded)
    zero = jnp.zeros_like(folded)
    left = lane < 64
    low = jnp.concatenate([jnp.where(left, folded, zero), jnp.where(left, other, zero)], axis=1)
    high = jnp.concatenate([jnp.where(left, zero, other), jnp.where(left, zero, folded)], axis=1)
    low_ref[...] = low.reshape(low_ref.shape)
    high_ref[...] = high.reshape(high_ref.shape)


SPAN = SRC_CHUNK * 128
ROWS = SRC_CHUNK * 32
CHUNKS = 32 // SRC_CHUNK


def hide(scores, bound):
    parts = scores.reshape(SRC_CHUNK, 32, LAT_TILE)
    row = lax.broadcasted_iota(jnp.int32, (1, 32, LAT_TILE), 1)
    first = lax.broadcasted_iota(jnp.int32, (SRC_CHUNK, 1, LAT_TILE), 0) * 128
    return jnp.where(row < bound[None] - first, parts, NEG).reshape(ROWS, LAT_TILE)


def all_chunks(step, carry):
    for chunk in range(CHUNKS):
        carry = step(chunk, carry)
    return carry


def stats_kernel(half_s, vis, data, out, q_low, q_high):
    half = half_s[0]
    unfold(data[:, 64:80, :], q_low, q_high)
    for tile in range(1024 // LAT_TILE):
        lanes = slice(tile * LAT_TILE, (tile + 1) * LAT_TILE)
        seen = vis[:, lanes] - half * 64
        ql = q_low[lanes, :]
        qh = q_high[lanes, :]

        def step(chunk, carry):
            top, total = carry
            k = data[slice(chunk * SRC_CHUNK, (chunk + 1) * SRC_CHUNK), 0:32, :].reshape(ROWS, 128)
            s_low = hide(dot_nt(k, ql), seen - chunk * SPAN)
            s_high = hide(dot_nt(k, qh), seen - 32 - chunk * SPAN)
            new = jnp.max(jnp.maximum(s_low, s_high), axis=0, keepdims=True)
            new = jnp.maximum(new, top)
            part = jnp.sum(jnp.exp2((s_low - new) * C) + jnp.exp2((s_high - new) * C), axis=0, keepdims=True)
            return new, total * jnp.exp2((top - new) * C) + part

        start = (jnp.full((1, LAT_TILE), FLOOR, F32), jnp.zeros((1, LAT_TILE), F32))
        top, total = all_chunks(step, start)
        out[0:1, lanes] = top
        out[1:2, lanes] = total
    out[2:8, :] = jnp.zeros((6, 1024), F32)


def grad_kernel(half_s, vis, data, own, other, out,
                q_low, q_high, g_low, g_high, k_t, dk_acc, dv_acc, delta_ref):
    half = half_s[0]
    unfold(data[:, 64:80, :], q_low, q_high)
    unfold(data[:, 80:96, :], g_low, g_high)
    for chunk in range(CHUNKS):
        k = data[chunk * SRC_CHUNK : (chunk + 1) * SRC_CHUNK, 0:32, :].reshape(ROWS, 128)
        turned = k.T
        k_t[chunk] = jnp.concatenate([turned[0:64], turned[64:128]], axis=1)
    dk_acc[...] = jnp.zeros_like(dk_acc)
    dv_acc[...] = jnp.zeros_like(dv_acc)
    lane = lax.broadcasted_iota(jnp.int32, (1, 128), 1)
    for block in range(8):
        joined = jnp.zeros((1, 128), F32)
        for place in range(4):
            parts = data[4 * block + place, 96:104, :].astype(F32)
            parts = jnp.sum(parts, axis=0, keepdims=True)
            if place:
                parts = pltpu.roll(parts, 32 * place, 1)
            joined = jnp.where((lane >> 5) == place, parts, joined)
        delta_ref[:, block * 128 : (block + 1) * 128] = joined
    top = jnp.maximum(own[0:1, :], other[0:1, :])
    total = own[1:2, :] * jnp.exp2((own[0:1, :] - top) * C) + other[1:2, :] * jnp.exp2((other[0:1, :] - top) * C)
    lse = top + jnp.log2(total) * (1.0 / C)
    for tile in range(1024 // LAT_TILE):
        lanes = slice(tile * LAT_TILE, (tile + 1) * LAT_TILE)
        seen = vis[:, lanes] - half * 64
        lse_t = lse[:, lanes]
        delta = delta_ref[:, lanes]
        ql, qh, gl, gh = q_low[lanes, :], q_high[lanes, :], g_low[lanes, :], g_high[lanes, :]

        def step(chunk, dq):
            srcs = slice(chunk * SRC_CHUNK, (chunk + 1) * SRC_CHUNK)
            k = data[srcs, 0:32, :].reshape(ROWS, 128)
            v = data[srcs, 32:64, :].reshape(ROWS, 128)
            s_low = hide(dot_nt(k, ql), seen - chunk * SPAN)
            s_high = hide(dot_nt(k, qh), seen - 32 - chunk * SPAN)
            p_low = jnp.exp2((s_low - lse_t) * C)
            p_high = jnp.exp2((s_high - lse_t) * C)
            ds_low = (p_low * (dot_nt(v, gl) - delta)).astype(BF)
            ds_high = (p_high * (dot_nt(v, gh) - delta)).astype(BF)
            place = slice(chunk * ROWS, (chunk + 1) * ROWS)
            dv_acc[place, :] += dot(p_low.astype(BF), gl) + dot(p_high.astype(BF), gh)
            dk_acc[place, :] += dot(ds_low, ql) + dot(ds_high, qh)
            return dq + dot(k_t[chunk], jnp.concatenate([ds_low, ds_high], axis=0))

        dq = all_chunks(step, jnp.zeros((DH, LAT_TILE), F32))
        dq = (dq * SCALE).T
        for block in range(LAT_TILE // 32):
            part = dq[block * 32 : (block + 1) * 32]
            out[tile * (LAT_TILE // 32) + block, 64:80, :] = fold(part, 16).astype(BF)
    out[:, 0:32, :] = (dk_acc[...] * SCALE).astype(BF).reshape(32, 32, 128)
    out[:, 32:64, :] = dv_acc[...].astype(BF).reshape(32, 32, 128)


def tokens_of(ref, half, side, start):
    pieces = []
    for head in range(16):
        pieces.append(ref[2 * head + half, start : start + 32, side * 64 : (side + 1) * 64])
    return jnp.concatenate(pieces, axis=1)


def join_kernel(folded, out):
    for half in range(2):
        for side in range(2):
            at = half * 64 + side * 32
            out[at : at + 32, :] = tokens_of(folded, half, side, 0)


def key_kernel(own_t, far_t, dk_0, dk_1, dk_2, dk_3, out):
    total = dot(own_t[0], dk_0[...]) + dot(own_t[1], dk_1[...])
    total += dot(far_t[0], dk_2[...]) + dot(far_t[1], dk_3[...])
    for block in range(64):
        out[block] = total[4 * block : 4 * block + 4].astype(BF)


def post_kernel(dk, folded, w_query, w_key, w_value, prefix_grad, latent_grad, dv, dq):
    @pl.when(pl.program_id(0) == 0)
    def _():
        for half in range(2):
            for side in range(2):
                at = half * 64 + side * 32
                dv[at : at + 32, :] = tokens_of(folded, half, side, 32)
        for side in range(2):
            pieces = []
            for head in range(16):
                part = [folded[2 * head + half, 64:80, side * 64 : (side + 1) * 64].astype(F32) for half in range(2)]
                pieces.append(part[0] + part[1])
            dq[side * 16 : (side + 1) * 16, :] = jnp.concatenate(pieces, axis=1).astype(BF)

    prefix_grad[...] = (dot_nt(dk[...], w_key[...]) + dot_nt(dv[...], w_value[...])).astype(BF)
    latent_grad[...] = dot_nt(dq[...], w_query[...]).astype(BF)


def call(kernel, out_shape, flops=0, nbytes=0, limit=48, **kwargs):
    return pl.pallas_call(
        kernel,
        out_shape=out_shape,
        compiler_params=pltpu.CompilerParams(vmem_limit_bytes=limit << 20),
        cost_estimate=pl.CostEstimate(flops=flops, bytes_accessed=nbytes, transcendentals=0),
        **kwargs,
    )


VMEM = pl.BlockSpec(memory_space=pltpu.VMEM)
SMEM = pl.BlockSpec(memory_space=pltpu.SMEM)
shape = jax.ShapeDtypeStruct


def whole(rows):
    return pl.BlockSpec((rows, 1024), lambda i: (0, 0))


def cols(rows):
    return pl.BlockSpec((rows, 256), lambda i: (0, i))


def wide(rows):
    return pl.BlockSpec((rows, 512), lambda i: (0, i))


def run_pre(prefix, latents, grad, saved, w_query, w_key, w_value):
    return call(
        pre_kernel,
        shape((32, 104, 128), BF),
        limit=60,
        flops=2 * 288 * 1024 * 1024,
        nbytes=8 << 20,
        grid=(2,),
        in_specs=[whole(128), whole(32), wide(32), wide(32), wide(1024), wide(1024), wide(1024)],
        out_specs=pl.BlockSpec((16, 104, 128), lambda i: (i, 0, 0)),
    )(prefix, latents, grad, saved, w_query, w_key, w_value)


def run_stats(half, vis_row, data):
    return call(
        stats_kernel,
        shape((8, 1024), F32),
        flops=2 * 1024 * 2048 * 64,
        nbytes=1 << 19,
        in_specs=[SMEM, VMEM, VMEM],
        out_specs=VMEM,
        scratch_shapes=[pltpu.VMEM((1024, 128), BF)] * 2,
    )(half, vis_row, data)


def run_grad(half, vis_row, data, stats, other):
    return call(
        grad_kernel,
        shape((32, 80, 128), BF),
        flops=10 * 1024 * 2048 * 64,
        nbytes=1 << 20,
        in_specs=[SMEM] + [VMEM] * 4,
        out_specs=VMEM,
        scratch_shapes=[pltpu.VMEM((1024, 128), BF)] * 4
        + [
            pltpu.VMEM((32 // SRC_CHUNK, DH, SRC_CHUNK * 64), BF),
            pltpu.VMEM((1024, 128), F32),
            pltpu.VMEM((1024, 128), F32),
            pltpu.VMEM((1, 1024), F32),
        ],
    )(half, vis_row, data, stats, other)


def run_join(back):
    return call(join_kernel, shape((128, 1024), BF), nbytes=1 << 19, in_specs=[VMEM], out_specs=VMEM)(back)


def run_key(own_t, far_t, *dks):
    return call(
        key_kernel,
        shape((64, 4, 1024), BF),
        flops=2 * 256 * 512 * 1024,
        nbytes=2 << 20,
        in_specs=[VMEM] * 6,
        out_specs=VMEM,
    )(own_t, far_t, *dks)


def run_post(dk, back, w_query, w_key, w_value):
    rows = pl.BlockSpec((256, 1024), lambda i: (i, 0))
    return call(
        post_kernel,
        (shape((128, 1024), BF), shape((32, 1024), BF)),
        limit=60,
        flops=2 * 288 * 1024 * 1024,
        nbytes=8 << 20,
        grid=(4,),
        in_specs=[whole(128), pl.BlockSpec((32, 80, 128), lambda i: (0, 0, 0))] + [rows] * 3,
        out_specs=(cols(128), cols(32)),
        scratch_shapes=[pltpu.VMEM((128, 1024), BF), pltpu.VMEM((32, 1024), BF)],
    )(dk, back, w_query, w_key, w_value)


def pick_rows(x_low, core):
    at = lax.broadcasted_iota(jnp.int32, (1024, 1024), 0)
    x_to, core_to = x_low ^ (at >> 9), core ^ ((at >> 8) & 1)
    wanted = ((at >> 2) & 31) * 32 + ((at >> 7) & 1) * 16 + x_to * 8 + core_to * 4 + (at & 3)
    return (wanted == lax.broadcasted_iota(jnp.int32, (1024, 1024), 1)).astype(BF)


def on_device(prefix, latents, saved, grad, visible, w_query, w_key, w_value):
    prefix, latents, saved, grad = prefix[0], latents[0], saved[0], grad[0]
    half = jnp.reshape(lax.axis_index("z") % 2, (1,)).astype(jnp.int32)
    over_core = lambda v: lax.ppermute(v, "core", [(0, 1), (1, 0)])
    over_x = lambda v: lax.ppermute(v, "x_low", [(0, 1), (1, 0)])

    data = run_pre(prefix, latents, grad, saved, w_query, w_key, w_value)
    data = lax.all_to_all(data, ("y", "z"), 0, 0, tiled=True)
    picked = pick_rows(lax.axis_index("x_low"), lax.axis_index("core"))
    turned = dot_nt(picked, prefix).astype(BF).reshape(4, 256, 128)
    gained = over_core(jnp.stack([turned[1], turned[3]]))
    own_t = jnp.stack([turned[0], gained[0]])
    far_t = over_x(jnp.stack([turned[2], gained[1]]))

    stats = run_stats(half, visible, data)
    stats, own_t, far_t = lax.optimization_barrier((stats, own_t, far_t))
    other = lax.ppermute(stats, "z", [(i, i ^ 1) for i in range(8)])
    back = run_grad(half, visible, data, stats, other)
    back = lax.all_to_all(back, ("y", "z"), 0, 0, tiled=True)

    dk = run_join(back)
    far_dk = over_x(dk)
    part = run_key(own_t, far_t, dk, over_core(dk), far_dk, over_core(far_dk))
    part = lax.all_to_all(part, ("x_high", "y", "z"), 0, 0, tiled=True)
    key_wgrad = jnp.sum(part.astype(F32), axis=0)
    prefix_grad, latent_grad = run_post(dk, back, w_query, w_key, w_value)
    return prefix_grad[None], latent_grad[None], key_wgrad


def solution(mesh):
    grid = Mesh(mesh.devices.reshape(4, 8, 2, 2, 2), ("y", "z", "x_high", "x_low", "core"))
    seq, dp = ("y", "z"), ("x_high", "x_low", "core")
    return jax.shard_map(
        on_device,
        mesh=grid,
        in_specs=(
            P(dp, seq, None),
            P(dp, seq, None),
            P(dp, seq, None),
            P(dp, seq, None),
            P(dp, None),
            P(),
            P(),
            P(),
        ),
        out_specs=(P(dp, seq, None), P(dp, seq, None), P(seq + dp, None)),
        check_vma=False,
    )
```

time: 123 us -> 116 us (0.943)
  Pallas kernels: 23.9 us -> 21.2 us
  waiting for transfers between devices: 48.8 us -> 47.1 us
    ppermute x2 -> x5, waiting for transfers between devices: 1.11 us -> 8.66 us  [the longest x2 5.8 us: on_device(): over_x = lambda v: lax.ppermute(v, 'x_low', [(0, 1), (1, 0)])]
    all_to_all x2 -> x1, waiting for transfers between devices: 20.5 us -> 14.3 us  [on_device(): part = lax.all_to_all(part, ('x_high', 'y', 'z'), 0, 0, tiled=True)]
    all_to_all x1, waiting for transfers between devices: 24.8 us -> 21.7 us  [on_device(): data = lax.all_to_all(data, ('y', 'z'), 0, 0, tiled=True)]
    pallas_call x6, Pallas kernels: 23.9 us -> 21.2 us  [the longest x1 6.03 us: run_post(): call(post_kernel, (shape((128, 1024), BF), shape((32, 1024), BF)), limit=...]
    all_to_all x2 -> x1, starting transfers between devices: 9.43 us -> 7.57 us  [on_device(): part = lax.all_to_all(part, ('x_high', 'y', 'z'), 0, 0, tiled=True)]
  transfers between devices with their start and end apart: 6 -> 8, of which waited for: 5 -> 6; matrix products, arithmetic and copies ran while one was open for 1% -> 1% of each run, Pallas kernels for 5% -> 8%
where the time goes in v3:
time: 116 us
  waiting for transfers between devices  47.1 us (41%)
  blocking collectives  22.8 us (20%)
  starting transfers between devices  22.1 us (19%)
  Pallas kernels  21.2 us (18%)
    all_to_all x1, blocking collectives, on_device(): back = lax.all_to_all(back, ('y', 'z'), 0, 0, tiled=True)  22.8 us
    all_to_all x1, waiting for transfers between devices, on_device(): data = lax.all_to_all(data, ('y', 'z'), 0, 0, tiled=True)  21.7 us
    all_to_all x1, waiting for transfers between devices, on_device(): part = lax.all_to_all(part, ('x_high', 'y', 'z'), 0, 0, tiled=True)  14.3 us
    all_to_all x1, starting transfers between devices, on_device(): data = lax.all_to_all(data, ('y', 'z'), 0, 0, tiled=True)  11.5 us
    all_to_all x1, starting transfers between devices, on_device(): part = lax.all_to_all(part, ('x_high', 'y', 'z'), 0, 0, tiled=True)  7.57 us
    pallas_call x1, Pallas kernels, run_post(): call(post_kernel, (shape((128, 1024), BF), shape((32, 1024), BF)), limit=...  6.03 us
    pallas_call x1, Pallas kernels, run_grad(): call(grad_kernel, shape((32, 80, 128), BF), flops=10 * 1024 * 2048 * 64,...  5.99 us
    ppermute x2, waiting for transfers between devices, on_device(): over_x = lambda v: lax.ppermute(v, 'x_low', [(0, 1), (1, 0)])  5.8 us
  transfers between devices with their start and end apart: 8, of which 6 were waited for; matrix products, arithmetic and copies ran while one was open for 1% of the time, Pallas kernels for 8%

profile of v3, /device:TPU:2, one launch (start us, length us, event | category | flops | bytes accessed | tf_op | source)
XLA Modules:
  0.0 115.7 jit_solution(12657691610855996440)
XLA Ops:
  0.6 0.0 copy-start.3
  0.6 4.5 %shard_map.103 = bf16[32,104,128]{2,1,0:T(8,128)(2,1)} custom-call(bf16[128,1024]{1,0:T(8,128)(2,1)} %bitcast.17, bf16[32,1024]{1,0:T(8,128)(2,1)} %bitcast.18, bf16[32,1024]{1,0:T(8,128)(2,1)} %bitcast.19, bf16[32,1024]{1,0:T(8,128)(2,1)} %bitcast.20, bf16[1024,1024]{1,0:T(8,128)(2,1)} %w_query.3, bf16[1024,1024]{1,0:T(8,128)(2,1)} %w_key.3, ...), custom_call_target="tpu_custom_call" | custom-call | flops 603979776 | bytes 8388608 | tf_op jit(solution)/shard_map/pallas_call | solution.py:243
  5.1 11.5 %all-to-all-start = ((bf16[32,104,128]{2,1,0:T(8,128)(2,1)}), bf16[32,104,128]{2,1,0:T(8,128)(2,1)S(1)}, u32[]{:S(2)}, u32[]{:S(2)}) async-start(bf16[32,104,128]{2,1,0:T(8,128)(2,1)} %shard_map.103), calls=%async_computation | async-start | bytes 1703936 | tf_op jit(solution)/shard_map/all_to_all | solution.py:329
  16.6 0.0 copy-start.2
  16.6 0.0 copy-done.3
  16.6 0.8 fusion.2
  17.5 0.1 collective-permute-start
  17.6 1.3 %collective-permute-done = bf16[2,256,128]{2,1,0:T(8,128)(2,1)S(1)} collective-permute-done((bf16[2,256,128]{2,1,0:T(8,128)(2,1)S(1)}, bf16[2,256,128]{2,1,0:T(8,128)(2,1)S(1)}, u32[]{:S(2)}, u32[]{:S(2)}) %collective-permute-start) | collective-permute-done | bytes 131104 | tf_op jit(solution)/shard_map/ppermute | solution.py:325
  19.0 0.6 collective-permute-start.1
  19.7 21.7 %all-to-all-done.data = bf16[32,104,128]{2,1,0:T(8,128)(2,1)S(1)} async-done(((bf16[32,104,128]{2,1,0:T(8,128)(2,1)}), bf16[32,104,128]{2,1,0:T(8,128)(2,1)S(1)}, u32[]{:S(2)}, u32[]{:S(2)}) %all-to-all-start) | async-done | bytes 852000 | tf_op jit(solution)/shard_map/all_to_all | solution.py:329
  41.4 0.0 copy-done.2
  41.4 3.0 %shard_map.104.own = f32[8,1024]{1,0:T(8,128)S(1)} custom-call(s32[1]{0:T(128)} %bitcast.half_s, s32[1,1024]{1,0:T(1,128)S(1)} %copy-done.2, bf16[32,104,128]{2,1,0:T(8,128)(2,1)S(1)} %all-to-all-done.data), custom_call_target="tpu_custom_call" | custom-call | flops 268435456 | bytes 524288 | tf_op jit(solution)/shard_map/pallas_call | solution.py:256
  44.4 0.0 collective-permute-done.1.far_t
  44.4 1.6 %collective-permute-start.2 = (f32[8,1024]{1,0:T(8,128)S(1)}, f32[8,1024]{1,0:T(8,128)S(1)}, u32[]{:S(2)}, u32[]{:S(2)}) collective-permute-start(f32[8,1024]{1,0:T(8,128)S(1)} %shard_map.104.own), channel_id=1, source_target_pairs={{0,8},{8,0},{16,24},{24,16},{32,40},{40,32},{48,56},{56,48},{1,9},... | collective-permute-start | bytes 98312 | tf_op jit(solution)/shard_map/ppermute | solution.py:338
  46.1 2.4 %collective-permute-done.2.other = f32[8,1024]{1,0:T(8,128)S(1)} collective-permute-done((f32[8,1024]{1,0:T(8,128)S(1)}, f32[8,1024]{1,0:T(8,128)S(1)}, u32[]{:S(2)}, u32[]{:S(2)}) %collective-permute-start.2) | collective-permute-done | bytes 32800 | tf_op jit(solution)/shard_map/ppermute | solution.py:338
  48.5 6.0 %shard_map.105 = bf16[32,80,128]{2,1,0:T(8,128)(2,1)S(1)} custom-call(s32[1]{0:T(128)} %bitcast.half_s, s32[1,1024]{1,0:T(1,128)S(1)} %copy-done.2, bf16[32,104,128]{2,1,0:T(8,128)(2,1)S(1)} %all-to-all-done.data, f32[8,1024]{1,0:T(8,128)S(1)} %shard_map.104.own, f32[8,1024]{1,0:T(8,128)S(1)} %collective-permute-done.2.other), custom_call_target="tpu_custom_call" | custom-call | flops 1342177280 | bytes 1048576 | tf_op jit(solution)/shard_map/pallas_call | solution.py:268
  54.5 22.8 %all_to_all.15.folded = bf16[32,80,128]{2,1,0:T(8,128)(2,1)S(1)} all-to-all(bf16[32,80,128]{2,1,0:T(8,128)(2,1)S(1)} %shard_map.105), channel_id=1, replica_groups=mesh['y'=4,'z'=8,'x_high'=2,'x_low'=2,'core'=2] {'y','z'}, dimensions={0} | all-to-all | bytes 1310720 | tf_op jit(solution)/shard_map/all_to_all | solution.py:340
  77.2 0.0 copy-start
  77.2 0.1 shard_map.106.dk.dk_0
  77.4 0.0 copy-start.1
  77.4 0.7 collective-permute-start.4
  78.0 0.0 collective-permute-start.3
  78.0 5.8 %collective-permute-done.4.dk_2 = bf16[128,1024]{1,0:T(8,128)(2,1)S(1)} collective-permute-done((bf16[128,1024]{1,0:T(8,128)(2,1)S(1)}, bf16[128,1024]{1,0:T(8,128)(2,1)S(1)}, u32[]{:S(2)}, u32[]{:S(2)}) %collective-permute-start.4) | collective-permute-done | bytes 262176 | tf_op jit(solution)/shard_map/ppermute | solution.py:326
  83.8 0.0 collective-permute-start.5
  83.8 0.0 collective-permute-done.3.dk_1
  83.8 1.5 %collective-permute-done.5.dk_3 = bf16[128,1024]{1,0:T(8,128)(2,1)S(1)} collective-permute-done((bf16[128,1024]{1,0:T(8,128)(2,1)S(1)}, bf16[128,1024]{1,0:T(8,128)(2,1)S(1)}, u32[]{:S(2)}, u32[]{:S(2)}) %collective-permute-start.5) | collective-permute-done | bytes 262176 | tf_op jit(solution)/shard_map/ppermute | solution.py:325
  85.4 1.5 %shard_map.108 = bf16[64,4,1024]{2,1,0:T(4,128)(2,1)} custom-call(bf16[2,256,128]{2,1,0:T(8,128)(2,1)S(1)} %pad_maximum_fusion.1.own_t, bf16[2,256,128]{2,1,0:T(8,128)(2,1)S(1)} %collective-permute-done.1.far_t, bf16[128,1024]{1,0:T(8,128)(2,1)S(1)} %shard_map.106.dk.dk_0, bf16[128,1024]{1,0:T(8,128)(2,1)S(1)} %collective-permute-done.3.dk_1, ...), custom_call_target="tpu_custom_call" | custom-call | flops 268435456 | bytes 2097152 | tf_op jit(solution)/shard_map/pallas_call | solution.py:290
  86.9 7.6 %all-to-all-start.2 = ((bf16[64,4,1024]{2,1,0:T(4,128)(2,1)}), bf16[64,4,1024]{2,1,0:T(4,128)(2,1)S(1)}, u32[]{:S(2)}, u32[]{:S(2)}) async-start(bf16[64,4,1024]{2,1,0:T(4,128)(2,1)} %shard_map.108), calls=%async_computation.2 | async-start | bytes 1048576 | tf_op jit(solution)/shard_map/all_to_all | solution.py:345
  94.4 0.0 copy-done
  94.4 0.0 copy-done.1
  94.5 6.0 %shard_map.107 = (bf16[128,1024]{1,0:T(8,128)(2,1)}, bf16[32,1024]{1,0:T(8,128)(2,1)}) custom-call(bf16[128,1024]{1,0:T(8,128)(2,1)} %copy-done.1, bf16[32,80,128]{2,1,0:T(8,128)(2,1)} %copy-done, bf16[1024,1024]{1,0:T(8,128)(2,1)} %w_query.3, bf16[1024,1024]{1,0:T(8,128)(2,1)} %w_key.3, bf16[1024,1024]{1,0:T(8,128)(2,1)} %w_value.3), custom_call_target="tpu_custom_call" | custom-call | flops 603979776 | bytes 8388608 | tf_op jit(solution)/shard_map/pallas_call | solution.py:302
  100.5 14.3 %all-to-all-done.2 = bf16[64,4,1024]{2,1,0:T(4,128)(2,1)S(1)} async-done(((bf16[64,4,1024]{2,1,0:T(4,128)(2,1)}), bf16[64,4,1024]{2,1,0:T(4,128)(2,1)S(1)}, u32[]{:S(2)}, u32[]{:S(2)}) %all-to-all-start.2) | async-done | bytes 524320 | tf_op jit(solution)/shard_map/all_to_all | solution.py:345
  114.8 0.8 convert_reduce_fusion
  (6 shorter events, 0.1 us)
Async XLA Ops:
  0.6 16.0 %copy-start.3 = (bf16[1,128,1024]{2,1,0:T(8,128)(2,1)S(1)}, bf16[1,128,1024]{2,1,0:T(8,128)(2,1)}, u32[]{:S(2)}) copy-start(bf16[1,128,1024]{2,1,0:T(8,128)(2,1)} %param.8) | copy-start | bytes 786436
  5.1 36.3 %all-to-all-start = ((bf16[32,104,128]{2,1,0:T(8,128)(2,1)}), bf16[32,104,128]{2,1,0:T(8,128)(2,1)S(1)}, u32[]{:S(2)}, u32[]{:S(2)}) async-start(bf16[32,104,128]{2,1,0:T(8,128)(2,1)} %shard_map.103), calls=%async_computation | async-start | bytes 1703936 | tf_op jit(solution)/shard_map/all_to_all | solution.py:329
  16.6 24.8 %copy-start.2 = (s32[1,1024]{1,0:T(1,128)S(1)}, s32[1,1024]{1,0:T(1,128)}, u32[]{:S(2)}) copy-start(s32[1,1024]{1,0:T(1,128)} %vis.3) | copy-start | bytes 12292
  17.5 1.4 %collective-permute-start = (bf16[2,256,128]{2,1,0:T(8,128)(2,1)S(1)}, bf16[2,256,128]{2,1,0:T(8,128)(2,1)S(1)}, u32[]{:S(2)}, u32[]{:S(2)}) collective-permute-start(bf16[2,256,128]{2,1,0:T(8,128)(2,1)S(1)} %pad_maximum_fusion), channel_id=1, source_target_pairs={{0,1},{1,0},{2,3},{3,2},{4,5},{5,4},{6,7},{7,6},{8,9},{9,8},{10,11... | collective-permute-start | bytes 393224 | tf_op jit(solution)/shard_map/ppermute | solution.py:325
  19.0 25.4 %collective-permute-start.1 = (bf16[2,256,128]{2,1,0:T(8,128)(2,1)S(1)}, bf16[2,256,128]{2,1,0:T(8,128)(2,1)S(1)}, u32[]{:S(2)}, u32[]{:S(2)}) collective-permute-start(bf16[2,256,128]{2,1,0:T(8,128)(2,1)S(1)} %pad_maximum_fusion.2), channel_id=1, source_target_pairs={{0,2},{2,0},{1,3},{3,1},{4,6},{6,4},{5,7},{7,5},{8,10},{10,8},{9,1... | collective-permute-start | bytes 393224 | tf_op jit(solution)/shard_map/ppermute | solution.py:326
  44.4 4.0 %collective-permute-start.2 = (f32[8,1024]{1,0:T(8,128)S(1)}, f32[8,1024]{1,0:T(8,128)S(1)}, u32[]{:S(2)}, u32[]{:S(2)}) collective-permute-start(f32[8,1024]{1,0:T(8,128)S(1)} %shard_map.104.own), channel_id=1, source_target_pairs={{0,8},{8,0},{16,24},{24,16},{32,40},{40,32},{48,56},{56,48},{1,9},... | collective-permute-start | bytes 98312 | tf_op jit(solution)/shard_map/ppermute | solution.py:338
  77.2 17.2 %copy-start = (bf16[32,80,128]{2,1,0:T(8,128)(2,1)}, bf16[32,80,128]{2,1,0:T(8,128)(2,1)S(1)}, u32[]{:S(2)}) copy-start(bf16[32,80,128]{2,1,0:T(8,128)(2,1)S(1)} %all_to_all.15.folded) | copy-start | bytes 1966084
  77.4 17.1 %copy-start.1 = (bf16[128,1024]{1,0:T(8,128)(2,1)}, bf16[128,1024]{1,0:T(8,128)(2,1)S(1)}, u32[]{:S(2)}) copy-start(bf16[128,1024]{1,0:T(8,128)(2,1)S(1)} %shard_map.106.dk.dk_0) | copy-start | bytes 786436
  77.4 6.5 %collective-permute-start.4 = (bf16[128,1024]{1,0:T(8,128)(2,1)S(1)}, bf16[128,1024]{1,0:T(8,128)(2,1)S(1)}, u32[]{:S(2)}, u32[]{:S(2)}) collective-permute-start(bf16[128,1024]{1,0:T(8,128)(2,1)S(1)} %shard_map.106.dk.dk_0), channel_id=1, source_target_pairs={{0,2},{2,0},{1,3},{3,1},{4,6},{6,4},{5,7},{7,5},{8,10},{10,8},{9,1... | collective-permute-start | bytes 786440 | tf_op jit(solution)/shard_map/ppermute | solution.py:326
  78.0 5.8 %collective-permute-start.3 = (bf16[128,1024]{1,0:T(8,128)(2,1)S(1)}, bf16[128,1024]{1,0:T(8,128)(2,1)S(1)}, u32[]{:S(2)}, u32[]{:S(2)}) collective-permute-start(bf16[128,1024]{1,0:T(8,128)(2,1)S(1)} %shard_map.106.dk.dk_0), channel_id=1, source_target_pairs={{0,1},{1,0},{2,3},{3,2},{4,5},{5,4},{6,7},{7,6},{8,9},{9,8},{10,11... | collective-permute-start | bytes 786440 | tf_op jit(solution)/shard_map/ppermute | solution.py:325
  83.8 1.5 %collective-permute-start.5 = (bf16[128,1024]{1,0:T(8,128)(2,1)S(1)}, bf16[128,1024]{1,0:T(8,128)(2,1)S(1)}, u32[]{:S(2)}, u32[]{:S(2)}) collective-permute-start(bf16[128,1024]{1,0:T(8,128)(2,1)S(1)} %collective-permute-done.4.dk_2), channel_id=1, source_target_pairs={{0,1},{1,0},{2,3},{3,2},{4,5},{5,4},{6,7},{7,6},{8,9},{9,8},{10,11... | collective-permute-start | bytes 786440 | tf_op jit(solution)/shard_map/ppermute | solution.py:325
  86.9 28.0 %all-to-all-start.2 = ((bf16[64,4,1024]{2,1,0:T(4,128)(2,1)}), bf16[64,4,1024]{2,1,0:T(4,128)(2,1)S(1)}, u32[]{:S(2)}, u32[]{:S(2)}) async-start(bf16[64,4,1024]{2,1,0:T(4,128)(2,1)} %shard_map.108), calls=%async_computation.2 | async-start | bytes 1048576 | tf_op jit(solution)/shard_map/all_to_all | solution.py:345

commit v4 on v3

--- a/solution.py
+++ b/solution.py
@@ -92,7 +92,7 @@
     return carry
 
 
-def stats_kernel(half_s, vis, data, out, q_low, q_high):
+def stats_kernel(half_s, vis, data, out, scores, q_low, q_high):
     half = half_s[0]
     unfold(data[:, 64:80, :], q_low, q_high)
     for tile in range(1024 // LAT_TILE):
@@ -106,6 +106,9 @@
             k = data[slice(chunk * SRC_CHUNK, (chunk + 1) * SRC_CHUNK), 0:32, :].reshape(ROWS, 128)
             s_low = hide(dot_nt(k, ql), seen - chunk * SPAN)
             s_high = hide(dot_nt(k, qh), seen - 32 - chunk * SPAN)
+            place = slice(chunk * ROWS, (chunk + 1) * ROWS)
+            scores[0, place, lanes] = s_low
+            scores[1, place, lanes] = s_high
             new = jnp.max(jnp.maximum(s_low, s_high), axis=0, keepdims=True)
             new = jnp.maximum(new, top)
             part = jnp.sum(jnp.exp2((s_low - new) * C) + jnp.exp2((s_high - new) * C), axis=0, keepdims=True)
@@ -118,17 +121,8 @@
     out[2:8, :] = jnp.zeros((6, 1024), F32)
 
 
-def grad_kernel(half_s, vis, data, own, other, out,
-                q_low, q_high, g_low, g_high, k_t, dk_acc, dv_acc, delta_ref):
-    half = half_s[0]
-    unfold(data[:, 64:80, :], q_low, q_high)
+def dprobs_kernel(data, out, g_low, g_high, delta_ref):
     unfold(data[:, 80:96, :], g_low, g_high)
-    for chunk in range(CHUNKS):
-        k = data[chunk * SRC_CHUNK : (chunk + 1) * SRC_CHUNK, 0:32, :].reshape(ROWS, 128)
-        turned = k.T
-        k_t[chunk] = jnp.concatenate([turned[0:64], turned[64:128]], axis=1)
-    dk_acc[...] = jnp.zeros_like(dk_acc)
-    dv_acc[...] = jnp.zeros_like(dv_acc)
     lane = lax.broadcasted_iota(jnp.int32, (1, 128), 1)
     for block in range(8):
         joined = jnp.zeros((1, 128), F32)
@@ -139,27 +133,38 @@
                 parts = pltpu.roll(parts, 32 * place, 1)
             joined = jnp.where((lane >> 5) == place, parts, joined)
         delta_ref[:, block * 128 : (block + 1) * 128] = joined
+    for chunk in range(CHUNKS):
+        place = slice(chunk * ROWS, (chunk + 1) * ROWS)
+        v = data[chunk * SRC_CHUNK : (chunk + 1) * SRC_CHUNK, 32:64, :].reshape(ROWS, 128)
+        for tile in range(1024 // LAT_TILE):
+            lanes = slice(tile * LAT_TILE, (tile + 1) * LAT_TILE)
+            out[0, place, lanes] = dot_nt(v, g_low[lanes, :]) - delta_ref[:, lanes]
+            out[1, place, lanes] = dot_nt(v, g_high[lanes, :]) - delta_ref[:, lanes]
+
+
+def grad_kernel(data, scores, dprobs, own, other, out, q_low, q_high, g_low, g_high, k_t, dk_acc, dv_acc):
+    unfold(data[:, 64:80, :], q_low, q_high)
+    unfold(data[:, 80:96, :], g_low, g_high)
+    for chunk in range(CHUNKS):
+        k = data[chunk * SRC_CHUNK : (chunk + 1) * SRC_CHUNK, 0:32, :].reshape(ROWS, 128)
+        turned = k.T
+        k_t[chunk] = jnp.concatenate([turned[0:64], turned[64:128]], axis=1)
+    dk_acc[...] = jnp.zeros_like(dk_acc)
+    dv_acc[...] = jnp.zeros_like(dv_acc)
     top = jnp.maximum(own[0:1, :], other[0:1, :])
     total = own[1:2, :] * jnp.exp2((own[0:1, :] - top) * C) + other[1:2, :] * jnp.exp2((other[0:1, :] - top) * C)
     lse = top + jnp.log2(total) * (1.0 / C)
     for tile in range(1024 // LAT_TILE):
         lanes = slice(tile * LAT_TILE, (tile + 1) * LAT_TILE)
-        seen = vis[:, lanes] - half * 64
         lse_t = lse[:, lanes]
-        delta = delta_ref[:, lanes]
         ql, qh, gl, gh = q_low[lanes, :], q_high[lanes, :], g_low[lanes, :], g_high[lanes, :]
 
         def step(chunk, dq):
-            srcs = slice(chunk * SRC_CHUNK, (chunk + 1) * SRC_CHUNK)
-            k = data[srcs, 0:32, :].reshape(ROWS, 128)
-            v = data[srcs, 32:64, :].reshape(ROWS, 128)
-            s_low = hide(dot_nt(k, ql), seen - chunk * SPAN)
-            s_high = hide(dot_nt(k, qh), seen - 32 - chunk * SPAN)
-            p_low = jnp.exp2((s_low - lse_t) * C)
-            p_high = jnp.exp2((s_high - lse_t) * C)
-            ds_low = (p_low * (dot_nt(v, gl) - delta)).astype(BF)
-            ds_high = (p_high * (dot_nt(v, gh) - delta)).astype(BF)
             place = slice(chunk * ROWS, (chunk + 1) * ROWS)
+            p_low = jnp.exp2((scores[0, place, lanes] - lse_t) * C)
+            p_high = jnp.exp2((scores[1, place, lanes] - lse_t) * C)
+            ds_low = (p_low * dprobs[0, place, lanes]).astype(BF)
+            ds_high = (p_high * dprobs[1, place, lanes]).astype(BF)
             dv_acc[place, :] += dot(p_low.astype(BF), gl) + dot(p_high.astype(BF), gh)
             dk_acc[place, :] += dot(ds_low, ql) + dot(ds_high, qh)
             return dq + dot(k_t[chunk], jnp.concatenate([ds_low, ds_high], axis=0))
@@ -187,9 +192,9 @@
             out[at : at + 32, :] = tokens_of(folded, half, side, 0)
 
 
-def key_kernel(own_t, far_t, dk_0, dk_1, dk_2, dk_3, out):
-    total = dot(own_t[0], dk_0[...]) + dot(own_t[1], dk_1[...])
-    total += dot(far_t[0], dk_2[...]) + dot(far_t[1], dk_3[...])
+def key_kernel(turned, dk_0, dk_1, dk_2, dk_3, out):
+    dks = jnp.concatenate([dk_0[...], dk_1[...], dk_2[...], dk_3[...]], axis=0)
+    total = dot(turned[...], dks)
     for block in range(64):
         out[block] = total[4 * block : 4 * block + 4].astype(BF)
 
@@ -212,7 +217,7 @@
     latent_grad[...] = dot_nt(dq[...], w_query[...]).astype(BF)
 
 
-def call(kernel, out_shape, flops=0, nbytes=0, limit=48, **kwargs):
+def call(kernel, out_shape, flops=0, nbytes=0, limit=24, **kwargs):
     return pl.pallas_call(
         kernel,
         out_shape=out_shape,
@@ -255,46 +260,57 @@
 def run_stats(half, vis_row, data):
     return call(
         stats_kernel,
-        shape((8, 1024), F32),
+        (shape((8, 1024), F32), shape((2, 1024, 1024), F32)),
         flops=2 * 1024 * 2048 * 64,
         nbytes=1 << 19,
         in_specs=[SMEM, VMEM, VMEM],
-        out_specs=VMEM,
+        out_specs=(VMEM, VMEM),
         scratch_shapes=[pltpu.VMEM((1024, 128), BF)] * 2,
     )(half, vis_row, data)
 
 
-def run_grad(half, vis_row, data, stats, other):
+def run_dprobs(data):
+    return call(
+        dprobs_kernel,
+        shape((2, 1024, 1024), F32),
+        flops=2 * 1024 * 2048 * 64,
+        nbytes=1 << 19,
+        in_specs=[VMEM],
+        out_specs=VMEM,
+        scratch_shapes=[pltpu.VMEM((1024, 128), BF)] * 2 + [pltpu.VMEM((1, 1024), F32)],
+    )(data)
+
+
+def run_grad(data, scores, dprobs, stats, other):
     return call(
         grad_kernel,
         shape((32, 80, 128), BF),
-        flops=10 * 1024 * 2048 * 64,
+        flops=6 * 1024 * 2048 * 64,
         nbytes=1 << 20,
-        in_specs=[SMEM] + [VMEM] * 4,
+        in_specs=[VMEM] * 5,
         out_specs=VMEM,
         scratch_shapes=[pltpu.VMEM((1024, 128), BF)] * 4
         + [
-            pltpu.VMEM((32 // SRC_CHUNK, DH, SRC_CHUNK * 64), BF),
+            pltpu.VMEM((CHUNKS, DH, SRC_CHUNK * 64), BF),
             pltpu.VMEM((1024, 128), F32),
             pltpu.VMEM((1024, 128), F32),
-            pltpu.VMEM((1, 1024), F32),
         ],
-    )(half, vis_row, data, stats, other)
+    )(data, scores, dprobs, stats, other)
 
 
 def run_join(back):
     return call(join_kernel, shape((128, 1024), BF), nbytes=1 << 19, in_specs=[VMEM], out_specs=VMEM)(back)
 
 
-def run_key(own_t, far_t, *dks):
+def run_key(turned, *dks):
     return call(
         key_kernel,
         shape((64, 4, 1024), BF),
         flops=2 * 256 * 512 * 1024,
         nbytes=2 << 20,
-        in_specs=[VMEM] * 6,
+        in_specs=[VMEM] * 5,
         out_specs=VMEM,
-    )(own_t, far_t, *dks)
+    )(turned, *dks)
 
 
 def run_post(dk, back, w_query, w_key, w_value):
@@ -330,18 +346,19 @@
     picked = pick_rows(lax.axis_index("x_low"), lax.axis_index("core"))
     turned = dot_nt(picked, prefix).astype(BF).reshape(4, 256, 128)
     gained = over_core(jnp.stack([turned[1], turned[3]]))
-    own_t = jnp.stack([turned[0], gained[0]])
     far_t = over_x(jnp.stack([turned[2], gained[1]]))
-
-    stats = run_stats(half, visible, data)
-    stats, own_t, far_t = lax.optimization_barrier((stats, own_t, far_t))
+    turned = jnp.concatenate([turned[0], gained[0], far_t[0], far_t[1]], axis=1)
+
+    stats, scores = run_stats(half, visible, data)
+    stats, turned = lax.optimization_barrier((stats, turned))
     other = lax.ppermute(stats, "z", [(i, i ^ 1) for i in range(8)])
-    back = run_grad(half, visible, data, stats, other)
+    dprobs = run_dprobs(data)
+    back = run_grad(data, scores, dprobs, stats, other)
     back = lax.all_to_all(back, ("y", "z"), 0, 0, tiled=True)
 
     dk = run_join(back)
     far_dk = over_x(dk)
-    part = run_key(own_t, far_t, dk, over_core(dk), far_dk, over_core(far_dk))
+    part = run_key(turned, dk, over_core(dk), far_dk, over_core(far_dk))
     part = lax.all_to_all(part, ("x_high", "y", "z"), 0, 0, tiled=True)
     key_wgrad = jnp.sum(part.astype(F32), axis=0)
     prefix_grad, latent_grad = run_post(dk, back, w_query, w_key, w_value)

time: 116 us -> 114 us (0.983)
  waiting for transfers between devices: 47.1 us -> 45.8 us
    all_to_all x1, waiting for transfers between devices: 21.7 us -> 16.7 us  [on_device(): data = lax.all_to_all(data, ('y', 'z'), 0, 0, tiled=True)]
    ppermute x2, waiting for transfers between devices: 5.8 us -> 10.8 us  [on_device(): over_x = lambda v: lax.ppermute(v, 'x_low', [(0, 1), (1, 0)])]
    ppermute x1, waiting for transfers between devices: 2.4 us -> 1.04 us  [on_device(): other = lax.ppermute(stats, 'z', [(i, i ^ 1) for i in range(8)])]
    pallas_call x2 -> x3, Pallas kernels: 9.03 us -> 8.17 us  [the longest x1 3.47 us: run_stats(): call(stats_kernel, (shape((8, 1024), F32), shape((2, 1024, 1024), F32)),...]
  transfers between devices with their start and end apart: 8 -> 8, of which waited for: 6 -> 7; matrix products, arithmetic and copies ran while one was open for 1% -> 1% of each run, Pallas kernels for 8% -> 7%
where the time goes in v4:
time: 114 us
  waiting for transfers between devices  45.8 us (40%)
  blocking collectives  22.8 us (20%)
  starting transfers between devices  22.3 us (20%)
  Pallas kernels  20.1 us (18%)
    all_to_all x1, blocking collectives, on_device(): back = lax.all_to_all(back, ('y', 'z'), 0, 0, tiled=True)  22.8 us
    all_to_all x1, waiting for transfers between devices, on_device(): data = lax.all_to_all(data, ('y', 'z'), 0, 0, tiled=True)  16.7 us
    all_to_all x1, waiting for transfers between devices, on_device(): part = lax.all_to_all(part, ('x_high', 'y', 'z'), 0, 0, tiled=True)  14.3 us
    all_to_all x1, starting transfers between devices, on_device(): data = lax.all_to_all(data, ('y', 'z'), 0, 0, tiled=True)  11.6 us
    ppermute x2, waiting for transfers between devices, on_device(): over_x = lambda v: lax.ppermute(v, 'x_low', [(0, 1), (1, 0)])  10.8 us
    all_to_all x1, starting transfers between devices, on_device(): part = lax.all_to_all(part, ('x_high', 'y', 'z'), 0, 0, tiled=True)  7.56 us
    pallas_call x1, Pallas kernels, run_post(): call(post_kernel, (shape((128, 1024), BF), shape((32, 1024), BF)), limit=...  6.04 us
    pallas_call x1, Pallas kernels, run_pre(): call(pre_kernel, shape((32, 104, 128), BF), limit=60, flops=2 * 288 * 102...  4.46 us
  transfers between devices with their start and end apart: 8, of which 7 were waited for; matrix products, arithmetic and copies ran while one was open for 1% of the time, Pallas kernels for 7%

profile of v4, /device:TPU:2, one launch (start us, length us, event | category | flops | bytes accessed | tf_op | source)
XLA Modules:
  0.0 113.5 jit_solution(3392815290400896713)
XLA Ops:
  0.6 0.0 copy-start.3
  0.6 4.5 %shard_map.103 = bf16[32,104,128]{2,1,0:T(8,128)(2,1)} custom-call(bf16[128,1024]{1,0:T(8,128)(2,1)} %bitcast.21, bf16[32,1024]{1,0:T(8,128)(2,1)} %bitcast.22, bf16[32,1024]{1,0:T(8,128)(2,1)} %bitcast.23, bf16[32,1024]{1,0:T(8,128)(2,1)} %bitcast.24, bf16[1024,1024]{1,0:T(8,128)(2,1)} %w_query.3, bf16[1024,1024]{1,0:T(8,128)(2,1)} %w_key.3, ...), custom_call_target="tpu_custom_call" | custom-call | flops 603979776 | bytes 8388608 | tf_op jit(solution)/shard_map/pallas_call | solution.py:248
  5.1 0.0 copy-start.2
  5.1 11.6 %all-to-all-start = ((bf16[32,104,128]{2,1,0:T(8,128)(2,1)}), bf16[32,104,128]{2,1,0:T(8,128)(2,1)S(1)}, u32[]{:S(2)}, u32[]{:S(2)}) async-start(bf16[32,104,128]{2,1,0:T(8,128)(2,1)} %shard_map.103), calls=%async_computation | async-start | bytes 1703936 | tf_op jit(solution)/shard_map/all_to_all | solution.py:345
  16.8 0.0 copy-done.3
  16.8 0.8 fusion.2
  17.6 0.1 collective-permute-start
  17.8 1.3 %collective-permute-done = bf16[2,256,128]{2,1,0:T(8,128)(2,1)S(1)} collective-permute-done((bf16[2,256,128]{2,1,0:T(8,128)(2,1)S(1)}, bf16[2,256,128]{2,1,0:T(8,128)(2,1)S(1)}, u32[]{:S(2)}, u32[]{:S(2)}) %collective-permute-start) | collective-permute-done | bytes 131104 | tf_op jit(solution)/shard_map/ppermute | solution.py:341
  19.1 0.6 collective-permute-start.1
  19.8 5.0 %collective-permute-done.1 = bf16[2,256,128]{2,1,0:T(8,128)(2,1)S(1)} collective-permute-done((bf16[2,256,128]{2,1,0:T(8,128)(2,1)S(1)}, bf16[2,256,128]{2,1,0:T(8,128)(2,1)S(1)}, u32[]{:S(2)}, u32[]{:S(2)}) %collective-permute-start.1) | collective-permute-done | bytes 131104 | tf_op jit(solution)/shard_map/ppermute | solution.py:342
  24.8 16.7 %all-to-all-done.data = bf16[32,104,128]{2,1,0:T(8,128)(2,1)S(1)} async-done(((bf16[32,104,128]{2,1,0:T(8,128)(2,1)}), bf16[32,104,128]{2,1,0:T(8,128)(2,1)S(1)}, u32[]{:S(2)}, u32[]{:S(2)}) %all-to-all-start) | async-done | bytes 852000 | tf_op jit(solution)/shard_map/all_to_all | solution.py:345
  41.5 0.0 copy-done.2
  41.5 3.5 %shard_map.104 = (f32[8,1024]{1,0:T(8,128)S(1)}, f32[2,1024,1024]{2,1,0:T(8,128)S(1)}) custom-call(s32[1]{0:T(128)} %bitcast.4.half_s, s32[1,1024]{1,0:T(1,128)S(1)} %copy-done.2, bf16[32,104,128]{2,1,0:T(8,128)(2,1)S(1)} %all-to-all-done.data), custom_call_target="tpu_custom_call" | custom-call | flops 268435456 | bytes 524288 | tf_op jit(solution)/shard_map/pallas_call | solution.py:261
  45.0 1.6 %collective-permute-start.2 = (f32[8,1024]{1,0:T(8,128)S(1)}, f32[8,1024]{1,0:T(8,128)S(1)}, u32[]{:S(2)}, u32[]{:S(2)}) collective-permute-start(f32[8,1024]{1,0:T(8,128)S(1)} %get-tuple-element.11.own), channel_id=1, source_target_pairs={{0,8},{8,0},{16,24},{24,16},{32,40},{40,32},{48,56},{56,48},{1,9},... | collective-permute-start | bytes 98312 | tf_op jit(solution)/shard_map/ppermute | solution.py:354
  46.6 1.3 %shard_map.105.dprobs = f32[2,1024,1024]{2,1,0:T(8,128)S(1)} custom-call(bf16[32,104,128]{2,1,0:T(8,128)(2,1)S(1)} %all-to-all-done.data), custom_call_target="tpu_custom_call" | custom-call | flops 268435456 | bytes 524288 | tf_op jit(solution)/shard_map/pallas_call | solution.py:273
  48.0 1.0 collective-permute-done.2.other
  49.0 3.4 %shard_map.106 = bf16[32,80,128]{2,1,0:T(8,128)(2,1)S(1)} custom-call(bf16[32,104,128]{2,1,0:T(8,128)(2,1)S(1)} %all-to-all-done.data, f32[2,1024,1024]{2,1,0:T(8,128)S(1)} %get-tuple-element.9.scores, f32[2,1024,1024]{2,1,0:T(8,128)S(1)} %shard_map.105.dprobs, f32[8,1024]{1,0:T(8,128)S(1)} %get-tuple-element.11.own, f32[8,1024]{1,0:T(8,128)S(1)} %collective-permute-done.2.other), custom_call_target="tpu_custom_call" | custom-call | flops 805306368 | bytes 1048576 | tf_op jit(solution)/shard_map/pallas_call | solution.py:285
  52.4 22.8 %all_to_all.15.folded = bf16[32,80,128]{2,1,0:T(8,128)(2,1)S(1)} all-to-all(bf16[32,80,128]{2,1,0:T(8,128)(2,1)S(1)} %shard_map.106), channel_id=1, replica_groups=mesh['y'=4,'z'=8,'x_high'=2,'x_low'=2,'core'=2] {'y','z'}, dimensions={0} | all-to-all | bytes 1310720 | tf_op jit(solution)/shard_map/all_to_all | solution.py:357
  75.1 0.0 copy-start
  75.1 0.1 shard_map.107.dk.dk_0
  75.3 0.0 copy-start.1
  75.3 0.8 collective-permute-start.4
  76.1 0.0 collective-permute-start.3
  76.1 5.8 %collective-permute-done.4.dk_2 = bf16[128,1024]{1,0:T(8,128)(2,1)S(1)} collective-permute-done((bf16[128,1024]{1,0:T(8,128)(2,1)S(1)}, bf16[128,1024]{1,0:T(8,128)(2,1)S(1)}, u32[]{:S(2)}, u32[]{:S(2)}) %collective-permute-start.4) | collective-permute-done | bytes 262176 | tf_op jit(solution)/shard_map/ppermute | solution.py:342
  81.9 0.0 collective-permute-start.5
  81.9 0.0 collective-permute-done.3.dk_1
  81.9 1.5 %collective-permute-done.5.dk_3 = bf16[128,1024]{1,0:T(8,128)(2,1)S(1)} collective-permute-done((bf16[128,1024]{1,0:T(8,128)(2,1)S(1)}, bf16[128,1024]{1,0:T(8,128)(2,1)S(1)}, u32[]{:S(2)}, u32[]{:S(2)}) %collective-permute-start.5) | collective-permute-done | bytes 262176 | tf_op jit(solution)/shard_map/ppermute | solution.py:341
  83.5 1.3 %shard_map.109 = bf16[64,4,1024]{2,1,0:T(4,128)(2,1)} custom-call(bf16[256,512]{1,0:T(8,128)(2,1)S(1)} %pad_maximum_fusion.turned, bf16[128,1024]{1,0:T(8,128)(2,1)S(1)} %shard_map.107.dk.dk_0, bf16[128,1024]{1,0:T(8,128)(2,1)S(1)} %collective-permute-done.3.dk_1, bf16[128,1024]{1,0:T(8,128)(2,1)S(1)} %collective-permute-done.4.dk_2, ...), custom_call_target="tpu_custom_call" | custom-call | flops 268435456 | bytes 2097152 | tf_op jit(solution)/shard_map/pallas_call | solution.py:306
  84.7 7.6 %all-to-all-start.2 = ((bf16[64,4,1024]{2,1,0:T(4,128)(2,1)}), bf16[64,4,1024]{2,1,0:T(4,128)(2,1)S(1)}, u32[]{:S(2)}, u32[]{:S(2)}) async-start(bf16[64,4,1024]{2,1,0:T(4,128)(2,1)} %shard_map.109), calls=%async_computation.2 | async-start | bytes 1048576 | tf_op jit(solution)/shard_map/all_to_all | solution.py:362
  92.3 0.0 copy-done
  92.3 0.0 copy-done.1
  92.3 6.0 %shard_map.108 = (bf16[128,1024]{1,0:T(8,128)(2,1)}, bf16[32,1024]{1,0:T(8,128)(2,1)}) custom-call(bf16[128,1024]{1,0:T(8,128)(2,1)} %copy-done.1, bf16[32,80,128]{2,1,0:T(8,128)(2,1)} %copy-done, bf16[1024,1024]{1,0:T(8,128)(2,1)} %w_query.3, bf16[1024,1024]{1,0:T(8,128)(2,1)} %w_key.3, bf16[1024,1024]{1,0:T(8,128)(2,1)} %w_value.3), custom_call_target="tpu_custom_call" | custom-call | flops 603979776 | bytes 8388608 | tf_op jit(solution)/shard_map/pallas_call | solution.py:318
  98.3 14.3 %all-to-all-done.2 = bf16[64,4,1024]{2,1,0:T(4,128)(2,1)S(1)} async-done(((bf16[64,4,1024]{2,1,0:T(4,128)(2,1)}), bf16[64,4,1024]{2,1,0:T(4,128)(2,1)S(1)}, u32[]{:S(2)}, u32[]{:S(2)}) %all-to-all-start.2) | async-done | bytes 524320 | tf_op jit(solution)/shard_map/all_to_all | solution.py:362
  112.7 0.8 convert_reduce_fusion
  (7 shorter events, 0.1 us)
Async XLA Ops:
  0.6 16.1 %copy-start.3 = (bf16[1,128,1024]{2,1,0:T(8,128)(2,1)S(1)}, bf16[1,128,1024]{2,1,0:T(8,128)(2,1)}, u32[]{:S(2)}) copy-start(bf16[1,128,1024]{2,1,0:T(8,128)(2,1)} %param.8) | copy-start | bytes 786436
  5.1 36.4 %copy-start.2 = (s32[1,1024]{1,0:T(1,128)S(1)}, s32[1,1024]{1,0:T(1,128)}, u32[]{:S(2)}) copy-start(s32[1,1024]{1,0:T(1,128)} %vis.1) | copy-start | bytes 12292
  5.1 36.4 %all-to-all-start = ((bf16[32,104,128]{2,1,0:T(8,128)(2,1)}), bf16[32,104,128]{2,1,0:T(8,128)(2,1)S(1)}, u32[]{:S(2)}, u32[]{:S(2)}) async-start(bf16[32,104,128]{2,1,0:T(8,128)(2,1)} %shard_map.103), calls=%async_computation | async-start | bytes 1703936 | tf_op jit(solution)/shard_map/all_to_all | solution.py:345
  17.6 1.4 %collective-permute-start = (bf16[2,256,128]{2,1,0:T(8,128)(2,1)S(1)}, bf16[2,256,128]{2,1,0:T(8,128)(2,1)S(1)}, u32[]{:S(2)}, u32[]{:S(2)}) collective-permute-start(bf16[2,256,128]{2,1,0:T(8,128)(2,1)S(1)} %pad_maximum_fusion.1), channel_id=1, source_target_pairs={{0,1},{1,0},{2,3},{3,2},{4,5},{5,4},{6,7},{7,6},{8,9},{9,8},{10,11... | collective-permute-start | bytes 393224 | tf_op jit(solution)/shard_map/ppermute | solution.py:341
  19.1 5.6 %collective-permute-start.1 = (bf16[2,256,128]{2,1,0:T(8,128)(2,1)S(1)}, bf16[2,256,128]{2,1,0:T(8,128)(2,1)S(1)}, u32[]{:S(2)}, u32[]{:S(2)}) collective-permute-start(bf16[2,256,128]{2,1,0:T(8,128)(2,1)S(1)} %pad_maximum_fusion.2), channel_id=1, source_target_pairs={{0,2},{2,0},{1,3},{3,1},{4,6},{6,4},{5,7},{7,5},{8,10},{10,8},{9,1... | collective-permute-start | bytes 393224 | tf_op jit(solution)/shard_map/ppermute | solution.py:342
  45.0 4.0 %collective-permute-start.2 = (f32[8,1024]{1,0:T(8,128)S(1)}, f32[8,1024]{1,0:T(8,128)S(1)}, u32[]{:S(2)}, u32[]{:S(2)}) collective-permute-start(f32[8,1024]{1,0:T(8,128)S(1)} %get-tuple-element.11.own), channel_id=1, source_target_pairs={{0,8},{8,0},{16,24},{24,16},{32,40},{40,32},{48,56},{56,48},{1,9},... | collective-permute-start | bytes 98312 | tf_op jit(solution)/shard_map/ppermute | solution.py:354
  75.1 17.2 %copy-start = (bf16[32,80,128]{2,1,0:T(8,128)(2,1)}, bf16[32,80,128]{2,1,0:T(8,128)(2,1)S(1)}, u32[]{:S(2)}) copy-start(bf16[32,80,128]{2,1,0:T(8,128)(2,1)S(1)} %all_to_all.15.folded) | copy-start | bytes 1966084
  75.3 17.0 %copy-start.1 = (bf16[128,1024]{1,0:T(8,128)(2,1)}, bf16[128,1024]{1,0:T(8,128)(2,1)S(1)}, u32[]{:S(2)}) copy-start(bf16[128,1024]{1,0:T(8,128)(2,1)S(1)} %shard_map.107.dk.dk_0) | copy-start | bytes 786436
  75.3 6.6 %collective-permute-start.4 = (bf16[128,1024]{1,0:T(8,128)(2,1)S(1)}, bf16[128,1024]{1,0:T(8,128)(2,1)S(1)}, u32[]{:S(2)}, u32[]{:S(2)}) collective-permute-start(bf16[128,1024]{1,0:T(8,128)(2,1)S(1)} %shard_map.107.dk.dk_0), channel_id=1, source_target_pairs={{0,2},{2,0},{1,3},{3,1},{4,6},{6,4},{5,7},{7,5},{8,10},{10,8},{9,1... | collective-permute-start | bytes 786440 | tf_op jit(solution)/shard_map/ppermute | solution.py:342
  76.1 5.8 %collective-permute-start.3 = (bf16[128,1024]{1,0:T(8,128)(2,1)S(1)}, bf16[128,1024]{1,0:T(8,128)(2,1)S(1)}, u32[]{:S(2)}, u32[]{:S(2)}) collective-permute-start(bf16[128,1024]{1,0:T(8,128)(2,1)S(1)} %shard_map.107.dk.dk_0), channel_id=1, source_target_pairs={{0,1},{1,0},{2,3},{3,2},{4,5},{5,4},{6,7},{7,6},{8,9},{9,8},{10,11... | collective-permute-start | bytes 786440 | tf_op jit(solution)/shard_map/ppermute | solution.py:341
  81.9 1.5 %collective-permute-start.5 = (bf16[128,1024]{1,0:T(8,128)(2,1)S(1)}, bf16[128,1024]{1,0:T(8,128)(2,1)S(1)}, u32[]{:S(2)}, u32[]{:S(2)}) collective-permute-start(bf16[128,1024]{1,0:T(8,128)(2,1)S(1)} %collective-permute-done.4.dk_2), channel_id=1, source_target_pairs={{0,1},{1,0},{2,3},{3,2},{4,5},{5,4},{6,7},{7,6},{8,9},{9,8},{10,11... | collective-permute-start | bytes 786440 | tf_op jit(solution)/shard_map/ppermute | solution.py:341
  84.7 28.0 %all-to-all-start.2 = ((bf16[64,4,1024]{2,1,0:T(4,128)(2,1)}), bf16[64,4,1024]{2,1,0:T(4,128)(2,1)S(1)}, u32[]{:S(2)}, u32[]{:S(2)}) async-start(bf16[64,4,1024]{2,1,0:T(4,128)(2,1)} %shard_map.109), calls=%async_computation.2 | async-start | bytes 1048576 | tf_op jit(solution)/shard_map/all_to_all | solution.py:362

commit v5 on v4

--- a/solution.py
+++ b/solution.py
@@ -331,7 +331,7 @@
 def pick_rows(x_low, core):
     at = lax.broadcasted_iota(jnp.int32, (1024, 1024), 0)
     x_to, core_to = x_low ^ (at >> 9), core ^ ((at >> 8) & 1)
-    wanted = ((at >> 2) & 31) * 32 + ((at >> 7) & 1) * 16 + x_to * 8 + core_to * 4 + (at & 3)
+    wanted = ((at >> 3) & 31) * 32 + ((at >> 2) & 1) * 16 + x_to * 8 + core_to * 4 + (at & 3)
     return (wanted == lax.broadcasted_iota(jnp.int32, (1024, 1024), 1)).astype(BF)
 
 
@@ -359,7 +359,7 @@
     dk = run_join(back)
     far_dk = over_x(dk)
     part = run_key(turned, dk, over_core(dk), far_dk, over_core(far_dk))
-    part = lax.all_to_all(part, ("x_high", "y", "z"), 0, 0, tiled=True)
+    part = lax.all_to_all(part, ("y", "z", "x_high"), 0, 0, tiled=True)
     key_wgrad = jnp.sum(part.astype(F32), axis=0)
     prefix_grad, latent_grad = run_post(dk, back, w_query, w_key, w_value)
     return prefix_grad[None], latent_grad[None], key_wgrad

time: 114 us -> 113 us (level)
  no operation moved by 1% of the time
where the time goes in v5:
time: 113 us
  waiting for transfers between devices  45 us (40%)
  blocking collectives  22.8 us (20%)
  starting transfers between devices  22.3 us (20%)
  Pallas kernels  20.1 us (18%)
    all_to_all x1, blocking collectives, on_device(): back = lax.all_to_all(back, ('y', 'z'), 0, 0, tiled=True)  22.8 us
    all_to_all x1, waiting for transfers between devices, on_device(): data = lax.all_to_all(data, ('y', 'z'), 0, 0, tiled=True)  16.7 us
    all_to_all x1, waiting for transfers between devices, on_device(): part = lax.all_to_all(part, ('y', 'z', 'x_high'), 0, 0, tiled=True)  13.6 us
    all_to_all x1, starting transfers between devices, on_device(): data = lax.all_to_all(data, ('y', 'z'), 0, 0, tiled=True)  11.6 us
    ppermute x2, waiting for transfers between devices, on_device(): over_x = lambda v: lax.ppermute(v, 'x_low', [(0, 1), (1, 0)])  10.8 us
    all_to_all x1, starting transfers between devices, on_device(): part = lax.all_to_all(part, ('y', 'z', 'x_high'), 0, 0, tiled=True)  7.56 us
    pallas_call x1, Pallas kernels, run_post(): call(post_kernel, (shape((128, 1024), BF), shape((32, 1024), BF)), limit=...  6.04 us
    pallas_call x1, Pallas kernels, run_pre(): call(pre_kernel, shape((32, 104, 128), BF), limit=60, flops=2 * 288 * 102...  4.46 us
  transfers between devices with their start and end apart: 8, of which 7 were waited for; matrix products, arithmetic and copies ran while one was open for 1% of the time, Pallas kernels for 7%

profile of v5, /device:TPU:2, one launch (start us, length us, event | category | flops | bytes accessed | tf_op | source)
XLA Modules:
  0.0 112.8 jit_solution(15111441020556960355)
XLA Ops:
  0.6 0.0 copy-start.3
  0.6 4.5 %shard_map.103 = bf16[32,104,128]{2,1,0:T(8,128)(2,1)} custom-call(bf16[128,1024]{1,0:T(8,128)(2,1)} %bitcast.21, bf16[32,1024]{1,0:T(8,128)(2,1)} %bitcast.22, bf16[32,1024]{1,0:T(8,128)(2,1)} %bitcast.23, bf16[32,1024]{1,0:T(8,128)(2,1)} %bitcast.24, bf16[1024,1024]{1,0:T(8,128)(2,1)} %w_query.3, bf16[1024,1024]{1,0:T(8,128)(2,1)} %w_key.3, ...), custom_call_target="tpu_custom_call" | custom-call | flops 603979776 | bytes 8388608 | tf_op jit(solution)/shard_map/pallas_call | solution.py:248
  5.1 0.0 copy-start.2
  5.1 11.6 %all-to-all-start = ((bf16[32,104,128]{2,1,0:T(8,128)(2,1)}), bf16[32,104,128]{2,1,0:T(8,128)(2,1)S(1)}, u32[]{:S(2)}, u32[]{:S(2)}) async-start(bf16[32,104,128]{2,1,0:T(8,128)(2,1)} %shard_map.103), calls=%async_computation | async-start | bytes 1703936 | tf_op jit(solution)/shard_map/all_to_all | solution.py:345
  16.8 0.0 copy-done.3
  16.8 0.8 fusion.2
  17.6 0.1 collective-permute-start
  17.8 1.3 %collective-permute-done = bf16[2,256,128]{2,1,0:T(8,128)(2,1)S(1)} collective-permute-done((bf16[2,256,128]{2,1,0:T(8,128)(2,1)S(1)}, bf16[2,256,128]{2,1,0:T(8,128)(2,1)S(1)}, u32[]{:S(2)}, u32[]{:S(2)}) %collective-permute-start) | collective-permute-done | bytes 131104 | tf_op jit(solution)/shard_map/ppermute | solution.py:341
  19.1 0.6 collective-permute-start.1
  19.8 5.0 %collective-permute-done.1 = bf16[2,256,128]{2,1,0:T(8,128)(2,1)S(1)} collective-permute-done((bf16[2,256,128]{2,1,0:T(8,128)(2,1)S(1)}, bf16[2,256,128]{2,1,0:T(8,128)(2,1)S(1)}, u32[]{:S(2)}, u32[]{:S(2)}) %collective-permute-start.1) | collective-permute-done | bytes 131104 | tf_op jit(solution)/shard_map/ppermute | solution.py:342
  24.8 16.7 %all-to-all-done.data = bf16[32,104,128]{2,1,0:T(8,128)(2,1)S(1)} async-done(((bf16[32,104,128]{2,1,0:T(8,128)(2,1)}), bf16[32,104,128]{2,1,0:T(8,128)(2,1)S(1)}, u32[]{:S(2)}, u32[]{:S(2)}) %all-to-all-start) | async-done | bytes 852000 | tf_op jit(solution)/shard_map/all_to_all | solution.py:345
  41.5 0.0 copy-done.2
  41.5 3.5 %shard_map.104 = (f32[8,1024]{1,0:T(8,128)S(1)}, f32[2,1024,1024]{2,1,0:T(8,128)S(1)}) custom-call(s32[1]{0:T(128)} %bitcast.4.half_s, s32[1,1024]{1,0:T(1,128)S(1)} %copy-done.2, bf16[32,104,128]{2,1,0:T(8,128)(2,1)S(1)} %all-to-all-done.data), custom_call_target="tpu_custom_call" | custom-call | flops 268435456 | bytes 524288 | tf_op jit(solution)/shard_map/pallas_call | solution.py:261
  45.0 1.6 %collective-permute-start.2 = (f32[8,1024]{1,0:T(8,128)S(1)}, f32[8,1024]{1,0:T(8,128)S(1)}, u32[]{:S(2)}, u32[]{:S(2)}) collective-permute-start(f32[8,1024]{1,0:T(8,128)S(1)} %get-tuple-element.11.own), channel_id=1, source_target_pairs={{0,8},{8,0},{16,24},{24,16},{32,40},{40,32},{48,56},{56,48},{1,9},... | collective-permute-start | bytes 98312 | tf_op jit(solution)/shard_map/ppermute | solution.py:354
  46.6 1.3 %shard_map.105.dprobs = f32[2,1024,1024]{2,1,0:T(8,128)S(1)} custom-call(bf16[32,104,128]{2,1,0:T(8,128)(2,1)S(1)} %all-to-all-done.data), custom_call_target="tpu_custom_call" | custom-call | flops 268435456 | bytes 524288 | tf_op jit(solution)/shard_map/pallas_call | solution.py:273
  48.0 1.0 collective-permute-done.2.other
  49.0 3.4 %shard_map.106 = bf16[32,80,128]{2,1,0:T(8,128)(2,1)S(1)} custom-call(bf16[32,104,128]{2,1,0:T(8,128)(2,1)S(1)} %all-to-all-done.data, f32[2,1024,1024]{2,1,0:T(8,128)S(1)} %get-tuple-element.9.scores, f32[2,1024,1024]{2,1,0:T(8,128)S(1)} %shard_map.105.dprobs, f32[8,1024]{1,0:T(8,128)S(1)} %get-tuple-element.11.own, f32[8,1024]{1,0:T(8,128)S(1)} %collective-permute-done.2.other), custom_call_target="tpu_custom_call" | custom-call | flops 805306368 | bytes 1048576 | tf_op jit(solution)/shard_map/pallas_call | solution.py:285
  52.4 22.8 %all_to_all.15.folded = bf16[32,80,128]{2,1,0:T(8,128)(2,1)S(1)} all-to-all(bf16[32,80,128]{2,1,0:T(8,128)(2,1)S(1)} %shard_map.106), channel_id=1, replica_groups=mesh['y'=4,'z'=8,'x_high'=2,'x_low'=2,'core'=2] {'y','z'}, dimensions={0} | all-to-all | bytes 1310720 | tf_op jit(solution)/shard_map/all_to_all | solution.py:357
  75.1 0.0 copy-start
  75.1 0.1 shard_map.107.dk.dk_0
  75.3 0.0 copy-start.1
  75.3 0.8 collective-permute-start.4
  76.1 0.0 collective-permute-start.3
  76.1 5.8 %collective-permute-done.4.dk_2 = bf16[128,1024]{1,0:T(8,128)(2,1)S(1)} collective-permute-done((bf16[128,1024]{1,0:T(8,128)(2,1)S(1)}, bf16[128,1024]{1,0:T(8,128)(2,1)S(1)}, u32[]{:S(2)}, u32[]{:S(2)}) %collective-permute-start.4) | collective-permute-done | bytes 262176 | tf_op jit(solution)/shard_map/ppermute | solution.py:342
  81.9 0.0 collective-permute-start.5
  81.9 0.0 collective-permute-done.3.dk_1
  81.9 1.5 %collective-permute-done.5.dk_3 = bf16[128,1024]{1,0:T(8,128)(2,1)S(1)} collective-permute-done((bf16[128,1024]{1,0:T(8,128)(2,1)S(1)}, bf16[128,1024]{1,0:T(8,128)(2,1)S(1)}, u32[]{:S(2)}, u32[]{:S(2)}) %collective-permute-start.5) | collective-permute-done | bytes 262176 | tf_op jit(solution)/shard_map/ppermute | solution.py:341
  83.5 1.3 %shard_map.109 = bf16[64,4,1024]{2,1,0:T(4,128)(2,1)} custom-call(bf16[256,512]{1,0:T(8,128)(2,1)S(1)} %pad_maximum_fusion.turned, bf16[128,1024]{1,0:T(8,128)(2,1)S(1)} %shard_map.107.dk.dk_0, bf16[128,1024]{1,0:T(8,128)(2,1)S(1)} %collective-permute-done.3.dk_1, bf16[128,1024]{1,0:T(8,128)(2,1)S(1)} %collective-permute-done.4.dk_2, ...), custom_call_target="tpu_custom_call" | custom-call | flops 268435456 | bytes 2097152 | tf_op jit(solution)/shard_map/pallas_call | solution.py:306
  84.7 7.6 %all-to-all-start.2 = ((bf16[64,4,1024]{2,1,0:T(4,128)(2,1)}), bf16[64,4,1024]{2,1,0:T(4,128)(2,1)S(1)}, u32[]{:S(2)}, u32[]{:S(2)}) async-start(bf16[64,4,1024]{2,1,0:T(4,128)(2,1)} %shard_map.109), calls=%async_computation.2 | async-start | bytes 1048576 | tf_op jit(solution)/shard_map/all_to_all | solution.py:362
  92.3 0.0 copy-done
  92.3 0.0 copy-done.1
  92.3 6.0 %shard_map.108 = (bf16[128,1024]{1,0:T(8,128)(2,1)}, bf16[32,1024]{1,0:T(8,128)(2,1)}) custom-call(bf16[128,1024]{1,0:T(8,128)(2,1)} %copy-done.1, bf16[32,80,128]{2,1,0:T(8,128)(2,1)} %copy-done, bf16[1024,1024]{1,0:T(8,128)(2,1)} %w_query.3, bf16[1024,1024]{1,0:T(8,128)(2,1)} %w_key.3, bf16[1024,1024]{1,0:T(8,128)(2,1)} %w_value.3), custom_call_target="tpu_custom_call" | custom-call | flops 603979776 | bytes 8388608 | tf_op jit(solution)/shard_map/pallas_call | solution.py:318
  98.3 13.6 %all-to-all-done.2 = bf16[64,4,1024]{2,1,0:T(4,128)(2,1)S(1)} async-done(((bf16[64,4,1024]{2,1,0:T(4,128)(2,1)}), bf16[64,4,1024]{2,1,0:T(4,128)(2,1)S(1)}, u32[]{:S(2)}, u32[]{:S(2)}) %all-to-all-start.2) | async-done | bytes 524320 | tf_op jit(solution)/shard_map/all_to_all | solution.py:362
  111.9 0.8 convert_reduce_fusion
  (7 shorter events, 0.1 us)
Async XLA Ops:
  0.6 16.1 %copy-start.3 = (bf16[1,128,1024]{2,1,0:T(8,128)(2,1)S(1)}, bf16[1,128,1024]{2,1,0:T(8,128)(2,1)}, u32[]{:S(2)}) copy-start(bf16[1,128,1024]{2,1,0:T(8,128)(2,1)} %param.8) | copy-start | bytes 786436
  5.1 36.4 %copy-start.2 = (s32[1,1024]{1,0:T(1,128)S(1)}, s32[1,1024]{1,0:T(1,128)}, u32[]{:S(2)}) copy-start(s32[1,1024]{1,0:T(1,128)} %vis.1) | copy-start | bytes 12292
  5.1 36.4 %all-to-all-start = ((bf16[32,104,128]{2,1,0:T(8,128)(2,1)}), bf16[32,104,128]{2,1,0:T(8,128)(2,1)S(1)}, u32[]{:S(2)}, u32[]{:S(2)}) async-start(bf16[32,104,128]{2,1,0:T(8,128)(2,1)} %shard_map.103), calls=%async_computation | async-start | bytes 1703936 | tf_op jit(solution)/shard_map/all_to_all | solution.py:345
  17.6 1.4 %collective-permute-start = (bf16[2,256,128]{2,1,0:T(8,128)(2,1)S(1)}, bf16[2,256,128]{2,1,0:T(8,128)(2,1)S(1)}, u32[]{:S(2)}, u32[]{:S(2)}) collective-permute-start(bf16[2,256,128]{2,1,0:T(8,128)(2,1)S(1)} %pad_maximum_fusion.1), channel_id=1, source_target_pairs={{0,1},{1,0},{2,3},{3,2},{4,5},{5,4},{6,7},{7,6},{8,9},{9,8},{10,11... | collective-permute-start | bytes 393224 | tf_op jit(solution)/shard_map/ppermute | solution.py:341
  19.1 5.6 %collective-permute-start.1 = (bf16[2,256,128]{2,1,0:T(8,128)(2,1)S(1)}, bf16[2,256,128]{2,1,0:T(8,128)(2,1)S(1)}, u32[]{:S(2)}, u32[]{:S(2)}) collective-permute-start(bf16[2,256,128]{2,1,0:T(8,128)(2,1)S(1)} %pad_maximum_fusion.2), channel_id=1, source_target_pairs={{0,2},{2,0},{1,3},{3,1},{4,6},{6,4},{5,7},{7,5},{8,10},{10,8},{9,1... | collective-permute-start | bytes 393224 | tf_op jit(solution)/shard_map/ppermute | solution.py:342
  45.0 4.0 %collective-permute-start.2 = (f32[8,1024]{1,0:T(8,128)S(1)}, f32[8,1024]{1,0:T(8,128)S(1)}, u32[]{:S(2)}, u32[]{:S(2)}) collective-permute-start(f32[8,1024]{1,0:T(8,128)S(1)} %get-tuple-element.11.own), channel_id=1, source_target_pairs={{0,8},{8,0},{16,24},{24,16},{32,40},{40,32},{48,56},{56,48},{1,9},... | collective-permute-start | bytes 98312 | tf_op jit(solution)/shard_map/ppermute | solution.py:354
  75.1 17.2 %copy-start = (bf16[32,80,128]{2,1,0:T(8,128)(2,1)}, bf16[32,80,128]{2,1,0:T(8,128)(2,1)S(1)}, u32[]{:S(2)}) copy-start(bf16[32,80,128]{2,1,0:T(8,128)(2,1)S(1)} %all_to_all.15.folded) | copy-start | bytes 1966084
  75.3 17.0 %copy-start.1 = (bf16[128,1024]{1,0:T(8,128)(2,1)}, bf16[128,1024]{1,0:T(8,128)(2,1)S(1)}, u32[]{:S(2)}) copy-start(bf16[128,1024]{1,0:T(8,128)(2,1)S(1)} %shard_map.107.dk.dk_0) | copy-start | bytes 786436
  75.3 6.6 %collective-permute-start.4 = (bf16[128,1024]{1,0:T(8,128)(2,1)S(1)}, bf16[128,1024]{1,0:T(8,128)(2,1)S(1)}, u32[]{:S(2)}, u32[]{:S(2)}) collective-permute-start(bf16[128,1024]{1,0:T(8,128)(2,1)S(1)} %shard_map.107.dk.dk_0), channel_id=1, source_target_pairs={{0,2},{2,0},{1,3},{3,1},{4,6},{6,4},{5,7},{7,5},{8,10},{10,8},{9,1... | collective-permute-start | bytes 786440 | tf_op jit(solution)/shard_map/ppermute | solution.py:342
  76.1 5.8 %collective-permute-start.3 = (bf16[128,1024]{1,0:T(8,128)(2,1)S(1)}, bf16[128,1024]{1,0:T(8,128)(2,1)S(1)}, u32[]{:S(2)}, u32[]{:S(2)}) collective-permute-start(bf16[128,1024]{1,0:T(8,128)(2,1)S(1)} %shard_map.107.dk.dk_0), channel_id=1, source_target_pairs={{0,1},{1,0},{2,3},{3,2},{4,5},{5,4},{6,7},{7,6},{8,9},{9,8},{10,11... | collective-permute-start | bytes 786440 | tf_op jit(solution)/shard_map/ppermute | solution.py:341
  81.9 1.5 %collective-permute-start.5 = (bf16[128,1024]{1,0:T(8,128)(2,1)S(1)}, bf16[128,1024]{1,0:T(8,128)(2,1)S(1)}, u32[]{:S(2)}, u32[]{:S(2)}) collective-permute-start(bf16[128,1024]{1,0:T(8,128)(2,1)S(1)} %collective-permute-done.4.dk_2), channel_id=1, source_target_pairs={{0,1},{1,0},{2,3},{3,2},{4,5},{5,4},{6,7},{7,6},{8,9},{9,8},{10,11... | collective-permute-start | bytes 786440 | tf_op jit(solution)/shard_map/ppermute | solution.py:341
  84.7 27.2 %all-to-all-start.2 = ((bf16[64,4,1024]{2,1,0:T(4,128)(2,1)}), bf16[64,4,1024]{2,1,0:T(4,128)(2,1)S(1)}, u32[]{:S(2)}, u32[]{:S(2)}) async-start(bf16[64,4,1024]{2,1,0:T(4,128)(2,1)} %shard_map.109), calls=%async_computation.2 | async-start | bytes 1048576 | tf_op jit(solution)/shard_map/all_to_all | solution.py:362

commit v6 on v5

--- a/solution.py
+++ b/solution.py
@@ -328,10 +328,10 @@
     )(dk, back, w_query, w_key, w_value)
 
 
-def pick_rows(x_low, core):
+def pick_rows(x_high, core):
     at = lax.broadcasted_iota(jnp.int32, (1024, 1024), 0)
-    x_to, core_to = x_low ^ (at >> 9), core ^ ((at >> 8) & 1)
-    wanted = ((at >> 3) & 31) * 32 + ((at >> 2) & 1) * 16 + x_to * 8 + core_to * 4 + (at & 3)
+    x_to, core_to = x_high ^ (at >> 9), core ^ ((at >> 8) & 1)
+    wanted = ((at >> 3) & 31) * 32 + x_to * 16 + ((at >> 2) & 1) * 8 + core_to * 4 + (at & 3)
     return (wanted == lax.broadcasted_iota(jnp.int32, (1024, 1024), 1)).astype(BF)
 
 
@@ -339,11 +339,11 @@
     prefix, latents, saved, grad = prefix[0], latents[0], saved[0], grad[0]
     half = jnp.reshape(lax.axis_index("z") % 2, (1,)).astype(jnp.int32)
     over_core = lambda v: lax.ppermute(v, "core", [(0, 1), (1, 0)])
-    over_x = lambda v: lax.ppermute(v, "x_low", [(0, 1), (1, 0)])
+    over_x = lambda v: lax.ppermute(v, "x_high", [(0, 1), (1, 0)])
 
     data = run_pre(prefix, latents, grad, saved, w_query, w_key, w_value)
     data = lax.all_to_all(data, ("y", "z"), 0, 0, tiled=True)
-    picked = pick_rows(lax.axis_index("x_low"), lax.axis_index("core"))
+    picked = pick_rows(lax.axis_index("x_high"), lax.axis_index("core"))
     turned = dot_nt(picked, prefix).astype(BF).reshape(4, 256, 128)
     gained = over_core(jnp.stack([turned[1], turned[3]]))
     far_t = over_x(jnp.stack([turned[2], gained[1]]))
@@ -359,7 +359,7 @@
     dk = run_join(back)
     far_dk = over_x(dk)
     part = run_key(turned, dk, over_core(dk), far_dk, over_core(far_dk))
-    part = lax.all_to_all(part, ("y", "z", "x_high"), 0, 0, tiled=True)
+    part = lax.all_to_all(part, ("y", "z", "x_low"), 0, 0, tiled=True)
     key_wgrad = jnp.sum(part.astype(F32), axis=0)
     prefix_grad, latent_grad = run_post(dk, back, w_query, w_key, w_value)
     return prefix_grad[None], latent_grad[None], key_wgrad

time: 113 us -> 112 us (level)
  waiting for transfers between devices: 45 us -> 40.5 us
  starting transfers between devices: 22.3 us -> 24.9 us
    ppermute x2, starting transfers between devices: 1.44 us -> 4.6 us  [on_device(): over_x = lambda v: lax.ppermute(v, 'x_high', [(0, 1), (1, 0)])]
    all_to_all x1, waiting for transfers between devices: 13.6 us -> 10.7 us  [on_device(): part = lax.all_to_all(part, ('y', 'z', 'x_low'), 0, 0, tiled=True)]
    all_to_all x1, waiting for transfers between devices: 16.7 us -> 15.2 us  [on_device(): data = lax.all_to_all(data, ('y', 'z'), 0, 0, tiled=True)]
where the time goes in v6:
time: 112 us; the launch traced here: 111 us
  waiting for transfers between devices  40.5 us (36%)
  starting transfers between devices  24.9 us (22%)
  blocking collectives  22.8 us (20%)
  Pallas kernels  20.1 us (18%)
    all_to_all x1, blocking collectives, on_device(): back = lax.all_to_all(back, ('y', 'z'), 0, 0, tiled=True)  22.8 us
    all_to_all x1, waiting for transfers between devices, on_device(): data = lax.all_to_all(data, ('y', 'z'), 0, 0, tiled=True)  15.2 us
    all_to_all x1, starting transfers between devices, on_device(): data = lax.all_to_all(data, ('y', 'z'), 0, 0, tiled=True)  11.6 us
    all_to_all x1, waiting for transfers between devices, on_device(): part = lax.all_to_all(part, ('y', 'z', 'x_low'), 0, 0, tiled=True)  10.7 us
    ppermute x2, waiting for transfers between devices, on_device(): over_x = lambda v: lax.ppermute(v, 'x_high', [(0, 1), (1, 0)])  10.7 us
    all_to_all x1, starting transfers between devices, on_device(): part = lax.all_to_all(part, ('y', 'z', 'x_low'), 0, 0, tiled=True)  7.01 us
    pallas_call x1, Pallas kernels, run_post(): call(post_kernel, (shape((128, 1024), BF), shape((32, 1024), BF)), limit=...  6.05 us
    ppermute x2, starting transfers between devices, on_device(): over_x = lambda v: lax.ppermute(v, 'x_high', [(0, 1), (1, 0)])  4.6 us
  transfers between devices with their start and end apart: 8, of which 7 were waited for; matrix products, arithmetic and copies ran while one was open for 1% of the time, Pallas kernels for 7%

profile of v6, /device:TPU:2, one launch (start us, length us, event | category | flops | bytes accessed | tf_op | source)
XLA Modules:
  0.0 110.9 jit_solution(14968783795550487039)
XLA Ops:
  0.6 0.0 copy-start.3
  0.6 4.5 %shard_map.103 = bf16[32,104,128]{2,1,0:T(8,128)(2,1)} custom-call(bf16[128,1024]{1,0:T(8,128)(2,1)} %bitcast.21, bf16[32,1024]{1,0:T(8,128)(2,1)} %bitcast.22, bf16[32,1024]{1,0:T(8,128)(2,1)} %bitcast.23, bf16[32,1024]{1,0:T(8,128)(2,1)} %bitcast.24, bf16[1024,1024]{1,0:T(8,128)(2,1)} %w_query.3, bf16[1024,1024]{1,0:T(8,128)(2,1)} %w_key.3, ...), custom_call_target="tpu_custom_call" | custom-call | flops 603979776 | bytes 8388608 | tf_op jit(solution)/shard_map/pallas_call | solution.py:248
  5.1 0.0 copy-start.2
  5.1 11.6 %all-to-all-start = ((bf16[32,104,128]{2,1,0:T(8,128)(2,1)}), bf16[32,104,128]{2,1,0:T(8,128)(2,1)S(1)}, u32[]{:S(2)}, u32[]{:S(2)}) async-start(bf16[32,104,128]{2,1,0:T(8,128)(2,1)} %shard_map.103), calls=%async_computation | async-start | bytes 1703936 | tf_op jit(solution)/shard_map/all_to_all | solution.py:345
  16.8 0.0 copy-done.3
  16.8 0.8 fusion.2
  17.6 0.1 collective-permute-start
  17.8 1.3 %collective-permute-done = bf16[2,256,128]{2,1,0:T(8,128)(2,1)S(1)} collective-permute-done((bf16[2,256,128]{2,1,0:T(8,128)(2,1)S(1)}, bf16[2,256,128]{2,1,0:T(8,128)(2,1)S(1)}, u32[]{:S(2)}, u32[]{:S(2)}) %collective-permute-start) | collective-permute-done | bytes 131104 | tf_op jit(solution)/shard_map/ppermute | solution.py:341
  19.1 2.2 %collective-permute-start.1 = (bf16[2,256,128]{2,1,0:T(8,128)(2,1)S(1)}, bf16[2,256,128]{2,1,0:T(8,128)(2,1)S(1)}, u32[]{:S(2)}, u32[]{:S(2)}) collective-permute-start(bf16[2,256,128]{2,1,0:T(8,128)(2,1)S(1)} %pad_maximum_fusion.2), channel_id=1, source_target_pairs={{0,4},{4,0},{1,5},{5,1},{2,6},{6,2},{3,7},{7,3},{8,12},{12,8},{9,1... | collective-permute-start | bytes 393224 | tf_op jit(solution)/shard_map/ppermute | solution.py:342
  21.3 4.9 %collective-permute-done.1 = bf16[2,256,128]{2,1,0:T(8,128)(2,1)S(1)} collective-permute-done((bf16[2,256,128]{2,1,0:T(8,128)(2,1)S(1)}, bf16[2,256,128]{2,1,0:T(8,128)(2,1)S(1)}, u32[]{:S(2)}, u32[]{:S(2)}) %collective-permute-start.1) | collective-permute-done | bytes 131104 | tf_op jit(solution)/shard_map/ppermute | solution.py:342
  26.3 15.2 %all-to-all-done.data = bf16[32,104,128]{2,1,0:T(8,128)(2,1)S(1)} async-done(((bf16[32,104,128]{2,1,0:T(8,128)(2,1)}), bf16[32,104,128]{2,1,0:T(8,128)(2,1)S(1)}, u32[]{:S(2)}, u32[]{:S(2)}) %all-to-all-start) | async-done | bytes 852000 | tf_op jit(solution)/shard_map/all_to_all | solution.py:345
  41.5 0.0 copy-done.2
  41.5 3.5 %shard_map.104 = (f32[8,1024]{1,0:T(8,128)S(1)}, f32[2,1024,1024]{2,1,0:T(8,128)S(1)}) custom-call(s32[1]{0:T(128)} %bitcast.4.half_s, s32[1,1024]{1,0:T(1,128)S(1)} %copy-done.2, bf16[32,104,128]{2,1,0:T(8,128)(2,1)S(1)} %all-to-all-done.data), custom_call_target="tpu_custom_call" | custom-call | flops 268435456 | bytes 524288 | tf_op jit(solution)/shard_map/pallas_call | solution.py:261
  45.0 1.6 %collective-permute-start.2 = (f32[8,1024]{1,0:T(8,128)S(1)}, f32[8,1024]{1,0:T(8,128)S(1)}, u32[]{:S(2)}, u32[]{:S(2)}) collective-permute-start(f32[8,1024]{1,0:T(8,128)S(1)} %get-tuple-element.11.own), channel_id=1, source_target_pairs={{0,8},{8,0},{16,24},{24,16},{32,40},{40,32},{48,56},{56,48},{1,9},... | collective-permute-start | bytes 98312 | tf_op jit(solution)/shard_map/ppermute | solution.py:354
  46.6 1.3 %shard_map.105.dprobs = f32[2,1024,1024]{2,1,0:T(8,128)S(1)} custom-call(bf16[32,104,128]{2,1,0:T(8,128)(2,1)S(1)} %all-to-all-done.data), custom_call_target="tpu_custom_call" | custom-call | flops 268435456 | bytes 524288 | tf_op jit(solution)/shard_map/pallas_call | solution.py:273
  48.0 1.0 collective-permute-done.2.other
  49.0 3.4 %shard_map.106 = bf16[32,80,128]{2,1,0:T(8,128)(2,1)S(1)} custom-call(bf16[32,104,128]{2,1,0:T(8,128)(2,1)S(1)} %all-to-all-done.data, f32[2,1024,1024]{2,1,0:T(8,128)S(1)} %get-tuple-element.9.scores, f32[2,1024,1024]{2,1,0:T(8,128)S(1)} %shard_map.105.dprobs, f32[8,1024]{1,0:T(8,128)S(1)} %get-tuple-element.11.own, f32[8,1024]{1,0:T(8,128)S(1)} %collective-permute-done.2.other), custom_call_target="tpu_custom_call" | custom-call | flops 805306368 | bytes 1048576 | tf_op jit(solution)/shard_map/pallas_call | solution.py:285
  52.4 22.8 %all_to_all.15.folded = bf16[32,80,128]{2,1,0:T(8,128)(2,1)S(1)} all-to-all(bf16[32,80,128]{2,1,0:T(8,128)(2,1)S(1)} %shard_map.106), channel_id=1, replica_groups=mesh['y'=4,'z'=8,'x_high'=2,'x_low'=2,'core'=2] {'y','z'}, dimensions={0} | all-to-all | bytes 1310720 | tf_op jit(solution)/shard_map/all_to_all | solution.py:357
  75.1 0.0 copy-start
  75.1 0.1 shard_map.107.dk.dk_0
  75.3 0.0 copy-start.1
  75.3 2.4 %collective-permute-start.4 = (bf16[128,1024]{1,0:T(8,128)(2,1)S(1)}, bf16[128,1024]{1,0:T(8,128)(2,1)S(1)}, u32[]{:S(2)}, u32[]{:S(2)}) collective-permute-start(bf16[128,1024]{1,0:T(8,128)(2,1)S(1)} %shard_map.107.dk.dk_0), channel_id=1, source_target_pairs={{0,4},{4,0},{1,5},{5,1},{2,6},{6,2},{3,7},{7,3},{8,12},{12,8},{9,1... | collective-permute-start | bytes 786440 | tf_op jit(solution)/shard_map/ppermute | solution.py:342
  77.7 0.0 collective-permute-start.3
  77.7 5.8 %collective-permute-done.4.dk_2 = bf16[128,1024]{1,0:T(8,128)(2,1)S(1)} collective-permute-done((bf16[128,1024]{1,0:T(8,128)(2,1)S(1)}, bf16[128,1024]{1,0:T(8,128)(2,1)S(1)}, u32[]{:S(2)}, u32[]{:S(2)}) %collective-permute-start.4) | collective-permute-done | bytes 262176 | tf_op jit(solution)/shard_map/ppermute | solution.py:342
  83.4 0.0 collective-permute-start.5
  83.4 0.0 collective-permute-done.3.dk_1
  83.4 1.5 %collective-permute-done.5.dk_3 = bf16[128,1024]{1,0:T(8,128)(2,1)S(1)} collective-permute-done((bf16[128,1024]{1,0:T(8,128)(2,1)S(1)}, bf16[128,1024]{1,0:T(8,128)(2,1)S(1)}, u32[]{:S(2)}, u32[]{:S(2)}) %collective-permute-start.5) | collective-permute-done | bytes 262176 | tf_op jit(solution)/shard_map/ppermute | solution.py:341
  85.0 1.3 %shard_map.109 = bf16[64,4,1024]{2,1,0:T(4,128)(2,1)} custom-call(bf16[256,512]{1,0:T(8,128)(2,1)S(1)} %pad_maximum_fusion.turned, bf16[128,1024]{1,0:T(8,128)(2,1)S(1)} %shard_map.107.dk.dk_0, bf16[128,1024]{1,0:T(8,128)(2,1)S(1)} %collective-permute-done.3.dk_1, bf16[128,1024]{1,0:T(8,128)(2,1)S(1)} %collective-permute-done.4.dk_2, ...), custom_call_target="tpu_custom_call" | custom-call | flops 268435456 | bytes 2097152 | tf_op jit(solution)/shard_map/pallas_call | solution.py:306
  86.2 7.0 %all-to-all-start.2 = ((bf16[64,4,1024]{2,1,0:T(4,128)(2,1)}), bf16[64,4,1024]{2,1,0:T(4,128)(2,1)S(1)}, u32[]{:S(2)}, u32[]{:S(2)}) async-start(bf16[64,4,1024]{2,1,0:T(4,128)(2,1)} %shard_map.109), calls=%async_computation.2 | async-start | bytes 1048576 | tf_op jit(solution)/shard_map/all_to_all | solution.py:362
  93.2 0.0 copy-done
  93.2 0.0 copy-done.1
  93.2 6.0 %shard_map.108 = (bf16[128,1024]{1,0:T(8,128)(2,1)}, bf16[32,1024]{1,0:T(8,128)(2,1)}) custom-call(bf16[128,1024]{1,0:T(8,128)(2,1)} %copy-done.1, bf16[32,80,128]{2,1,0:T(8,128)(2,1)} %copy-done, bf16[1024,1024]{1,0:T(8,128)(2,1)} %w_query.3, bf16[1024,1024]{1,0:T(8,128)(2,1)} %w_key.3, bf16[1024,1024]{1,0:T(8,128)(2,1)} %w_value.3), custom_call_target="tpu_custom_call" | custom-call | flops 603979776 | bytes 8388608 | tf_op jit(solution)/shard_map/pallas_call | solution.py:318
  99.3 10.7 %all-to-all-done.2 = bf16[64,4,1024]{2,1,0:T(4,128)(2,1)S(1)} async-done(((bf16[64,4,1024]{2,1,0:T(4,128)(2,1)}), bf16[64,4,1024]{2,1,0:T(4,128)(2,1)S(1)}, u32[]{:S(2)}, u32[]{:S(2)}) %all-to-all-start.2) | async-done | bytes 524320 | tf_op jit(solution)/shard_map/all_to_all | solution.py:362
  110.0 0.8 convert_reduce_fusion
  (7 shorter events, 0.1 us)
Async XLA Ops:
  0.6 16.1 %copy-start.3 = (bf16[1,128,1024]{2,1,0:T(8,128)(2,1)S(1)}, bf16[1,128,1024]{2,1,0:T(8,128)(2,1)}, u32[]{:S(2)}) copy-start(bf16[1,128,1024]{2,1,0:T(8,128)(2,1)} %param.8) | copy-start | bytes 786436
  5.1 36.4 %copy-start.2 = (s32[1,1024]{1,0:T(1,128)S(1)}, s32[1,1024]{1,0:T(1,128)}, u32[]{:S(2)}) copy-start(s32[1,1024]{1,0:T(1,128)} %vis.1) | copy-start | bytes 12292
  5.1 36.4 %all-to-all-start = ((bf16[32,104,128]{2,1,0:T(8,128)(2,1)}), bf16[32,104,128]{2,1,0:T(8,128)(2,1)S(1)}, u32[]{:S(2)}, u32[]{:S(2)}) async-start(bf16[32,104,128]{2,1,0:T(8,128)(2,1)} %shard_map.103), calls=%async_computation | async-start | bytes 1703936 | tf_op jit(solution)/shard_map/all_to_all | solution.py:345
  17.6 1.4 %collective-permute-start = (bf16[2,256,128]{2,1,0:T(8,128)(2,1)S(1)}, bf16[2,256,128]{2,1,0:T(8,128)(2,1)S(1)}, u32[]{:S(2)}, u32[]{:S(2)}) collective-permute-start(bf16[2,256,128]{2,1,0:T(8,128)(2,1)S(1)} %pad_maximum_fusion.1), channel_id=1, source_target_pairs={{0,1},{1,0},{2,3},{3,2},{4,5},{5,4},{6,7},{7,6},{8,9},{9,8},{10,11... | collective-permute-start | bytes 393224 | tf_op jit(solution)/shard_map/ppermute | solution.py:341
  19.1 7.1 %collective-permute-start.1 = (bf16[2,256,128]{2,1,0:T(8,128)(2,1)S(1)}, bf16[2,256,128]{2,1,0:T(8,128)(2,1)S(1)}, u32[]{:S(2)}, u32[]{:S(2)}) collective-permute-start(bf16[2,256,128]{2,1,0:T(8,128)(2,1)S(1)} %pad_maximum_fusion.2), channel_id=1, source_target_pairs={{0,4},{4,0},{1,5},{5,1},{2,6},{6,2},{3,7},{7,3},{8,12},{12,8},{9,1... | collective-permute-start | bytes 393224 | tf_op jit(solution)/shard_map/ppermute | solution.py:342
  45.0 4.0 %collective-permute-start.2 = (f32[8,1024]{1,0:T(8,128)S(1)}, f32[8,1024]{1,0:T(8,128)S(1)}, u32[]{:S(2)}, u32[]{:S(2)}) collective-permute-start(f32[8,1024]{1,0:T(8,128)S(1)} %get-tuple-element.11.own), channel_id=1, source_target_pairs={{0,8},{8,0},{16,24},{24,16},{32,40},{40,32},{48,56},{56,48},{1,9},... | collective-permute-start | bytes 98312 | tf_op jit(solution)/shard_map/ppermute | solution.py:354
  75.1 18.1 %copy-start = (bf16[32,80,128]{2,1,0:T(8,128)(2,1)}, bf16[32,80,128]{2,1,0:T(8,128)(2,1)S(1)}, u32[]{:S(2)}) copy-start(bf16[32,80,128]{2,1,0:T(8,128)(2,1)S(1)} %all_to_all.15.folded) | copy-start | bytes 1966084
  75.3 18.0 %copy-start.1 = (bf16[128,1024]{1,0:T(8,128)(2,1)}, bf16[128,1024]{1,0:T(8,128)(2,1)S(1)}, u32[]{:S(2)}) copy-start(bf16[128,1024]{1,0:T(8,128)(2,1)S(1)} %shard_map.107.dk.dk_0) | copy-start | bytes 786436
  75.3 8.1 %collective-permute-start.4 = (bf16[128,1024]{1,0:T(8,128)(2,1)S(1)}, bf16[128,1024]{1,0:T(8,128)(2,1)S(1)}, u32[]{:S(2)}, u32[]{:S(2)}) collective-permute-start(bf16[128,1024]{1,0:T(8,128)(2,1)S(1)} %shard_map.107.dk.dk_0), channel_id=1, source_target_pairs={{0,4},{4,0},{1,5},{5,1},{2,6},{6,2},{3,7},{7,3},{8,12},{12,8},{9,1... | collective-permute-start | bytes 786440 | tf_op jit(solution)/shard_map/ppermute | solution.py:342
  77.7 5.8 %collective-permute-start.3 = (bf16[128,1024]{1,0:T(8,128)(2,1)S(1)}, bf16[128,1024]{1,0:T(8,128)(2,1)S(1)}, u32[]{:S(2)}, u32[]{:S(2)}) collective-permute-start(bf16[128,1024]{1,0:T(8,128)(2,1)S(1)} %shard_map.107.dk.dk_0), channel_id=1, source_target_pairs={{0,1},{1,0},{2,3},{3,2},{4,5},{5,4},{6,7},{7,6},{8,9},{9,8},{10,11... | collective-permute-start | bytes 786440 | tf_op jit(solution)/shard_map/ppermute | solution.py:341
  83.4 1.5 %collective-permute-start.5 = (bf16[128,1024]{1,0:T(8,128)(2,1)S(1)}, bf16[128,1024]{1,0:T(8,128)(2,1)S(1)}, u32[]{:S(2)}, u32[]{:S(2)}) collective-permute-start(bf16[128,1024]{1,0:T(8,128)(2,1)S(1)} %collective-permute-done.4.dk_2), channel_id=1, source_target_pairs={{0,1},{1,0},{2,3},{3,2},{4,5},{5,4},{6,7},{7,6},{8,9},{9,8},{10,11... | collective-permute-start | bytes 786440 | tf_op jit(solution)/shard_map/ppermute | solution.py:341
  86.2 23.8 %all-to-all-start.2 = ((bf16[64,4,1024]{2,1,0:T(4,128)(2,1)}), bf16[64,4,1024]{2,1,0:T(4,128)(2,1)S(1)}, u32[]{:S(2)}, u32[]{:S(2)}) async-start(bf16[64,4,1024]{2,1,0:T(4,128)(2,1)} %shard_map.109), calls=%async_computation.2 | async-start | bytes 1048576 | tf_op jit(solution)/shard_map/all_to_all | solution.py:362

commit v7 on v6

--- a/solution.py
+++ b/solution.py
@@ -121,8 +121,13 @@
     out[2:8, :] = jnp.zeros((6, 1024), F32)
 
 
-def dprobs_kernel(data, out, g_low, g_high, delta_ref):
+def dprobs_kernel(data, out, q_low, q_high, g_low, g_high, k_t, delta_ref):
+    unfold(data[:, 64:80, :], q_low, q_high)
     unfold(data[:, 80:96, :], g_low, g_high)
+    for chunk in range(CHUNKS):
+        k = data[chunk * SRC_CHUNK : (chunk + 1) * SRC_CHUNK, 0:32, :].reshape(ROWS, 128)
+        turned = k.T
+        k_t[chunk] = jnp.concatenate([turned[0:64], turned[64:128]], axis=1)
     lane = lax.broadcasted_iota(jnp.int32, (1, 128), 1)
     for block in range(8):
         joined = jnp.zeros((1, 128), F32)
@@ -142,13 +147,7 @@
             out[1, place, lanes] = dot_nt(v, g_high[lanes, :]) - delta_ref[:, lanes]
 
 
-def grad_kernel(data, scores, dprobs, own, other, out, q_low, q_high, g_low, g_high, k_t, dk_acc, dv_acc):
-    unfold(data[:, 64:80, :], q_low, q_high)
-    unfold(data[:, 80:96, :], g_low, g_high)
-    for chunk in range(CHUNKS):
-        k = data[chunk * SRC_CHUNK : (chunk + 1) * SRC_CHUNK, 0:32, :].reshape(ROWS, 128)
-        turned = k.T
-        k_t[chunk] = jnp.concatenate([turned[0:64], turned[64:128]], axis=1)
+def grad_kernel(scores, dprobs, q_low, q_high, g_low, g_high, k_t, own, other, out, dk_acc, dv_acc):
     dk_acc[...] = jnp.zeros_like(dk_acc)
     dv_acc[...] = jnp.zeros_like(dv_acc)
     top = jnp.maximum(own[0:1, :], other[0:1, :])
@@ -272,30 +271,27 @@
 def run_dprobs(data):
     return call(
         dprobs_kernel,
-        shape((2, 1024, 1024), F32),
+        (shape((2, 1024, 1024), F32),)
+        + (shape((1024, 128), BF),) * 4
+        + (shape((CHUNKS, DH, SRC_CHUNK * 64), BF),),
         flops=2 * 1024 * 2048 * 64,
         nbytes=1 << 19,
         in_specs=[VMEM],
-        out_specs=VMEM,
-        scratch_shapes=[pltpu.VMEM((1024, 128), BF)] * 2 + [pltpu.VMEM((1, 1024), F32)],
+        out_specs=(VMEM,) * 6,
+        scratch_shapes=[pltpu.VMEM((1, 1024), F32)],
     )(data)
 
 
-def run_grad(data, scores, dprobs, stats, other):
+def run_grad(scores, local, stats, other):
     return call(
         grad_kernel,
         shape((32, 80, 128), BF),
         flops=6 * 1024 * 2048 * 64,
         nbytes=1 << 20,
-        in_specs=[VMEM] * 5,
+        in_specs=[VMEM] * 9,
         out_specs=VMEM,
-        scratch_shapes=[pltpu.VMEM((1024, 128), BF)] * 4
-        + [
-            pltpu.VMEM((CHUNKS, DH, SRC_CHUNK * 64), BF),
-            pltpu.VMEM((1024, 128), F32),
-            pltpu.VMEM((1024, 128), F32),
-        ],
-    )(data, scores, dprobs, stats, other)
+        scratch_shapes=[pltpu.VMEM((1024, 128), F32)] * 2,
+    )(scores, *local, stats, other)
 
 
 def run_join(back):
@@ -352,8 +348,7 @@
     stats, scores = run_stats(half, visible, data)
     stats, turned = lax.optimization_barrier((stats, turned))
     other = lax.ppermute(stats, "z", [(i, i ^ 1) for i in range(8)])
-    dprobs = run_dprobs(data)
-    back = run_grad(data, scores, dprobs, stats, other)
+    back = run_grad(scores, run_dprobs(data), stats, other)
     back = lax.all_to_all(back, ("y", "z"), 0, 0, tiled=True)
 
     dk = run_join(back)

time: 112 us -> 112 us (level)
  no operation moved by 1% of the time
where the time goes in v7:
time: 112 us; the launch traced here: 111 us
  waiting for transfers between devices  40.5 us (36%)
  starting transfers between devices  24.9 us (22%)
  blocking collectives  22.8 us (20%)
  Pallas kernels  19.9 us (18%)
    all_to_all x1, blocking collectives, on_device(): back = lax.all_to_all(back, ('y', 'z'), 0, 0, tiled=True)  22.8 us
    all_to_all x1, waiting for transfers between devices, on_device(): data = lax.all_to_all(data, ('y', 'z'), 0, 0, tiled=True)  15.2 us
    all_to_all x1, starting transfers between devices, on_device(): data = lax.all_to_all(data, ('y', 'z'), 0, 0, tiled=True)  11.6 us
    all_to_all x1, waiting for transfers between devices, on_device(): part = lax.all_to_all(part, ('y', 'z', 'x_low'), 0, 0, tiled=True)  10.7 us
    ppermute x2, waiting for transfers between devices, on_device(): over_x = lambda v: lax.ppermute(v, 'x_high', [(0, 1), (1, 0)])  10.7 us
    all_to_all x1, starting transfers between devices, on_device(): part = lax.all_to_all(part, ('y', 'z', 'x_low'), 0, 0, tiled=True)  7.01 us
    pallas_call x1, Pallas kernels, run_post(): call(post_kernel, (shape((128, 1024), BF), shape((32, 1024), BF)), limit=...  6.04 us
    ppermute x2, starting transfers between devices, on_device(): over_x = lambda v: lax.ppermute(v, 'x_high', [(0, 1), (1, 0)])  4.6 us
  transfers between devices with their start and end apart: 8, of which 7 were waited for; matrix products, arithmetic and copies ran while one was open for 1% of the time, Pallas kernels for 7%

profile of v7, /device:TPU:2, one launch (start us, length us, event | category | flops | bytes accessed | tf_op | source)
XLA Modules:
  0.0 110.7 jit_solution(1838248741853569811)
XLA Ops:
  0.6 0.0 copy-start.3
  0.6 4.5 %shard_map.103 = bf16[32,104,128]{2,1,0:T(8,128)(2,1)} custom-call(bf16[128,1024]{1,0:T(8,128)(2,1)} %bitcast.21, bf16[32,1024]{1,0:T(8,128)(2,1)} %bitcast.22, bf16[32,1024]{1,0:T(8,128)(2,1)} %bitcast.23, bf16[32,1024]{1,0:T(8,128)(2,1)} %bitcast.24, bf16[1024,1024]{1,0:T(8,128)(2,1)} %w_query.3, bf16[1024,1024]{1,0:T(8,128)(2,1)} %w_key.3, ...), custom_call_target="tpu_custom_call" | custom-call | flops 603979776 | bytes 8388608 | tf_op jit(solution)/shard_map/pallas_call | solution.py:247
  5.1 0.0 copy-start.2
  5.1 11.6 %all-to-all-start = ((bf16[32,104,128]{2,1,0:T(8,128)(2,1)}), bf16[32,104,128]{2,1,0:T(8,128)(2,1)S(1)}, u32[]{:S(2)}, u32[]{:S(2)}) async-start(bf16[32,104,128]{2,1,0:T(8,128)(2,1)} %shard_map.103), calls=%async_computation | async-start | bytes 1703936 | tf_op jit(solution)/shard_map/all_to_all | solution.py:341
  16.7 0.0 copy-done.3
  16.8 0.8 fusion.2
  17.6 0.1 collective-permute-start
  17.7 1.3 %collective-permute-done = bf16[2,256,128]{2,1,0:T(8,128)(2,1)S(1)} collective-permute-done((bf16[2,256,128]{2,1,0:T(8,128)(2,1)S(1)}, bf16[2,256,128]{2,1,0:T(8,128)(2,1)S(1)}, u32[]{:S(2)}, u32[]{:S(2)}) %collective-permute-start) | collective-permute-done | bytes 131104 | tf_op jit(solution)/shard_map/ppermute | solution.py:337
  19.1 2.2 %collective-permute-start.1 = (bf16[2,256,128]{2,1,0:T(8,128)(2,1)S(1)}, bf16[2,256,128]{2,1,0:T(8,128)(2,1)S(1)}, u32[]{:S(2)}, u32[]{:S(2)}) collective-permute-start(bf16[2,256,128]{2,1,0:T(8,128)(2,1)S(1)} %pad_maximum_fusion.2), channel_id=1, source_target_pairs={{0,4},{4,0},{1,5},{5,1},{2,6},{6,2},{3,7},{7,3},{8,12},{12,8},{9,1... | collective-permute-start | bytes 393224 | tf_op jit(solution)/shard_map/ppermute | solution.py:338
  21.3 4.9 %collective-permute-done.1 = bf16[2,256,128]{2,1,0:T(8,128)(2,1)S(1)} collective-permute-done((bf16[2,256,128]{2,1,0:T(8,128)(2,1)S(1)}, bf16[2,256,128]{2,1,0:T(8,128)(2,1)S(1)}, u32[]{:S(2)}, u32[]{:S(2)}) %collective-permute-start.1) | collective-permute-done | bytes 131104 | tf_op jit(solution)/shard_map/ppermute | solution.py:338
  26.3 15.2 %all-to-all-done.data = bf16[32,104,128]{2,1,0:T(8,128)(2,1)S(1)} async-done(((bf16[32,104,128]{2,1,0:T(8,128)(2,1)}), bf16[32,104,128]{2,1,0:T(8,128)(2,1)S(1)}, u32[]{:S(2)}, u32[]{:S(2)}) %all-to-all-start) | async-done | bytes 852000 | tf_op jit(solution)/shard_map/all_to_all | solution.py:341
  41.5 0.0 copy-done.2
  41.5 3.5 %shard_map.104 = (f32[8,1024]{1,0:T(8,128)S(1)}, f32[2,1024,1024]{2,1,0:T(8,128)S(1)}) custom-call(s32[1]{0:T(128)} %bitcast.half_s, s32[1,1024]{1,0:T(1,128)S(1)} %copy-done.2, bf16[32,104,128]{2,1,0:T(8,128)(2,1)S(1)} %all-to-all-done.data), custom_call_target="tpu_custom_call" | custom-call | flops 268435456 | bytes 524288 | tf_op jit(solution)/shard_map/pallas_call | solution.py:260
  45.0 1.6 %collective-permute-start.2 = (f32[8,1024]{1,0:T(8,128)S(1)}, f32[8,1024]{1,0:T(8,128)S(1)}, u32[]{:S(2)}, u32[]{:S(2)}) collective-permute-start(f32[8,1024]{1,0:T(8,128)S(1)} %get-tuple-element.23.own), channel_id=1, source_target_pairs={{0,8},{8,0},{16,24},{24,16},{32,40},{40,32},{48,56},{56,48},{1,9},... | collective-permute-start | bytes 98312 | tf_op jit(solution)/shard_map/ppermute | solution.py:350
  46.6 1.4 %shard_map.105 = (f32[2,1024,1024]{2,1,0:T(8,128)S(1)}, bf16[1024,128]{1,0:T(8,128)(2,1)S(1)}, bf16[1024,128]{1,0:T(8,128)(2,1)S(1)}, bf16[1024,128]{1,0:T(8,128...) custom-call(bf16[32,104,128]{2,1,0:T(8,128)(2,1)S(1)} %all-to-all-done.data), custom_call_target="tpu_custom_call" | custom-call | flops 268435456 | bytes 524288 | tf_op jit(solution)/shard_map/pallas_call | solution.py:272
  47.9 1.0 collective-permute-done.2.other
  49.0 3.2 %shard_map.106 = bf16[32,80,128]{2,1,0:T(8,128)(2,1)S(1)} custom-call(f32[2,1024,1024]{2,1,0:T(8,128)S(1)} %get-tuple-element.15.scores, f32[2,1024,1024]{2,1,0:T(8,128)S(1)} %get-tuple-element.16.dprobs, bf16[1024,128]{1,0:T(8,128)(2,1)S(1)} %get-tuple-element.17.q_low, bf16[1024,128]{1,0:T(8,128)(2,1)S(1)} %get-tuple-element.18.q_high, ...), custom_call_target="tpu_custom_call" | custom-call | flops 805306368 | bytes 1048576 | tf_op jit(solution)/shard_map/pallas_call | solution.py:286
  52.2 22.8 %all_to_all.15.folded = bf16[32,80,128]{2,1,0:T(8,128)(2,1)S(1)} all-to-all(bf16[32,80,128]{2,1,0:T(8,128)(2,1)S(1)} %shard_map.106), channel_id=1, replica_groups=mesh['y'=4,'z'=8,'x_high'=2,'x_low'=2,'core'=2] {'y','z'}, dimensions={0} | all-to-all | bytes 1310720 | tf_op jit(solution)/shard_map/all_to_all | solution.py:352
  75.0 0.0 copy-start
  75.0 0.1 shard_map.107.dk.dk_0
  75.1 0.0 copy-start.1
  75.1 2.4 %collective-permute-start.4 = (bf16[128,1024]{1,0:T(8,128)(2,1)S(1)}, bf16[128,1024]{1,0:T(8,128)(2,1)S(1)}, u32[]{:S(2)}, u32[]{:S(2)}) collective-permute-start(bf16[128,1024]{1,0:T(8,128)(2,1)S(1)} %shard_map.107.dk.dk_0), channel_id=1, source_target_pairs={{0,4},{4,0},{1,5},{5,1},{2,6},{6,2},{3,7},{7,3},{8,12},{12,8},{9,1... | collective-permute-start | bytes 786440 | tf_op jit(solution)/shard_map/ppermute | solution.py:338
  77.5 0.0 collective-permute-start.3
  77.5 5.8 %collective-permute-done.4.dk_2 = bf16[128,1024]{1,0:T(8,128)(2,1)S(1)} collective-permute-done((bf16[128,1024]{1,0:T(8,128)(2,1)S(1)}, bf16[128,1024]{1,0:T(8,128)(2,1)S(1)}, u32[]{:S(2)}, u32[]{:S(2)}) %collective-permute-start.4) | collective-permute-done | bytes 262176 | tf_op jit(solution)/shard_map/ppermute | solution.py:338
  83.3 0.0 collective-permute-start.5
  83.3 0.0 collective-permute-done.3.dk_1
  83.3 1.5 %collective-permute-done.5.dk_3 = bf16[128,1024]{1,0:T(8,128)(2,1)S(1)} collective-permute-done((bf16[128,1024]{1,0:T(8,128)(2,1)S(1)}, bf16[128,1024]{1,0:T(8,128)(2,1)S(1)}, u32[]{:S(2)}, u32[]{:S(2)}) %collective-permute-start.5) | collective-permute-done | bytes 262176 | tf_op jit(solution)/shard_map/ppermute | solution.py:337
  84.8 1.2 %shard_map.109 = bf16[64,4,1024]{2,1,0:T(4,128)(2,1)} custom-call(bf16[256,512]{1,0:T(8,128)(2,1)S(1)} %pad_maximum_fusion.turned, bf16[128,1024]{1,0:T(8,128)(2,1)S(1)} %shard_map.107.dk.dk_0, bf16[128,1024]{1,0:T(8,128)(2,1)S(1)} %collective-permute-done.3.dk_1, bf16[128,1024]{1,0:T(8,128)(2,1)S(1)} %collective-permute-done.4.dk_2, ...), custom_call_target="tpu_custom_call" | custom-call | flops 268435456 | bytes 2097152 | tf_op jit(solution)/shard_map/pallas_call | solution.py:302
  86.1 7.0 %all-to-all-start.2 = ((bf16[64,4,1024]{2,1,0:T(4,128)(2,1)}), bf16[64,4,1024]{2,1,0:T(4,128)(2,1)S(1)}, u32[]{:S(2)}, u32[]{:S(2)}) async-start(bf16[64,4,1024]{2,1,0:T(4,128)(2,1)} %shard_map.109), calls=%async_computation.2 | async-start | bytes 1048576 | tf_op jit(solution)/shard_map/all_to_all | solution.py:357
  93.1 0.0 copy-done
  93.1 0.0 copy-done.1
  93.1 6.0 %shard_map.108 = (bf16[128,1024]{1,0:T(8,128)(2,1)}, bf16[32,1024]{1,0:T(8,128)(2,1)}) custom-call(bf16[128,1024]{1,0:T(8,128)(2,1)} %copy-done.1, bf16[32,80,128]{2,1,0:T(8,128)(2,1)} %copy-done, bf16[1024,1024]{1,0:T(8,128)(2,1)} %w_query.3, bf16[1024,1024]{1,0:T(8,128)(2,1)} %w_key.3, bf16[1024,1024]{1,0:T(8,128)(2,1)} %w_value.3), custom_call_target="tpu_custom_call" | custom-call | flops 603979776 | bytes 8388608 | tf_op jit(solution)/shard_map/pallas_call | solution.py:314
  99.1 10.7 %all-to-all-done.2 = bf16[64,4,1024]{2,1,0:T(4,128)(2,1)S(1)} async-done(((bf16[64,4,1024]{2,1,0:T(4,128)(2,1)}), bf16[64,4,1024]{2,1,0:T(4,128)(2,1)S(1)}, u32[]{:S(2)}, u32[]{:S(2)}) %all-to-all-start.2) | async-done | bytes 524320 | tf_op jit(solution)/shard_map/all_to_all | solution.py:357
  109.9 0.8 convert_reduce_fusion
  (7 shorter events, 0.1 us)
Async XLA Ops:
  0.6 16.1 %copy-start.3 = (bf16[1,128,1024]{2,1,0:T(8,128)(2,1)S(1)}, bf16[1,128,1024]{2,1,0:T(8,128)(2,1)}, u32[]{:S(2)}) copy-start(bf16[1,128,1024]{2,1,0:T(8,128)(2,1)} %param.8) | copy-start | bytes 786436
  5.1 36.4 %copy-start.2 = (s32[1,1024]{1,0:T(1,128)S(1)}, s32[1,1024]{1,0:T(1,128)}, u32[]{:S(2)}) copy-start(s32[1,1024]{1,0:T(1,128)} %vis.1) | copy-start | bytes 12292
  5.1 36.4 %all-to-all-start = ((bf16[32,104,128]{2,1,0:T(8,128)(2,1)}), bf16[32,104,128]{2,1,0:T(8,128)(2,1)S(1)}, u32[]{:S(2)}, u32[]{:S(2)}) async-start(bf16[32,104,128]{2,1,0:T(8,128)(2,1)} %shard_map.103), calls=%async_computation | async-start | bytes 1703936 | tf_op jit(solution)/shard_map/all_to_all | solution.py:341
  17.6 1.4 %collective-permute-start = (bf16[2,256,128]{2,1,0:T(8,128)(2,1)S(1)}, bf16[2,256,128]{2,1,0:T(8,128)(2,1)S(1)}, u32[]{:S(2)}, u32[]{:S(2)}) collective-permute-start(bf16[2,256,128]{2,1,0:T(8,128)(2,1)S(1)} %pad_maximum_fusion.1), channel_id=1, source_target_pairs={{0,1},{1,0},{2,3},{3,2},{4,5},{5,4},{6,7},{7,6},{8,9},{9,8},{10,11... | collective-permute-start | bytes 393224 | tf_op jit(solution)/shard_map/ppermute | solution.py:337
  19.1 7.1 %collective-permute-start.1 = (bf16[2,256,128]{2,1,0:T(8,128)(2,1)S(1)}, bf16[2,256,128]{2,1,0:T(8,128)(2,1)S(1)}, u32[]{:S(2)}, u32[]{:S(2)}) collective-permute-start(bf16[2,256,128]{2,1,0:T(8,128)(2,1)S(1)} %pad_maximum_fusion.2), channel_id=1, source_target_pairs={{0,4},{4,0},{1,5},{5,1},{2,6},{6,2},{3,7},{7,3},{8,12},{12,8},{9,1... | collective-permute-start | bytes 393224 | tf_op jit(solution)/shard_map/ppermute | solution.py:338
  45.0 4.0 %collective-permute-start.2 = (f32[8,1024]{1,0:T(8,128)S(1)}, f32[8,1024]{1,0:T(8,128)S(1)}, u32[]{:S(2)}, u32[]{:S(2)}) collective-permute-start(f32[8,1024]{1,0:T(8,128)S(1)} %get-tuple-element.23.own), channel_id=1, source_target_pairs={{0,8},{8,0},{16,24},{24,16},{32,40},{40,32},{48,56},{56,48},{1,9},... | collective-permute-start | bytes 98312 | tf_op jit(solution)/shard_map/ppermute | solution.py:350
  75.0 18.1 %copy-start = (bf16[32,80,128]{2,1,0:T(8,128)(2,1)}, bf16[32,80,128]{2,1,0:T(8,128)(2,1)S(1)}, u32[]{:S(2)}) copy-start(bf16[32,80,128]{2,1,0:T(8,128)(2,1)S(1)} %all_to_all.15.folded) | copy-start | bytes 1966084
  75.1 18.0 %copy-start.1 = (bf16[128,1024]{1,0:T(8,128)(2,1)}, bf16[128,1024]{1,0:T(8,128)(2,1)S(1)}, u32[]{:S(2)}) copy-start(bf16[128,1024]{1,0:T(8,128)(2,1)S(1)} %shard_map.107.dk.dk_0) | copy-start | bytes 786436
  75.1 8.1 %collective-permute-start.4 = (bf16[128,1024]{1,0:T(8,128)(2,1)S(1)}, bf16[128,1024]{1,0:T(8,128)(2,1)S(1)}, u32[]{:S(2)}, u32[]{:S(2)}) collective-permute-start(bf16[128,1024]{1,0:T(8,128)(2,1)S(1)} %shard_map.107.dk.dk_0), channel_id=1, source_target_pairs={{0,4},{4,0},{1,5},{5,1},{2,6},{6,2},{3,7},{7,3},{8,12},{12,8},{9,1... | collective-permute-start | bytes 786440 | tf_op jit(solution)/shard_map/ppermute | solution.py:338
  77.5 5.8 %collective-permute-start.3 = (bf16[128,1024]{1,0:T(8,128)(2,1)S(1)}, bf16[128,1024]{1,0:T(8,128)(2,1)S(1)}, u32[]{:S(2)}, u32[]{:S(2)}) collective-permute-start(bf16[128,1024]{1,0:T(8,128)(2,1)S(1)} %shard_map.107.dk.dk_0), channel_id=1, source_target_pairs={{0,1},{1,0},{2,3},{3,2},{4,5},{5,4},{6,7},{7,6},{8,9},{9,8},{10,11... | collective-permute-start | bytes 786440 | tf_op jit(solution)/shard_map/ppermute | solution.py:337
  83.3 1.5 %collective-permute-start.5 = (bf16[128,1024]{1,0:T(8,128)(2,1)S(1)}, bf16[128,1024]{1,0:T(8,128)(2,1)S(1)}, u32[]{:S(2)}, u32[]{:S(2)}) collective-permute-start(bf16[128,1024]{1,0:T(8,128)(2,1)S(1)} %collective-permute-done.4.dk_2), channel_id=1, source_target_pairs={{0,1},{1,0},{2,3},{3,2},{4,5},{5,4},{6,7},{7,6},{8,9},{9,8},{10,11... | collective-permute-start | bytes 786440 | tf_op jit(solution)/shard_map/ppermute | solution.py:337
  86.1 23.8 %all-to-all-start.2 = ((bf16[64,4,1024]{2,1,0:T(4,128)(2,1)}), bf16[64,4,1024]{2,1,0:T(4,128)(2,1)S(1)}, u32[]{:S(2)}, u32[]{:S(2)}) async-start(bf16[64,4,1024]{2,1,0:T(4,128)(2,1)} %shard_map.109), calls=%async_computation.2 | async-start | bytes 1048576 | tf_op jit(solution)/shard_map/all_to_all | solution.py:357

commit v8 on v7

--- a/solution.py
+++ b/solution.py
@@ -148,8 +148,6 @@
 
 
 def grad_kernel(scores, dprobs, q_low, q_high, g_low, g_high, k_t, own, other, out, dk_acc, dv_acc):
-    dk_acc[...] = jnp.zeros_like(dk_acc)
-    dv_acc[...] = jnp.zeros_like(dv_acc)
     top = jnp.maximum(own[0:1, :], other[0:1, :])
     total = own[1:2, :] * jnp.exp2((own[0:1, :] - top) * C) + other[1:2, :] * jnp.exp2((other[0:1, :] - top) * C)
     lse = top + jnp.log2(total) * (1.0 / C)
@@ -164,8 +162,10 @@
             p_high = jnp.exp2((scores[1, place, lanes] - lse_t) * C)
             ds_low = (p_low * dprobs[0, place, lanes]).astype(BF)
             ds_high = (p_high * dprobs[1, place, lanes]).astype(BF)
-            dv_acc[place, :] += dot(p_low.astype(BF), gl) + dot(p_high.astype(BF), gh)
-            dk_acc[place, :] += dot(ds_low, ql) + dot(ds_high, qh)
+            dv = dot(p_low.astype(BF), gl) + dot(p_high.astype(BF), gh)
+            dk = dot(ds_low, ql) + dot(ds_high, qh)
+            dv_acc[place, :] = dv_acc[place, :] + dv if tile else dv
+            dk_acc[place, :] = dk_acc[place, :] + dk if tile else dk
             return dq + dot(k_t[chunk], jnp.concatenate([ds_low, ds_high], axis=0))
 
         dq = all_chunks(step, jnp.zeros((DH, LAT_TILE), F32))

time: 112 us -> 112 us (level)
  no operation moved by 1% of the time
where the time goes in v8:
time: 112 us; the launch traced here: 111 us
  waiting for transfers between devices  40.5 us (36%)
  starting transfers between devices  24.9 us (22%)
  blocking collectives  22.8 us (20%)
  Pallas kernels  19.9 us (18%)
    all_to_all x1, blocking collectives, on_device(): back = lax.all_to_all(back, ('y', 'z'), 0, 0, tiled=True)  22.8 us
    all_to_all x1, waiting for transfers between devices, on_device(): data = lax.all_to_all(data, ('y', 'z'), 0, 0, tiled=True)  15.2 us
    all_to_all x1, starting transfers between devices, on_device(): data = lax.all_to_all(data, ('y', 'z'), 0, 0, tiled=True)  11.6 us
    all_to_all x1, waiting for transfers between devices, on_device(): part = lax.all_to_all(part, ('y', 'z', 'x_low'), 0, 0, tiled=True)  10.7 us
    ppermute x2, waiting for transfers between devices, on_device(): over_x = lambda v: lax.ppermute(v, 'x_high', [(0, 1), (1, 0)])  10.7 us
    all_to_all x1, starting transfers between devices, on_device(): part = lax.all_to_all(part, ('y', 'z', 'x_low'), 0, 0, tiled=True)  7.01 us
    pallas_call x1, Pallas kernels, run_post(): call(post_kernel, (shape((128, 1024), BF), shape((32, 1024), BF)), limit=...  6.04 us
    ppermute x2, starting transfers between devices, on_device(): over_x = lambda v: lax.ppermute(v, 'x_high', [(0, 1), (1, 0)])  4.6 us
  transfers between devices with their start and end apart: 8, of which 7 were waited for; matrix products, arithmetic and copies ran while one was open for 1% of the time, Pallas kernels for 7%

profile of v8, /device:TPU:2, one launch (start us, length us, event | category | flops | bytes accessed | tf_op | source)
XLA Modules:
  0.0 110.7 jit_solution(1838248741853569811)
XLA Ops:
  0.6 0.0 copy-start.3
  0.6 4.5 %shard_map.103 = bf16[32,104,128]{2,1,0:T(8,128)(2,1)} custom-call(bf16[128,1024]{1,0:T(8,128)(2,1)} %bitcast.21, bf16[32,1024]{1,0:T(8,128)(2,1)} %bitcast.22, bf16[32,1024]{1,0:T(8,128)(2,1)} %bitcast.23, bf16[32,1024]{1,0:T(8,128)(2,1)} %bitcast.24, bf16[1024,1024]{1,0:T(8,128)(2,1)} %w_query.3, bf16[1024,1024]{1,0:T(8,128)(2,1)} %w_key.3, ...), custom_call_target="tpu_custom_call" | custom-call | flops 603979776 | bytes 8388608 | tf_op jit(solution)/shard_map/pallas_call | solution.py:247
  5.1 0.0 copy-start.2
  5.1 11.6 %all-to-all-start = ((bf16[32,104,128]{2,1,0:T(8,128)(2,1)}), bf16[32,104,128]{2,1,0:T(8,128)(2,1)S(1)}, u32[]{:S(2)}, u32[]{:S(2)}) async-start(bf16[32,104,128]{2,1,0:T(8,128)(2,1)} %shard_map.103), calls=%async_computation | async-start | bytes 1703936 | tf_op jit(solution)/shard_map/all_to_all | solution.py:341
  16.7 0.0 copy-done.3
  16.8 0.8 fusion.2
  17.6 0.1 collective-permute-start
  17.7 1.3 %collective-permute-done = bf16[2,256,128]{2,1,0:T(8,128)(2,1)S(1)} collective-permute-done((bf16[2,256,128]{2,1,0:T(8,128)(2,1)S(1)}, bf16[2,256,128]{2,1,0:T(8,128)(2,1)S(1)}, u32[]{:S(2)}, u32[]{:S(2)}) %collective-permute-start) | collective-permute-done | bytes 131104 | tf_op jit(solution)/shard_map/ppermute | solution.py:337
  19.1 2.2 %collective-permute-start.1 = (bf16[2,256,128]{2,1,0:T(8,128)(2,1)S(1)}, bf16[2,256,128]{2,1,0:T(8,128)(2,1)S(1)}, u32[]{:S(2)}, u32[]{:S(2)}) collective-permute-start(bf16[2,256,128]{2,1,0:T(8,128)(2,1)S(1)} %pad_maximum_fusion.2), channel_id=1, source_target_pairs={{0,4},{4,0},{1,5},{5,1},{2,6},{6,2},{3,7},{7,3},{8,12},{12,8},{9,1... | collective-permute-start | bytes 393224 | tf_op jit(solution)/shard_map/ppermute | solution.py:338
  21.3 4.9 %collective-permute-done.1 = bf16[2,256,128]{2,1,0:T(8,128)(2,1)S(1)} collective-permute-done((bf16[2,256,128]{2,1,0:T(8,128)(2,1)S(1)}, bf16[2,256,128]{2,1,0:T(8,128)(2,1)S(1)}, u32[]{:S(2)}, u32[]{:S(2)}) %collective-permute-start.1) | collective-permute-done | bytes 131104 | tf_op jit(solution)/shard_map/ppermute | solution.py:338
  26.3 15.2 %all-to-all-done.data = bf16[32,104,128]{2,1,0:T(8,128)(2,1)S(1)} async-done(((bf16[32,104,128]{2,1,0:T(8,128)(2,1)}), bf16[32,104,128]{2,1,0:T(8,128)(2,1)S(1)}, u32[]{:S(2)}, u32[]{:S(2)}) %all-to-all-start) | async-done | bytes 852000 | tf_op jit(solution)/shard_map/all_to_all | solution.py:341
  41.5 0.0 copy-done.2
  41.5 3.5 %shard_map.104 = (f32[8,1024]{1,0:T(8,128)S(1)}, f32[2,1024,1024]{2,1,0:T(8,128)S(1)}) custom-call(s32[1]{0:T(128)} %bitcast.half_s, s32[1,1024]{1,0:T(1,128)S(1)} %copy-done.2, bf16[32,104,128]{2,1,0:T(8,128)(2,1)S(1)} %all-to-all-done.data), custom_call_target="tpu_custom_call" | custom-call | flops 268435456 | bytes 524288 | tf_op jit(solution)/shard_map/pallas_call | solution.py:260
  45.0 1.6 %collective-permute-start.2 = (f32[8,1024]{1,0:T(8,128)S(1)}, f32[8,1024]{1,0:T(8,128)S(1)}, u32[]{:S(2)}, u32[]{:S(2)}) collective-permute-start(f32[8,1024]{1,0:T(8,128)S(1)} %get-tuple-element.23.own), channel_id=1, source_target_pairs={{0,8},{8,0},{16,24},{24,16},{32,40},{40,32},{48,56},{56,48},{1,9},... | collective-permute-start | bytes 98312 | tf_op jit(solution)/shard_map/ppermute | solution.py:350
  46.6 1.4 %shard_map.105 = (f32[2,1024,1024]{2,1,0:T(8,128)S(1)}, bf16[1024,128]{1,0:T(8,128)(2,1)S(1)}, bf16[1024,128]{1,0:T(8,128)(2,1)S(1)}, bf16[1024,128]{1,0:T(8,128...) custom-call(bf16[32,104,128]{2,1,0:T(8,128)(2,1)S(1)} %all-to-all-done.data), custom_call_target="tpu_custom_call" | custom-call | flops 268435456 | bytes 524288 | tf_op jit(solution)/shard_map/pallas_call | solution.py:272
  47.9 1.0 collective-permute-done.2.other
  49.0 3.2 %shard_map.106 = bf16[32,80,128]{2,1,0:T(8,128)(2,1)S(1)} custom-call(f32[2,1024,1024]{2,1,0:T(8,128)S(1)} %get-tuple-element.15.scores, f32[2,1024,1024]{2,1,0:T(8,128)S(1)} %get-tuple-element.16.dprobs, bf16[1024,128]{1,0:T(8,128)(2,1)S(1)} %get-tuple-element.17.q_low, bf16[1024,128]{1,0:T(8,128)(2,1)S(1)} %get-tuple-element.18.q_high, ...), custom_call_target="tpu_custom_call" | custom-call | flops 805306368 | bytes 1048576 | tf_op jit(solution)/shard_map/pallas_call | solution.py:286
  52.2 22.8 %all_to_all.15.folded = bf16[32,80,128]{2,1,0:T(8,128)(2,1)S(1)} all-to-all(bf16[32,80,128]{2,1,0:T(8,128)(2,1)S(1)} %shard_map.106), channel_id=1, replica_groups=mesh['y'=4,'z'=8,'x_high'=2,'x_low'=2,'core'=2] {'y','z'}, dimensions={0} | all-to-all | bytes 1310720 | tf_op jit(solution)/shard_map/all_to_all | solution.py:352
  75.0 0.0 copy-start
  75.0 0.1 shard_map.107.dk.dk_0
  75.1 0.0 copy-start.1
  75.1 2.4 %collective-permute-start.4 = (bf16[128,1024]{1,0:T(8,128)(2,1)S(1)}, bf16[128,1024]{1,0:T(8,128)(2,1)S(1)}, u32[]{:S(2)}, u32[]{:S(2)}) collective-permute-start(bf16[128,1024]{1,0:T(8,128)(2,1)S(1)} %shard_map.107.dk.dk_0), channel_id=1, source_target_pairs={{0,4},{4,0},{1,5},{5,1},{2,6},{6,2},{3,7},{7,3},{8,12},{12,8},{9,1... | collective-permute-start | bytes 786440 | tf_op jit(solution)/shard_map/ppermute | solution.py:338
  77.5 0.0 collective-permute-start.3
  77.5 5.8 %collective-permute-done.4.dk_2 = bf16[128,1024]{1,0:T(8,128)(2,1)S(1)} collective-permute-done((bf16[128,1024]{1,0:T(8,128)(2,1)S(1)}, bf16[128,1024]{1,0:T(8,128)(2,1)S(1)}, u32[]{:S(2)}, u32[]{:S(2)}) %collective-permute-start.4) | collective-permute-done | bytes 262176 | tf_op jit(solution)/shard_map/ppermute | solution.py:338
  83.3 0.0 collective-permute-start.5
  83.3 0.0 collective-permute-done.3.dk_1
  83.3 1.5 %collective-permute-done.5.dk_3 = bf16[128,1024]{1,0:T(8,128)(2,1)S(1)} collective-permute-done((bf16[128,1024]{1,0:T(8,128)(2,1)S(1)}, bf16[128,1024]{1,0:T(8,128)(2,1)S(1)}, u32[]{:S(2)}, u32[]{:S(2)}) %collective-permute-start.5) | collective-permute-done | bytes 262176 | tf_op jit(solution)/shard_map/ppermute | solution.py:337
  84.8 1.2 %shard_map.109 = bf16[64,4,1024]{2,1,0:T(4,128)(2,1)} custom-call(bf16[256,512]{1,0:T(8,128)(2,1)S(1)} %pad_maximum_fusion.turned, bf16[128,1024]{1,0:T(8,128)(2,1)S(1)} %shard_map.107.dk.dk_0, bf16[128,1024]{1,0:T(8,128)(2,1)S(1)} %collective-permute-done.3.dk_1, bf16[128,1024]{1,0:T(8,128)(2,1)S(1)} %collective-permute-done.4.dk_2, ...), custom_call_target="tpu_custom_call" | custom-call | flops 268435456 | bytes 2097152 | tf_op jit(solution)/shard_map/pallas_call | solution.py:302
  86.1 7.0 %all-to-all-start.2 = ((bf16[64,4,1024]{2,1,0:T(4,128)(2,1)}), bf16[64,4,1024]{2,1,0:T(4,128)(2,1)S(1)}, u32[]{:S(2)}, u32[]{:S(2)}) async-start(bf16[64,4,1024]{2,1,0:T(4,128)(2,1)} %shard_map.109), calls=%async_computation.2 | async-start | bytes 1048576 | tf_op jit(solution)/shard_map/all_to_all | solution.py:357
  93.1 0.0 copy-done
  93.1 0.0 copy-done.1
  93.1 6.0 %shard_map.108 = (bf16[128,1024]{1,0:T(8,128)(2,1)}, bf16[32,1024]{1,0:T(8,128)(2,1)}) custom-call(bf16[128,1024]{1,0:T(8,128)(2,1)} %copy-done.1, bf16[32,80,128]{2,1,0:T(8,128)(2,1)} %copy-done, bf16[1024,1024]{1,0:T(8,128)(2,1)} %w_query.3, bf16[1024,1024]{1,0:T(8,128)(2,1)} %w_key.3, bf16[1024,1024]{1,0:T(8,128)(2,1)} %w_value.3), custom_call_target="tpu_custom_call" | custom-call | flops 603979776 | bytes 8388608 | tf_op jit(solution)/shard_map/pallas_call | solution.py:314
  99.1 10.7 %all-to-all-done.2 = bf16[64,4,1024]{2,1,0:T(4,128)(2,1)S(1)} async-done(((bf16[64,4,1024]{2,1,0:T(4,128)(2,1)}), bf16[64,4,1024]{2,1,0:T(4,128)(2,1)S(1)}, u32[]{:S(2)}, u32[]{:S(2)}) %all-to-all-start.2) | async-done | bytes 524320 | tf_op jit(solution)/shard_map/all_to_all | solution.py:357
  109.9 0.8 convert_reduce_fusion
  (7 shorter events, 0.1 us)
Async XLA Ops:
  0.6 16.1 %copy-start.3 = (bf16[1,128,1024]{2,1,0:T(8,128)(2,1)S(1)}, bf16[1,128,1024]{2,1,0:T(8,128)(2,1)}, u32[]{:S(2)}) copy-start(bf16[1,128,1024]{2,1,0:T(8,128)(2,1)} %param.8) | copy-start | bytes 786436
  5.1 36.4 %copy-start.2 = (s32[1,1024]{1,0:T(1,128)S(1)}, s32[1,1024]{1,0:T(1,128)}, u32[]{:S(2)}) copy-start(s32[1,1024]{1,0:T(1,128)} %vis.1) | copy-start | bytes 12292
  5.1 36.4 %all-to-all-start = ((bf16[32,104,128]{2,1,0:T(8,128)(2,1)}), bf16[32,104,128]{2,1,0:T(8,128)(2,1)S(1)}, u32[]{:S(2)}, u32[]{:S(2)}) async-start(bf16[32,104,128]{2,1,0:T(8,128)(2,1)} %shard_map.103), calls=%async_computation | async-start | bytes 1703936 | tf_op jit(solution)/shard_map/all_to_all | solution.py:341
  17.6 1.4 %collective-permute-start = (bf16[2,256,128]{2,1,0:T(8,128)(2,1)S(1)}, bf16[2,256,128]{2,1,0:T(8,128)(2,1)S(1)}, u32[]{:S(2)}, u32[]{:S(2)}) collective-permute-start(bf16[2,256,128]{2,1,0:T(8,128)(2,1)S(1)} %pad_maximum_fusion.1), channel_id=1, source_target_pairs={{0,1},{1,0},{2,3},{3,2},{4,5},{5,4},{6,7},{7,6},{8,9},{9,8},{10,11... | collective-permute-start | bytes 393224 | tf_op jit(solution)/shard_map/ppermute | solution.py:337
  19.1 7.1 %collective-permute-start.1 = (bf16[2,256,128]{2,1,0:T(8,128)(2,1)S(1)}, bf16[2,256,128]{2,1,0:T(8,128)(2,1)S(1)}, u32[]{:S(2)}, u32[]{:S(2)}) collective-permute-start(bf16[2,256,128]{2,1,0:T(8,128)(2,1)S(1)} %pad_maximum_fusion.2), channel_id=1, source_target_pairs={{0,4},{4,0},{1,5},{5,1},{2,6},{6,2},{3,7},{7,3},{8,12},{12,8},{9,1... | collective-permute-start | bytes 393224 | tf_op jit(solution)/shard_map/ppermute | solution.py:338
  45.0 4.0 %collective-permute-start.2 = (f32[8,1024]{1,0:T(8,128)S(1)}, f32[8,1024]{1,0:T(8,128)S(1)}, u32[]{:S(2)}, u32[]{:S(2)}) collective-permute-start(f32[8,1024]{1,0:T(8,128)S(1)} %get-tuple-element.23.own), channel_id=1, source_target_pairs={{0,8},{8,0},{16,24},{24,16},{32,40},{40,32},{48,56},{56,48},{1,9},... | collective-permute-start | bytes 98312 | tf_op jit(solution)/shard_map/ppermute | solution.py:350
  75.0 18.1 %copy-start = (bf16[32,80,128]{2,1,0:T(8,128)(2,1)}, bf16[32,80,128]{2,1,0:T(8,128)(2,1)S(1)}, u32[]{:S(2)}) copy-start(bf16[32,80,128]{2,1,0:T(8,128)(2,1)S(1)} %all_to_all.15.folded) | copy-start | bytes 1966084
  75.1 18.0 %copy-start.1 = (bf16[128,1024]{1,0:T(8,128)(2,1)}, bf16[128,1024]{1,0:T(8,128)(2,1)S(1)}, u32[]{:S(2)}) copy-start(bf16[128,1024]{1,0:T(8,128)(2,1)S(1)} %shard_map.107.dk.dk_0) | copy-start | bytes 786436
  75.1 8.1 %collective-permute-start.4 = (bf16[128,1024]{1,0:T(8,128)(2,1)S(1)}, bf16[128,1024]{1,0:T(8,128)(2,1)S(1)}, u32[]{:S(2)}, u32[]{:S(2)}) collective-permute-start(bf16[128,1024]{1,0:T(8,128)(2,1)S(1)} %shard_map.107.dk.dk_0), channel_id=1, source_target_pairs={{0,4},{4,0},{1,5},{5,1},{2,6},{6,2},{3,7},{7,3},{8,12},{12,8},{9,1... | collective-permute-start | bytes 786440 | tf_op jit(solution)/shard_map/ppermute | solution.py:338
  77.5 5.8 %collective-permute-start.3 = (bf16[128,1024]{1,0:T(8,128)(2,1)S(1)}, bf16[128,1024]{1,0:T(8,128)(2,1)S(1)}, u32[]{:S(2)}, u32[]{:S(2)}) collective-permute-start(bf16[128,1024]{1,0:T(8,128)(2,1)S(1)} %shard_map.107.dk.dk_0), channel_id=1, source_target_pairs={{0,1},{1,0},{2,3},{3,2},{4,5},{5,4},{6,7},{7,6},{8,9},{9,8},{10,11... | collective-permute-start | bytes 786440 | tf_op jit(solution)/shard_map/ppermute | solution.py:337
  83.3 1.5 %collective-permute-start.5 = (bf16[128,1024]{1,0:T(8,128)(2,1)S(1)}, bf16[128,1024]{1,0:T(8,128)(2,1)S(1)}, u32[]{:S(2)}, u32[]{:S(2)}) collective-permute-start(bf16[128,1024]{1,0:T(8,128)(2,1)S(1)} %collective-permute-done.4.dk_2), channel_id=1, source_target_pairs={{0,1},{1,0},{2,3},{3,2},{4,5},{5,4},{6,7},{7,6},{8,9},{9,8},{10,11... | collective-permute-start | bytes 786440 | tf_op jit(solution)/shard_map/ppermute | solution.py:337
  86.1 23.8 %all-to-all-start.2 = ((bf16[64,4,1024]{2,1,0:T(4,128)(2,1)}), bf16[64,4,1024]{2,1,0:T(4,128)(2,1)S(1)}, u32[]{:S(2)}, u32[]{:S(2)}) async-start(bf16[64,4,1024]{2,1,0:T(4,128)(2,1)} %shard_map.109), calls=%async_computation.2 | async-start | bytes 1048576 | tf_op jit(solution)/shard_map/all_to_all | solution.py:357
